TPU v7x, 32 devices: a whole 2x2x4 slice. The times are simulated.
32 devices in a mesh: dp: 2 (over x), seq: 16 (over z, y, core).
Axes of the slice: x: 2, y: 2, z: 4, core: 2. Of those that a mesh axis runs over, the one named last changes fastest.
Arguments:
- tokens: bfloat16 [16384, 768], P(('dp', 'seq')), may hold values from -6 to 6
- t_embed: bfloat16 [4, 768], P('dp'), may hold values from -6 to 6
- frame_clip: int32 [64], P('dp'), may hold values from 0 to 1, as said below
- boxes: int32 [64, 4], P(('dp', 'seq')), may hold values from 0 to 16, as said below
- mod_weight: bfloat16 [768, 6912], replicated, may hold values from -0.21875 to 0.21875
- mod_bias: bfloat16 [6912], replicated, may hold values from -3 to 3
- space_qkv: bfloat16 [768, 2304], replicated, may hold values from -0.21875 to 0.21875
- space_qv_bias: bfloat16 [1536], replicated, may hold values from -4 to 4
- space_out: bfloat16 [768, 768], replicated, may hold values from -1.75 to 1.75
- space_out_bias: bfloat16 [768], replicated, may hold values from -4 to 4
- time_qkv: bfloat16 [768, 2304], replicated, may hold values from -0.21875 to 0.21875
- time_qv_bias: bfloat16 [1536], replicated, may hold values from -4 to 4
- time_out: bfloat16 [768, 768], replicated, may hold values from -0.625 to 0.625
- time_out_bias: bfloat16 [768], replicated, may hold values from -4 to 4
- up_weight: bfloat16 [768, 3072], replicated, may hold values from -0.21875 to 0.21875
- up_bias: bfloat16 [3072], replicated, may hold values from -4 to 4
- down_weight: bfloat16 [3072, 768], replicated, may hold values from -0.109375 to 0.109375
- down_bias: bfloat16 [768], replicated, may hold values from -4 to 4
- cotangent: bfloat16 [16384, 768], P(('dp', 'seq')), may hold values from -6 to 6
Outputs:
- result: bfloat16 [16384, 768], P(('dp', 'seq'))
- grad_tokens: bfloat16 [16384, 768], P(('dp', 'seq'))
- grad_mod_weight: float32 [768, 6912], replicated
- grad_mod_bias: float32 [6912], replicated
- grad_space_qkv: float32 [768, 2304], replicated
- grad_space_qv_bias: float32 [1536], replicated
- grad_space_out: float32 [768, 768], replicated
- grad_space_out_bias: float32 [768], replicated
- grad_time_qkv: float32 [768, 2304], replicated
- grad_time_qv_bias: float32 [1536], replicated
- grad_time_out: float32 [768, 768], replicated
- grad_time_out_bias: float32 [768], replicated
- grad_up_weight: float32 [768, 3072], replicated
- grad_up_bias: float32 [3072], replicated
- grad_down_weight: float32 [3072, 768], replicated
- grad_down_bias: float32 [768], replicated
Inputs may be any that keep to these rules, and one draw needn't show every extreme that they name: `frame_clip`: within each replica group of 32 frames every clip number appears exactly 16 times, and the group's first and last frames belong to the same clip. `boxes`: each box has 1 to 8 rows and 1 to 8 columns inside the grid (first < end).
All inputs are finite; a program needn't handle non-finite values.
Results may differ from a plain program's by a relative error of at most 0.015.
Values may be sent and summed in bfloat16 or wider, within the bound.
No kernel may reach another device: no remote copies, remote signals or barrier semaphores. Data moves between devices by JAX's collectives and lax.ppermute only.
A program may use at most 320 MiB of HBM per device.

v0:
```python
import jax
import jax.numpy as jnp
from jax import lax
from jax.sharding import PartitionSpec as P

H = 12
HD = 64
GRID_W = 16


EPS = 1e-06
HIGH = lax.Precision.HIGHEST
NEG = -1e30


def layer_norm(values):
    center = values - jnp.mean(values, axis=-1, keepdims=True)
    spread = jnp.mean(center * center, axis=-1, keepdims=True)
    return center * lax.rsqrt(spread + EPS)


def modulate(values, shift_by, scale_by):
    return layer_norm(values) * (1.0 + scale_by) + shift_by


def modulate_back(values, shift_by, scale_by, upstream):
    _, pull_back = jax.vjp(modulate, values, shift_by, scale_by)
    return pull_back(upstream)


def smooth_gelu(values):
    return jax.nn.gelu(values, approximate=True)


def attend(query_in, key_in, value_in, allowed, q_form, k_form):
    factor = query_in.shape[-1] ** (-0.5)
    scores = (
        jnp.einsum(
            q_form + "," + k_form + "->bhqk", query_in, key_in, preferred_element_type=jnp.float32
        )
        * factor
    )
    scores = jnp.where(allowed, scores, NEG)
    exp_scores = jnp.exp(scores - jnp.max(scores, axis=-1, keepdims=True))
    soft_rows = exp_scores / jnp.sum(exp_scores, axis=-1, keepdims=True)
    low_probs = soft_rows.astype(jnp.bfloat16)
    mixed = jnp.einsum(
        "bhqk," + k_form + "->" + q_form, low_probs, value_in, preferred_element_type=jnp.float32
    )
    return (mixed, soft_rows, low_probs)


def attend_back(query_in, key_in, value_in, soft_rows, low_probs, grad_in, q_form, k_form):
    factor = query_in.shape[-1] ** (-0.5)
    grad_value = jnp.einsum(
        "bhqk," + q_form + "->" + k_form, low_probs, grad_in, preferred_element_type=jnp.float32
    )
    grad_soft = jnp.einsum(
        q_form + "," + k_form + "->bhqk", grad_in, value_in, preferred_element_type=jnp.float32
    )
    inner_sum = jnp.sum(grad_soft * soft_rows, axis=-1, keepdims=True)
    grad_scores = (soft_rows * (grad_soft - inner_sum)).astype(jnp.bfloat16)
    grad_query = (
        jnp.einsum(
            "bhqk," + k_form + "->" + q_form,
            grad_scores,
            key_in,
            preferred_element_type=jnp.float32,
        )
        * factor
    )
    grad_key = (
        jnp.einsum(
            "bhqk," + q_form + "->" + k_form,
            grad_scores,
            query_in,
            preferred_element_type=jnp.float32,
        )
        * factor
    )
    return (grad_query, grad_key, grad_value)


def split_heads(packed, model_width, head_shape):
    query_part = packed[..., :model_width].reshape(head_shape)
    key_part = packed[..., model_width : 2 * model_width].reshape(head_shape)
    value_part = packed[..., 2 * model_width :].reshape(head_shape)
    return (query_part, key_part, value_part)


def join_heads(parts, flat_shape):
    return jnp.concatenate([member.reshape(flat_shape) for member in parts], axis=-1).astype(
        jnp.bfloat16
    )


def full_bias(qv_bias, model_width):
    wide = qv_bias.astype(jnp.float32)
    return jnp.concatenate(
        [wide[:model_width], jnp.zeros((model_width,), jnp.float32), wide[model_width:]]
    )


def qv_sums(grad_packed, model_width):
    column_sums = jnp.sum(grad_packed.astype(jnp.float32), axis=(0, 1))
    return jnp.concatenate([column_sums[:model_width], column_sums[2 * model_width :]])


def per_device(
    tokens,
    t_embed,
    frame_clip,
    boxes,
    mod_weight,
    mod_bias,
    space_qkv,
    space_qv_bias,
    space_out,
    space_out_bias,
    time_qkv,
    time_qv_bias,
    time_out,
    time_out_bias,
    up_weight,
    up_bias,
    down_weight,
    down_bias,
    cotangent,
):
    frames = boxes.shape[0]
    model_width = tokens.shape[1]
    patch_count = tokens.shape[0] // frames
    group_frames = frame_clip.shape[0]
    positions = patch_count // lax.axis_size("seq")
    own_clip = lax.dynamic_slice_in_dim(frame_clip, lax.axis_index("seq") * frames, frames)
    clip_ids = jnp.arange(t_embed.shape[0], dtype=jnp.int32)
    selector = (own_clip[:, None] == clip_ids[None, :]).astype(jnp.float32)
    smooth = jax.nn.silu(t_embed.astype(jnp.float32)).astype(jnp.bfloat16)
    per_clip = jnp.dot(smooth, mod_weight, preferred_element_type=jnp.float32) + mod_bias.astype(
        jnp.float32
    )
    per_frame = jnp.dot(selector, per_clip, precision=HIGH).reshape(frames, 9, 1, model_width)
    shift_a, scale_a, gate_a, shift_b, scale_b, gate_b, shift_c, scale_c, gate_c = [
        per_frame[:, member] for member in range(9)
    ]
    cells = jnp.arange(patch_count, dtype=jnp.int32)
    cell_row = cells // GRID_W
    cell_col = cells % GRID_W
    inside = (
        (cell_row[None] >= boxes[:, 0:1])
        & (cell_row[None] < boxes[:, 1:2])
        & (cell_col[None] >= boxes[:, 2:3])
        & (cell_col[None] < boxes[:, 3:4])
    )
    visible = jnp.logical_not(inside)[:, None, None, :]
    same_clip = (frame_clip[:, None] == frame_clip[None, :])[None, None]
    space_shape = (frames, patch_count, H, HD)
    time_shape = (group_frames, positions, H, HD)
    home_flat = (frames, patch_count, model_width)
    pos_flat = (group_frames, positions, model_width)
    inputs = tokens.astype(jnp.float32).reshape(home_flat)
    normed_a = modulate(inputs, shift_a, scale_a).astype(jnp.bfloat16)
    packed_a = (
        jnp.einsum("fpd,de->fpe", normed_a, space_qkv, preferred_element_type=jnp.float32)
        + full_bias(space_qv_bias, model_width)
    ).astype(jnp.bfloat16)
    query_a, key_a, value_a = split_heads(packed_a, model_width, space_shape)
    mixed_a, soft_a, lowp_a = attend(query_a, key_a, value_a, visible, "bqhe", "bkhe")
    attended_a = mixed_a.reshape(home_flat).astype(jnp.bfloat16)
    branch_a = jnp.einsum(
        "fpd,de->fpe", attended_a, space_out, preferred_element_type=jnp.float32
    ) + space_out_bias.astype(jnp.float32)
    mid_a = inputs + gate_a * branch_a
    time_bias = full_bias(time_qv_bias, model_width)
    normed_b = modulate(mid_a, shift_b, scale_b).astype(jnp.bfloat16)
    packed_home = (
        jnp.einsum("fpd,de->fpe", normed_b, time_qkv, preferred_element_type=jnp.float32)
        + time_bias
    ).astype(jnp.bfloat16)
    packed_b = lax.all_to_all(packed_home, "seq", split_axis=1, concat_axis=0, tiled=True)
    query_b, key_b, value_b = split_heads(packed_b, model_width, time_shape)
    mixed_b, soft_b, lowp_b = attend(query_b, key_b, value_b, same_clip, "qbhe", "kbhe")
    attended_pos = mixed_b.reshape(pos_flat).astype(jnp.bfloat16)
    attended_b = lax.all_to_all(attended_pos, "seq", split_axis=0, concat_axis=1, tiled=True)
    branch_b = jnp.einsum(
        "fpd,de->fpe", attended_b, time_out, preferred_element_type=jnp.float32
    ) + time_out_bias.astype(jnp.float32)
    mid_b = mid_a + gate_b * branch_b
    normed_c = modulate(mid_b, shift_c, scale_c).astype(jnp.bfloat16)
    hidden_up = jnp.einsum(
        "fpd,dh->fph", normed_c, up_weight, preferred_element_type=jnp.float32
    ) + up_bias.astype(jnp.float32)
    activated = smooth_gelu(hidden_up).astype(jnp.bfloat16)
    branch_c = jnp.einsum(
        "fph,hd->fpd", activated, down_weight, preferred_element_type=jnp.float32
    ) + down_bias.astype(jnp.float32)
    result_out = (mid_b + gate_c * branch_c).astype(jnp.bfloat16).reshape(tokens.shape)
    upstream = cotangent.astype(jnp.float32).reshape(home_flat)
    grad_gate_c = jnp.sum(branch_c * upstream, axis=1, keepdims=True)
    grad_branch_c = (gate_c * upstream).astype(jnp.bfloat16)
    grad_down_b = jnp.sum(grad_branch_c.astype(jnp.float32), axis=(0, 1))
    grad_down = jnp.einsum(
        "fph,fpd->hd", activated, grad_branch_c, preferred_element_type=jnp.float32
    )
    grad_act = jnp.einsum(
        "fpd,hd->fph", grad_branch_c, down_weight, preferred_element_type=jnp.float32
    )
    _, gelu_pull = jax.vjp(smooth_gelu, hidden_up)
    grad_hidden = gelu_pull(grad_act)[0].astype(jnp.bfloat16)
    grad_up_b = jnp.sum(grad_hidden.astype(jnp.float32), axis=(0, 1))
    grad_up = jnp.einsum("fpd,fph->dh", normed_c, grad_hidden, preferred_element_type=jnp.float32)
    grad_normed_c = jnp.einsum(
        "fph,dh->fpd", grad_hidden, up_weight, preferred_element_type=jnp.float32
    )
    grad_into_b, grad_shift_c, grad_scale_c = modulate_back(mid_b, shift_c, scale_c, grad_normed_c)
    grad_mid_b = upstream + grad_into_b
    grad_gate_b = jnp.sum(branch_b * grad_mid_b, axis=1, keepdims=True)
    grad_branch_b = (gate_b * grad_mid_b).astype(jnp.bfloat16)
    grad_tout_b = jnp.sum(grad_branch_b.astype(jnp.float32), axis=(0, 1))
    grad_time_out = jnp.einsum(
        "fpd,fpe->de", attended_b, grad_branch_b, preferred_element_type=jnp.float32
    )
    grad_attended_b = jnp.einsum(
        "fpe,de->fpd", grad_branch_b, time_out, preferred_element_type=jnp.float32
    ).astype(jnp.bfloat16)
    grad_attended_pos = lax.all_to_all(
        grad_attended_b, "seq", split_axis=1, concat_axis=0, tiled=True
    )
    grad_parts_b = attend_back(
        query_b,
        key_b,
        value_b,
        soft_b,
        lowp_b,
        grad_attended_pos.reshape(time_shape),
        "qbhe",
        "kbhe",
    )
    grad_packed_b = join_heads(grad_parts_b, pos_flat)
    grad_tqv_b = qv_sums(grad_packed_b, model_width)
    grad_packed_home = lax.all_to_all(grad_packed_b, "seq", split_axis=0, concat_axis=1, tiled=True)
    grad_time_qkv = jnp.einsum(
        "fpd,fpe->de", normed_b, grad_packed_home, preferred_element_type=jnp.float32
    )
    grad_normed_b = jnp.einsum(
        "fpe,de->fpd", grad_packed_home, time_qkv, preferred_element_type=jnp.float32
    )
    grad_into_a, grad_shift_b, grad_scale_b = modulate_back(mid_a, shift_b, scale_b, grad_normed_b)
    grad_mid_a = grad_mid_b + grad_into_a
    grad_gate_a = jnp.sum(branch_a * grad_mid_a, axis=1, keepdims=True)
    grad_branch_a = (gate_a * grad_mid_a).astype(jnp.bfloat16)
    grad_sout_b = jnp.sum(grad_branch_a.astype(jnp.float32), axis=(0, 1))
    grad_space_out = jnp.einsum(
        "fpd,fpe->de", attended_a, grad_branch_a, preferred_element_type=jnp.float32
    )
    grad_attended_a = jnp.einsum(
        "fpe,de->fpd", grad_branch_a, space_out, preferred_element_type=jnp.float32
    ).astype(jnp.bfloat16)
    grad_parts_a = attend_back(
        query_a,
        key_a,
        value_a,
        soft_a,
        lowp_a,
        grad_attended_a.reshape(space_shape),
        "bqhe",
        "bkhe",
    )
    grad_packed_a = join_heads(grad_parts_a, home_flat)
    grad_sqv_b = qv_sums(grad_packed_a, model_width)
    grad_space_qkv = jnp.einsum(
        "fpd,fpe->de", normed_a, grad_packed_a, preferred_element_type=jnp.float32
    )
    grad_normed_a = jnp.einsum(
        "fpe,de->fpd", grad_packed_a, space_qkv, preferred_element_type=jnp.float32
    )
    grad_into_in, grad_shift_a, grad_scale_a = modulate_back(
        inputs, shift_a, scale_a, grad_normed_a
    )
    grad_tokens = (grad_mid_a + grad_into_in).astype(jnp.bfloat16).reshape(tokens.shape)
    grad_frame = jnp.concatenate(
        [
            grad_shift_a,
            grad_scale_a,
            grad_gate_a,
            grad_shift_b,
            grad_scale_b,
            grad_gate_b,
            grad_shift_c,
            grad_scale_c,
            grad_gate_c,
        ],
        axis=1,
    )
    grad_frame = grad_frame.reshape(frames, 9 * model_width)
    grad_clip = jnp.dot(selector.T, grad_frame, precision=HIGH)
    rest_grads = [
        grad_space_qkv,
        grad_sqv_b,
        grad_space_out,
        grad_sout_b,
        grad_time_qkv,
        grad_tqv_b,
        grad_time_out,
        grad_tout_b,
        grad_up,
        grad_up_b,
        grad_down,
        grad_down_b,
    ]
    grad_mod = None
    grad_mod_b = None
    travel = [
        jnp.dot(smooth.astype(jnp.float32).T, grad_clip, precision=HIGH),
        jnp.sum(grad_clip, axis=0),
    ] + rest_grads
    flat_grads = jnp.concatenate([matrix.reshape(-1) for matrix in travel])
    total_devices = lax.axis_size("dp") * lax.axis_size("seq")
    padding = -flat_grads.shape[0] % total_devices
    flat_grads = jnp.concatenate([flat_grads, jnp.zeros((padding,), jnp.float32)])
    share_sum = lax.psum_scatter(flat_grads, ("dp", "seq"), scatter_dimension=0, tiled=True)
    summed = lax.all_gather(
        share_sum.astype(jnp.bfloat16), ("dp", "seq"), axis=0, tiled=True
    ).astype(share_sum.dtype)
    pieces = []
    offset = 0
    for matrix in travel:
        length = matrix.size
        pieces.append(summed[offset : offset + length].reshape(matrix.shape))
        offset = offset + length
    grad_mod = pieces[0]
    grad_mod_b = pieces[1]
    pieces = pieces[2:]
    return (result_out, grad_tokens, grad_mod, grad_mod_b) + tuple(pieces)


def solution(mesh):
    placed = (
        P(("dp", "seq"), None),
        P("dp", None),
        P("dp"),
        P(("dp", "seq"), None),
        P(),
        P(),
        P(),
        P(),
        P(),
        P(),
        P(),
        P(),
        P(),
        P(),
        P(),
        P(),
        P(),
        P(),
        P(("dp", "seq"), None),
    )
    return jax.shard_map(
        per_device,
        mesh=mesh,
        in_specs=placed,
        out_specs=(
            P(("dp", "seq"), None),
            P(("dp", "seq"), None),
            P(),
            P(),
            P(),
            P(),
            P(),
            P(),
            P(),
            P(),
            P(),
            P(),
            P(),
            P(),
            P(),
            P(),
        ),
        check_vma=False,
    )
```

profile of v0, /device:TPU:0, one launch (start us, length us, event | category | flops | bytes accessed | tf_op | source)
XLA Modules:
  0.0 2255.4 jit_solution(15539702407360882888)
XLA Ops:
  80.1 44.3 %all-to-all-done = bf16[2,256,2304]{2,0,1:T(2,128)(2,1)} async-done(((bf16[2,256,2304]{2,0,1:T(2,128)(2,1)}), bf16[2,256,2304]{2,0,1:T(2,128)(2,1)}, u32[]{:S(2)}, u32[]{:S(2)}) %all-to-all-start) | async-done | bytes 2359328 | tf_op jit(solution)/shard_map/all_to_all | solution.py:180
  152.5 12.5 all-to-all-start.1
  170.2 13.6 all-to-all-done.1
  215.5 25.9 %all_to_all.69 = bf16[2,256,768]{2,0,1:T(2,128)(2,1)S(1)} all-to-all(bf16[2,256,768]{2,0,1:T(2,128)(2,1)S(1)} %copy.143), channel_id=1, replica_groups=mesh['dp'=2,'seq'=16] {'seq'}, dimensions={1} | all-to-all | bytes 1572864 | tf_op jit(solution)/shard_map/all_to_all | solution.py:226
  310.5 10.5 convolution_bitcast_fusion.2
  321.0 11.0 reshape.498
  392.7 11.9 fusion.88
  404.7 22.2 reshape.492
  426.9 14.9 constant_dynamic-update-slice_fusion.12
  443.1 60.9 %dynamic-update-slice.3 = f32[14760960]{0:T(1024)} dynamic-update-slice(f32[14760960]{0:T(1024)} %constant_dynamic-update-slice_fusion.18, f32[1769472]{0:T(1024)} %reshape.493, s32[]{} %constant.99) | dynamic-update-slice | bytes 14155780
  516.3 20.3 dynamic-update-slice.6
  545.8 20.2 dynamic-update-slice.11
  567.3 80.3 %dynamic-update-slice.13 = f32[14760960]{0:T(1024)} dynamic-update-slice(f32[14760960]{0:T(1024)} %constant_dynamic-update-slice_fusion.15, f32[2359296]{0:T(1024)} %bitcast.186, s32[]{} %constant.109) | dynamic-update-slice | bytes 18874372
  649.0 80.4 %dynamic-update-slice.15 = f32[14760960]{0:T(1024)} dynamic-update-slice(f32[14760960]{0:T(1024)} %constant_dynamic-update-slice_fusion.14, f32[2359296]{0:T(1024)} %reshape.498, s32[]{} %constant.111) | dynamic-update-slice | bytes 18874372
  730.6 938.3 %all-reduce.6 = bf16[14760960]{0:T(1024)(128)(2,1)} all-reduce(f32[14760960]{0:T(1024)} %constant_dynamic-update-slice_fusion.13), channel_id=2, replica_groups=mesh['dp'=2,'seq'=16] {'dp','seq'}, use_global_device_ids=true, to_apply=%region_34.35.clone | all-reduce | flops 14760960 | bytes 88565760
  1670.6 9.7 broadcast.322
  1680.3 14.9 dynamic-update-slice
  1695.2 447.1 %all-reduce.5.cloned.1.call-done = bf16[14760960]{0:T(1024)(128)(2,1)} async-done(((bf16[14760960]{0:T(1024)(128)(2,1)}), bf16[14760960]{0:T(1024)(128)(2,1)}) %all-reduce.5.cloned.1.call-update) | async-done | bytes 29521936
  2142.3 12.1 slice.220
  2154.5 23.5 %reshape.499 = f32[768,6912]{1,0:T(8,128)} reshape(f32[5308416]{0:T(1024)} %slice.220) | data formatting | bytes 42467328 | tf_op jit(solution)/shard_map/reshape | solution.py:329
  2178.0 10.0 fusion.93
  2188.0 10.9 reshape.502
  2198.9 11.3 slice.195
  2217.8 8.2 reshape.500
  (355 shorter events, 325.1 us)
Async XLA Ops:
  7.2 56.3 %copy-start = (bf16[768,2304]{1,0:T(8,128)(2,1)S(1)}, bf16[768,2304]{1,0:T(8,128)(2,1)}, u32[]{:S(2)}) copy-start(bf16[768,2304]{1,0:T(8,128)(2,1)} %param.29) | copy-start | bytes 10616836
  27.0 6.5 copy-start.68
  42.7 12.3 copy-start.48
  71.3 53.2 %all-to-all-start = ((bf16[2,256,2304]{2,0,1:T(2,128)(2,1)}), bf16[2,256,2304]{2,0,1:T(2,128)(2,1)}, u32[]{:S(2)}, u32[]{:S(2)}) async-start(bf16[2,256,2304]{2,0,1:T(2,128)(2,1)} %copy.134), calls=%async_computation | async-start | bytes 4718592 | tf_op jit(solution)/shard_map/all_to_all | solution.py:180
  152.5 31.3 %all-to-all-start.1 = ((bf16[32,16,768]{2,1,0:T(8,128)(2,1)}), bf16[32,16,768]{2,1,0:T(8,128)(2,1)}, u32[]{:S(2)}, u32[]{:S(2)}) async-start(bf16[32,16,768]{2,1,0:T(8,128)(2,1)} %convert_element_type.155), calls=%async_computation.1 | async-start | bytes 1572864 | tf_op jit(solution)/shard_map/all_to_all | solution.py:184
  185.4 8.8 slice-start.2
  188.8 22.5 copy-start.7
  188.8 22.5 copy-start.57
  189.2 22.1 copy-start.73
  194.3 12.8 slice-start.4
  199.9 11.4 copy-start.34
  199.9 7.2 slice-start.5
  285.8 50.2 %all-to-all-start.3 = ((bf16[32,16,2304]{2,1,0:T(8,128)(2,1)}), bf16[32,16,2304]{2,1,0:T(8,128)(2,1)}, u32[]{:S(2)}, u32[]{:S(2)}) async-start(bf16[32,16,2304]{2,1,0:T(8,128)(2,1)} %constant_dynamic-update-slice_fusion), calls=%async_computation.3 | async-start | bytes 4718592 | tf_op jit(solution)/shard_map/all_to_all | solution.py:241
  290.4 1851.9 %all-reduce.5.cloned.1.call-start = ((), (), s32[]{:S(2)}) async-start(), calls=%async_computation.4 | async-start | bytes 59043840
  365.4 7.2 copy-start.56
  365.4 7.2 copy-start.72
  378.7 7.9 copy-start.66
  443.1 63.5 %copy-start.11 = (f32[768,768]{1,0:T(8,128)S(1)}, f32[768,768]{1,0:T(8,128)}, u32[]{:S(2)}) copy-start(f32[768,768]{1,0:T(8,128)} %convolution_bitcast_fusion.5) | copy-start | bytes 7077892
  508.2 8.1 copy-start.12
  537.8 7.9 copy-start.10
  545.8 20.2 copy-start.74
  567.3 80.3 %copy-start.77 = (f32[3072]{0:T(1024)S(1)}, f32[3072]{0:T(1024)}, u32[]{:S(2)}) copy-start(f32[3072]{0:T(1024)} %get-tuple-element.94) | copy-start | bytes 36868
  649.0 80.4 %copy-start.75 = (f32[768]{0:T(1024)S(1)}, f32[768]{0:T(1024)}, u32[]{:S(2)}) copy-start(f32[768]{0:T(1024)} %convert_reduce_fusion.3) | copy-start | bytes 9220
  2239.4 9.0 copy-start.1
  (79 other events, 250.3 us)
Sparse Core Ops, SparseCore 0:
  1695.4 446.8 all-reduce.4
where the time goes:
time: 2290 us; the launch traced here: 2260 us
  blocking collectives  964 us (42%)
  local copies, waits for them, and re-layouts  574 us (25%)
  waiting for transfers between devices  506 us (22%)
  matrix products  130 us (6%)
  other arithmetic  40.6 us (2%)
  starting transfers between devices  24.6 us (1%)
    unnamed x1, blocking collectives  938 us
    unnamed x2, waiting for transfers between devices  447 us
    unnamed x232, local copies, waits for them, and re-layouts  341 us
    slice x11, local copies, waits for them, and re-layouts, per_device(): pieces.append(summed[offset:offset + length].reshape(matrix.shape))  55.2 us
    reshape x6, local copies, waits for them, and re-layouts, per_device(): flat_grads = jnp.concatenate([matrix.reshape(-1) for matrix in travel])  54 us
    reshape x4, local copies, waits for them, and re-layouts, per_device(): pieces.append(summed[offset:offset + length].reshape(matrix.shape))  50.9 us
  transfers between devices with their start and end apart: 4, of which 4 were waited for; matrix products, arithmetic and copies ran while one was open for 2% of the time, Pallas kernels for 0%

commit v1 on v0

v1 whole, which is shorter than its diff:
```python
import functools

import jax
import jax.numpy as jnp
from jax import lax
from jax.experimental import pallas as pl
from jax.experimental.pallas import tpu as pltpu
from jax.sharding import PartitionSpec as P

HD = 64
GRID_W = 16
EPS = 1e-06
NEG = -1e30
BLOCK = 256
LANES = 128
BF = jnp.bfloat16
F32 = jnp.float32
VMEM_BYTES = 56 * 1024 * 1024
BOTH = ("dp", "seq")
BRIEF = pl.CostEstimate(flops=1000, bytes_accessed=1000, transcendentals=0)
LONG = pl.CostEstimate(flops=3 * 10**10, bytes_accessed=1000, transcendentals=0)

SCHEDULE = (
    ("time",),
    ("t", "cross", 0),
    ("space",),
    ("t", "cross", 1),
    ("s", "cross", 0),
    ("small",),
    ("t", "along"),
    ("small",),
    ("s", "cross", 1),
    ("t", "finish"),
    ("ff",),
    ("s", "along"),
    ("small",),
    ("t", "gather"),
    ("s", "finish"),
    ("t", "relay"),
    ("small",),
    ("s", "gather"),
    ("t", "reflect"),
    ("small",),
    ("t", "widen", 0),
    ("s", "relay"),
    ("t", "widen", 1),
    ("mod",),
    ("s", "reflect"),
    ("s", "widen", 0),
    ("s", "widen", 1),
)


def params():
    return pltpu.CompilerParams(vmem_limit_bytes=VMEM_BYTES)


def alone():
    return pltpu.CompilerParams(vmem_limit_bytes=60 * 1024 * 1024)


def dot_nn(a, b):
    return lax.dot_general(a, b, (((1,), (0,)), ((), ())), preferred_element_type=F32)


def dot_nt(a, b):
    return lax.dot_general(a, b, (((1,), (1,)), ((), ())), preferred_element_type=F32)


def dot_tn(a, b):
    return lax.dot_general(a, b, (((0,), (0,)), ((), ())), preferred_element_type=F32)


def normalize(x):
    center = x - jnp.mean(x, axis=-1, keepdims=True)
    r = lax.rsqrt(jnp.mean(center * center, axis=-1, keepdims=True) + EPS)
    return center * r, r


def normalize_back(n, r, m):
    return r * (
        m - jnp.mean(m, axis=-1, keepdims=True) - n * jnp.mean(m * n, axis=-1, keepdims=True)
    )


def head_halves(width):
    lane = lax.broadcasted_iota(jnp.int32, (1, width), 1)
    low = (lane < HD).astype(F32).astype(BF)
    return low, (lane >= HD).astype(F32).astype(BF)


def attend(packed, attended, bias, blocks, width):
    halves = head_halves(2 * HD)

    def pair(index, carry):
        off = pl.multiple_of(index * 2 * HD, 2 * HD)
        for b in range(blocks):
            rows = pl.ds(b * BLOCK, BLOCK)
            q = packed[rows, pl.ds(off, 2 * HD)]
            k = packed[rows, pl.ds(width + off, 2 * HD)]
            v = packed[rows, pl.ds(2 * width + off, 2 * HD)]
            out = None
            for half in halves:
                s = dot_nt(q, k * half) * (HD**-0.5) + bias(b)
                e = jnp.exp(s - jnp.max(s, axis=-1, keepdims=True))
                p = (e * (1.0 / jnp.sum(e, axis=-1, keepdims=True))).astype(BF)
                o = dot_nn(p, v * half)
                out = o if out is None else out + o
            attended[rows, pl.ds(off, 2 * HD)] = out.astype(BF)
        return carry

    lax.fori_loop(0, width // (2 * HD), pair, 0)


def attend_back(packed, grad_in, grad_packed, bias, blocks, width):
    halves = head_halves(2 * HD)
    factor = HD**-0.5

    def pair(index, carry):
        off = pl.multiple_of(index * 2 * HD, 2 * HD)
        for b in range(blocks):
            rows = pl.ds(b * BLOCK, BLOCK)
            q = packed[rows, pl.ds(off, 2 * HD)]
            k = packed[rows, pl.ds(width + off, 2 * HD)]
            v = packed[rows, pl.ds(2 * width + off, 2 * HD)]
            g = grad_in[rows, pl.ds(off, 2 * HD)]
            dq = dk = dv = 0.0
            for half in halves:
                kh = k * half
                s = dot_nt(q, kh) * factor + bias(b)
                e = jnp.exp(s - jnp.max(s, axis=-1, keepdims=True))
                p = e * (1.0 / jnp.sum(e, axis=-1, keepdims=True))
                gs = dot_nt(g, v * half)
                ds = (p * (gs - jnp.sum(p * gs, axis=-1, keepdims=True))).astype(BF)
                dv = dv + dot_tn(p.astype(BF), g * half)
                dq = dq + dot_nn(ds, kh)
                dk = dk + dot_tn(ds, q * half)
            grad_packed[rows, pl.ds(off, 2 * HD)] = (dq * factor).astype(BF)
            grad_packed[rows, pl.ds(width + off, 2 * HD)] = (dk * factor).astype(BF)
            grad_packed[rows, pl.ds(2 * width + off, 2 * HD)] = dv.astype(BF)
        return carry

    lax.fori_loop(0, width // (2 * HD), pair, 0)


def project_qkv(normed, weight, qv_bias, packed, width):
    for c in range(3):
        cols = pl.ds(c * width, width)
        value = dot_nn(normed[...], weight[:, cols])
        if c != 1:
            value = value + as_row(qv_bias[pl.ds((c // 2) * width, width)])
        packed[:, cols] = value.astype(BF)


def modulation_kernel(first, t_ref, w_ref, b_ref, out_ref):
    t = t_ref[...].astype(F32)
    smooth = (t / (1.0 + jnp.exp(-t))).astype(BF)
    bias = chunk_row(b_ref, first + pl.program_id(0), t.shape[1])
    out_ref[0] = dot_nn(smooth, w_ref[...]) + bias


def modulation(t_embed, weight, bias, first, count):
    clips, width = t_embed.shape
    return pl.pallas_call(
        functools.partial(modulation_kernel, first),
        grid=(count,),
        in_specs=[
            pl.BlockSpec((clips, width), lambda i: (0, 0)),
            pl.BlockSpec((width, width), lambda i: (0, first + i)),
            vmem(),
        ],
        out_specs=pl.BlockSpec((1, clips, width), lambda i: (i, 0, 0)),
        out_shape=jax.ShapeDtypeStruct((count, clips, width), F32),
        cost_estimate=BRIEF,
        name="modulation",
    )(t_embed, weight, bias)


def as_row(vector):
    return vector.astype(F32).reshape(1, -1)


def chunk_row(vector_ref, index, width):
    return as_row(vector_ref[pl.ds(pl.multiple_of(index * width, width), width)])


def own_clips(clip_ref, frames):
    first = lax.axis_index("seq") * frames
    return [clip_ref[first + f] for f in range(frames)]


def frame_row(table, member, clip):
    total = jnp.zeros(table.shape[2:], F32)[None]
    for c in range(table.shape[1]):
        total = jnp.where(clip == c, table[member, c : c + 1, :], total)
    return total


def frame_rows(table, member, clip_col):
    total = jnp.zeros((clip_col.shape[0], table.shape[2]), F32)
    for c in range(table.shape[1]):
        total = jnp.where(clip_col == c, table[member, c : c + 1, :], total)
    return total


def visible_bias(box_ref, frame, patches):
    cell = lax.broadcasted_iota(jnp.int32, (1, patches), 1)
    row, col = cell // GRID_W, cell % GRID_W
    inside = (
        (row >= box_ref[frame, 0])
        & (row < box_ref[frame, 1])
        & (col >= box_ref[frame, 2])
        & (col < box_ref[frame, 3])
    )
    return jnp.where(inside, NEG, 0.0)


def space_forward_kernel(
    clip_ref, box_ref, x_ref, table_ref, wqkv_ref, bqv_ref, wout_ref, bout_ref,
    send_ref, packed_ref, attended_ref, branch_ref, normed,
):
    frames = box_ref.shape[0]
    width = x_ref.shape[1]
    dst, _, pos, _ = send_ref.shape
    clip = own_clips(clip_ref, frames)
    for f in range(frames):
        rows = pl.ds(f * BLOCK, BLOCK)
        n, _ = normalize(x_ref[rows, :].astype(F32))
        shift = frame_row(table_ref, 0, clip[f])
        scale = frame_row(table_ref, 1, clip[f])
        normed[rows, :] = (n * (1.0 + scale) + shift).astype(BF)
    project_qkv(normed, wqkv_ref, bqv_ref, packed_ref, width)
    biases = [visible_bias(box_ref, f, BLOCK) for f in range(frames)]
    attend(packed_ref, attended_ref, lambda b: biases[b], frames, width)
    for f in range(frames):
        rows = pl.ds(f * BLOCK, BLOCK)
        branch = dot_nn(attended_ref[rows, :], wout_ref[...]) + as_row(bout_ref[...])
        branch_ref[rows, :] = branch
        gate = frame_row(table_ref, 2, clip[f])
        mid = x_ref[rows, :].astype(F32) + gate * branch
        send_ref[:, f] = mid.astype(BF).reshape(dst, pos, width)


def vmem():
    return pl.BlockSpec(memory_space=pltpu.VMEM)


def smem():
    return pl.BlockSpec(memory_space=pltpu.SMEM)


def space_forward(frame_clip, boxes, tokens, table, wqkv, bqv, wout, bout, owners):
    rows, width = tokens.shape
    frames = boxes.shape[0]
    pos = rows // frames // owners
    return pl.pallas_call(
        space_forward_kernel,
        in_specs=[smem(), smem()] + [vmem()] * 6,
        out_specs=[vmem()] * 4,
        out_shape=[
            jax.ShapeDtypeStruct((owners, frames, pos, width), BF),
            jax.ShapeDtypeStruct((rows, 3 * width), BF),
            jax.ShapeDtypeStruct((rows, width), BF),
            jax.ShapeDtypeStruct((rows, width), F32),
        ],
        scratch_shapes=[pltpu.VMEM((rows, width), BF)],
        compiler_params=params(),
        cost_estimate=BRIEF,
        name="space_forward",
    )(frame_clip, boxes, tokens, table, wqkv, bqv, wout, bout)


def to_positions(source, stage, target):
    frames, pos, width = source.shape
    for lane in range(0, width, LANES):
        cols = pl.ds(lane, LANES)
        stage[lane // LANES] = source[:, :, cols].astype(F32).reshape(frames * pos, LANES)
        for p in range(pos):
            target[pl.ds(p * frames, frames), cols] = stage[
                lane // LANES, pl.ds(p, frames, stride=pos), :
            ].astype(target.dtype)


def stage_positions(stage, value, frames, pos, first):
    for lane in range(0, value.shape[1], LANES):
        for p in range(value.shape[0] // frames):
            stage[lane // LANES, pl.ds(first + p, frames, stride=pos), :] = value[
                p * frames : (p + 1) * frames, lane : lane + LANES
            ]


def to_frames(stage, target):
    frames, pos, width = target.shape
    for lane in range(0, width, LANES):
        target[:, :, pl.ds(lane, LANES)] = (
            stage[lane // LANES].reshape(frames, pos, LANES).astype(BF)
        )


def time_mask(ids_row_ref, clip_col, positions, clips):
    frames = clip_col.shape[0]
    place = lax.broadcasted_iota(jnp.int32, (positions, frames, 1), 0) * clips
    col = (place + clip_col[None]).reshape(positions * frames, 1)
    return jnp.where(col == ids_row_ref[...], 0.0, NEG)


def spread(rows, positions):
    frames, width = rows.shape
    return jnp.broadcast_to(rows[None], (positions, frames, width)).reshape(
        positions * frames, width
    )


def gather_frames(value, frames):
    return jnp.sum(value.reshape(-1, frames, value.shape[-1]), axis=0)


def per_clip_sums(out_ref, member, rows, clip_col):
    for c in range(out_ref.shape[1]):
        out_ref[member, c : c + 1, :] = jnp.sum(
            jnp.where(clip_col == c, rows, 0.0), axis=0, keepdims=True
        )


def gelu_and_slope(v):
    c = 0.7978845608028654
    square = v * v
    t = jnp.tanh(v * (c + (c * 0.044715) * square))
    half = 0.5 + 0.5 * t
    slope = half + (0.5 * v) * (1.0 - t * t) * (c + (3.0 * c * 0.044715) * square)
    return v * half, slope


def time_forward_kernel(
    mid_ref, cot_ref, table_ref, clip_col_ref, ids_row_ref, wqkv_ref, bqv_ref, wout_ref, bout_ref,
    xa_ref, packed_ref, attended_ref, branch_ref, midb_ref, normed_ref, gbranch_ref, cot_out, gdownb_ref,
    stage, mid, cot, normed, bias,
):
    frames, pos, width = mid_ref.shape
    blocks = frames * pos // BLOCK
    per_block = BLOCK // frames
    clips = table_ref.shape[1]
    clip_col = clip_col_ref[...]

    def modvec(member):
        return spread(frame_rows(table_ref, member, clip_col), per_block)

    to_positions(mid_ref, stage, mid)
    to_positions(cot_ref, stage, cot)
    xa_ref[...] = mid[...].astype(BF)
    cot_out[...] = cot[...].astype(BF)
    bias[...] = time_mask(ids_row_ref, clip_col, per_block, clips)
    shift_b, scale_b = modvec(0), modvec(1)
    for b in range(blocks):
        part = pl.ds(b * BLOCK, BLOCK)
        n, _ = normalize(mid[part, :])
        normed[part, :] = (n * (1.0 + scale_b) + shift_b).astype(BF)
    project_qkv(normed, wqkv_ref, bqv_ref, packed_ref, width)
    attend(packed_ref, attended_ref, lambda b: bias[...], blocks, width)
    gate_b, shift_c, scale_c, gate_c = modvec(2), modvec(3), modvec(4), modvec(5)
    for b in range(blocks):
        part = pl.ds(b * BLOCK, BLOCK)
        branch = dot_nn(attended_ref[part, :], wout_ref[...]) + as_row(bout_ref[...])
        branch_ref[part, :] = branch
        mid_b = mid[part, :] + gate_b * branch
        midb_ref[part, :] = mid_b
        n, _ = normalize(mid_b)
        normed_ref[part, :] = (n * (1.0 + scale_c) + shift_c).astype(BF)
        gbranch_ref[part, :] = (gate_c * cot[part, :]).astype(BF)
    gdownb_ref[...] = jnp.sum(gbranch_ref[...].astype(F32), axis=0, keepdims=True)


def time_forward(mid, cot, table, clip_col, ids_row, wqkv, bqv, wout, bout):
    frames, pos, width = mid.shape
    rows = frames * pos
    like = lambda cols, dtype: jax.ShapeDtypeStruct((rows, cols), dtype)
    return pl.pallas_call(
        time_forward_kernel,
        in_specs=[vmem()] * 9,
        out_specs=[vmem()] * 9,
        out_shape=[
            like(width, BF),
            like(3 * width, BF),
            like(width, BF),
            like(width, F32),
            like(width, F32),
            like(width, BF),
            like(width, BF),
            like(width, BF),
            jax.ShapeDtypeStruct((1, width), F32),
        ],
        scratch_shapes=[
            pltpu.VMEM((width // LANES, rows, LANES), F32),
            pltpu.VMEM((rows, width), F32),
            pltpu.VMEM((rows, width), F32),
            pltpu.VMEM((rows, width), BF),
            pltpu.VMEM((BLOCK, BLOCK), F32),
        ],
        compiler_params=params(),
        cost_estimate=BRIEF,
        name="time_forward",
    )(mid, cot, table, clip_col, ids_row, wqkv, bqv, wout, bout)


def ff_kernel(
    last, normed_ref, gbranch_ref, branch_in, gnorm_in, up_ref, upb_ref, down_ref,
    midb_ref, cot_ref, table_ref, clip_col_ref, downb_ref, *refs,
):
    if last:
        _, grad_ref, gupb_ref, gmid_ref, result_ref, gclip_ref = refs[:6]
        normed_t, act, ghid, branch_acc, gnorm_acc, stage = refs[6:]
    else:
        grad_ref, gupb_ref, branch_acc, gnorm_acc, normed_t, act, ghid = refs
    step = pl.program_id(0)
    width = normed_ref.shape[1]
    blocks = normed_ref.shape[0] // BLOCK
    first = pl.num_programs(0) if last else 0
    up_bias = chunk_row(upb_ref, first + step, act.shape[1])

    @pl.when(step == 0)
    def _():
        normed_t[...] = normed_ref[...].T
        if last:
            branch_acc[...] = branch_in[...]
            gnorm_acc[...] = gnorm_in[...]
        else:
            branch_acc[...] = jnp.zeros_like(branch_acc)
            gnorm_acc[...] = jnp.zeros_like(gnorm_acc)

    for b in range(blocks):
        part = pl.ds(b * BLOCK, BLOCK)
        hidden = dot_nn(normed_ref[part, :], up_ref[...]) + up_bias
        value, slope = gelu_and_slope(hidden)
        value = value.astype(BF)
        act[part, :] = value
        gh = (dot_nt(gbranch_ref[part, :], down_ref[...]) * slope).astype(BF)
        ghid[part, :] = gh
        branch_acc[part, :] += dot_nn(value, down_ref[...])
        gnorm_acc[part, :] += dot_nt(gh, up_ref[...])
    grad_up = dot_nn(normed_t[...], ghid[...])
    grad_down = dot_tn(act[...], gbranch_ref[...])
    grad_ref[0] = grad_up.astype(BF)
    grad_ref[1] = grad_down.astype(BF)
    gupb_ref[0] = jnp.sum(ghid[...].astype(F32), axis=0, keepdims=True)

    if last:

        @pl.when(step == pl.num_programs(0) - 1)
        def _():
            clip_col = clip_col_ref[...]
            frames, pos, _ = result_ref.shape
            per_block = BLOCK // frames

            def modvec(member):
                return spread(frame_rows(table_ref, member, clip_col), per_block)

            scale_c, gate_c = modvec(4), modvec(5)
            sums = [0.0, 0.0, 0.0]
            for b in range(blocks):
                part = pl.ds(b * BLOCK, BLOCK)
                up = cot_ref[part, :].astype(F32)
                branch = branch_acc[part, :] + as_row(downb_ref[...])
                sums[2] = sums[2] + gather_frames(branch * up, frames)
                mid_b = midb_ref[part, :]
                n, r = normalize(mid_b)
                g = gnorm_acc[part, :]
                sums[0] = sums[0] + gather_frames(g, frames)
                sums[1] = sums[1] + gather_frames(g * n, frames)
                gmid_ref[part, :] = up + normalize_back(n, r, g * (1.0 + scale_c))
                stage_positions(stage, mid_b + gate_c * branch, frames, pos, b * per_block)
            to_frames(stage, result_ref)
            for member in range(3):
                per_clip_sums(gclip_ref, member, sums[member], clip_col)


def ff_half(half, normed, gbranch, branch_in, gnorm_in, up, upb, down, midb, cot, table, clip_col, downb, *before):
    rows, width = normed.shape
    clips = table.shape[1]
    frames = clip_col.shape[0]
    pos = rows // frames
    ff = up.shape[1]
    chunk = width
    steps = ff // chunk // 2
    last = half == 1
    first = half * steps
    whole = lambda *shape: pl.BlockSpec(shape, lambda i: (0,) * len(shape))
    grad_specs = [pl.BlockSpec((1, 1, chunk), lambda i: (i, 0, 0))]
    grad_shapes = [jax.ShapeDtypeStruct((steps, 1, chunk), F32)]
    grad_specs = [pl.BlockSpec((2, width, chunk), lambda i: (0, first + i, 0))] + grad_specs
    grad_shapes = [jax.ShapeDtypeStruct((2, 2 * steps * width, chunk), BF)] + grad_shapes
    wide = pltpu.VMEM((rows, width), F32)
    scratch = [pltpu.VMEM((width, rows), BF), pltpu.VMEM((rows, chunk), BF), pltpu.VMEM((rows, chunk), BF)]
    if last:
        out_specs = grad_specs + [whole(rows, width), whole(frames, pos, width), whole(3, clips, width)]
        out_shape = grad_shapes + [
            jax.ShapeDtypeStruct((rows, width), F32),
            jax.ShapeDtypeStruct((frames, pos, width), BF),
            jax.ShapeDtypeStruct((3, clips, width), F32),
        ]
        scratch = scratch + [wide, wide, pltpu.VMEM((width // LANES, rows, LANES), F32)]
    else:
        out_specs = grad_specs + [whole(rows, width), whole(rows, width)]
        out_shape = grad_shapes + [jax.ShapeDtypeStruct((rows, width), F32)] * 2
    unused = pl.BlockSpec(memory_space=pl.ANY)
    late = vmem() if last else unused
    if not last:
        branch_in = gnorm_in = midb
    return pl.pallas_call(
        functools.partial(ff_kernel, last),
        grid=(steps,),
        in_specs=[vmem(), vmem(), late, late]
        + [
            pl.BlockSpec((width, chunk), lambda i: (0, first + i)),
            vmem(),
            pl.BlockSpec((chunk, width), lambda i: (first + i, 0)),
        ]
        + [late] * 5
        + [hbm()] * len(before),
        input_output_aliases={12 + i: i for i in range(len(before))},
        out_specs=out_specs,
        out_shape=out_shape,
        scratch_shapes=scratch,
        compiler_params=params(),
        cost_estimate=BRIEF,
        name="ff_half_%d" % half,
    )(normed, gbranch, branch_in, gnorm_in, up, upb, down, midb, cot, table, clip_col, downb, *before)


def put(grads, core, quarter, value):
    rows = pl.ds((quarter % 2) * value.shape[0], value.shape[0])
    value = value.astype(BF)
    for target, owner in zip(grads, (quarter // 2, 1 - quarter // 2)):

        @pl.when(core == owner)
        def _(target=target):
            target[rows, :] = value


def this_core():
    return lax.rem(lax.axis_index("seq"), 2)


def qkv_back(normed, grad_packed, wqkv_ref, grads, gqv_ref, gnorm, width):
    for c in range(3):
        cols = pl.ds(c * width, width)
        gp = grad_packed[:, cols]
        put(grads, this_core(), c, dot_tn(normed[...], gp))
        if c != 1:
            gqv_ref[c // 2 : c // 2 + 1, :] = jnp.sum(gp.astype(F32), axis=0, keepdims=True)
        back = dot_nt(gp, wqkv_ref[:, cols])
        gnorm[...] = back if c == 0 else gnorm[...] + back


def owner_backward_kernel(
    xa_ref, packed_ref, attended_ref, branch_ref, gmid_ref, table_ref, clip_col_ref, ids_row_ref,
    wqkv_ref, wout_ref,
    send_ref, kept_ref, other_ref, gclip_ref, goutb_ref, gqv_ref,
    stage, normed, gbranch, gatt, gpacked, bias, gnorm,
):
    frames, pos, width = send_ref.shape
    rows = frames * pos
    blocks = rows // BLOCK
    per_block = BLOCK // frames
    clips = table_ref.shape[1]
    clip_col = clip_col_ref[...]

    def modvec(member):
        return spread(frame_rows(table_ref, member, clip_col), per_block)

    shift, scale, gate = modvec(0), modvec(1), modvec(2)
    bias[...] = time_mask(ids_row_ref, clip_col, per_block, clips)
    gate_sum = 0.0
    for b in range(blocks):
        part = pl.ds(b * BLOCK, BLOCK)
        gm = gmid_ref[part, :]
        gate_sum = gate_sum + gather_frames(branch_ref[part, :] * gm, frames)
        gb = (gate * gm).astype(BF)
        gbranch[part, :] = gb
        gatt[part, :] = dot_nt(gb, wout_ref[...]).astype(BF)
        n, _ = normalize(xa_ref[part, :].astype(F32))
        normed[part, :] = (n * (1.0 + scale) + shift).astype(BF)
    per_clip_sums(gclip_ref, 2, gate_sum, clip_col)
    goutb_ref[...] = jnp.sum(gbranch[...].astype(F32), axis=0, keepdims=True)
    grads = (kept_ref, other_ref)
    put(grads, this_core(), 3, dot_tn(attended_ref[...], gbranch[...]))
    attend_back(packed_ref, gatt, gpacked, lambda b: bias[...], blocks, width)
    qkv_back(normed, gpacked, wqkv_ref, grads, gqv_ref, gnorm, width)
    sums = [0.0, 0.0]
    for b in range(blocks):
        part = pl.ds(b * BLOCK, BLOCK)
        n, r = normalize(xa_ref[part, :].astype(F32))
        g = gnorm[part, :]
        sums[0] = sums[0] + gather_frames(g, frames)
        sums[1] = sums[1] + gather_frames(g * n, frames)
        total = gmid_ref[part, :] + normalize_back(n, r, g * (1.0 + scale))
        stage_positions(stage, total, frames, pos, b * per_block)
    to_frames(stage, send_ref)
    for member in range(2):
        per_clip_sums(gclip_ref, member, sums[member], clip_col)


def owner_backward(xa, packed, attended, branch, gmid, table, clip_col, ids_row, wqkv, wout):
    frames = clip_col.shape[0]
    rows, width = xa.shape
    clips = table.shape[1]
    return pl.pallas_call(
        owner_backward_kernel,
        in_specs=[vmem()] * 10,
        out_specs=[vmem()] * 6,
        out_shape=[
            jax.ShapeDtypeStruct((frames, rows // frames, width), BF),
            jax.ShapeDtypeStruct((2 * width, width), BF),
            jax.ShapeDtypeStruct((2 * width, width), BF),
            jax.ShapeDtypeStruct((3, clips, width), F32),
            jax.ShapeDtypeStruct((1, width), F32),
            jax.ShapeDtypeStruct((2, width), F32),
        ],
        scratch_shapes=[
            pltpu.VMEM((width // LANES, rows, LANES), F32),
            pltpu.VMEM((rows, width), BF),
            pltpu.VMEM((rows, width), BF),
            pltpu.VMEM((rows, width), BF),
            pltpu.VMEM((rows, 3 * width), BF),
            pltpu.VMEM((BLOCK, BLOCK), F32),
            pltpu.VMEM((rows, width), F32),
        ],
        compiler_params=params(),
        cost_estimate=LONG,
        name="owner_backward",
    )(xa, packed, attended, branch, gmid, table, clip_col, ids_row, wqkv, wout)


def space_backward_kernel(
    clip_ref, box_ref, x_ref, packed_ref, attended_ref, branch_ref, gmid_ref, table_ref,
    wqkv_ref, wout_ref, t_ref, gclip_b_ref, gclip_c_ref, gqv_b_ref, goutb_b_ref, gupb_0_ref, gupb_1_ref,
    gdownb_ref,
    gx_ref, kept_ref, other_ref, small_ref,
    normed, gbranch, gatt, gpacked, gnorm, goutb_ref, gqv_ref,
):
    frames = box_ref.shape[0]
    width = x_ref.shape[1]
    clips = table_ref.shape[1]
    clip = own_clips(clip_ref, frames)
    sums = [[None] * frames for _ in range(3)]
    for f in range(frames):
        part = pl.ds(f * BLOCK, BLOCK)
        gm = gmid_ref[:, f].reshape(BLOCK, width).astype(F32)
        sums[2][f] = jnp.sum(branch_ref[part, :] * gm, axis=0, keepdims=True)
        gb = (frame_row(table_ref, 2, clip[f]) * gm).astype(BF)
        gbranch[part, :] = gb
        gatt[part, :] = dot_nt(gb, wout_ref[...]).astype(BF)
        n, _ = normalize(x_ref[part, :].astype(F32))
        shift = frame_row(table_ref, 0, clip[f])
        scale = frame_row(table_ref, 1, clip[f])
        normed[part, :] = (n * (1.0 + scale) + shift).astype(BF)
    goutb_ref[...] = jnp.sum(gbranch[...].astype(F32), axis=0, keepdims=True)
    grads = (kept_ref, other_ref)
    put(grads, this_core(), 3, dot_tn(attended_ref[...], gbranch[...]))
    biases = [visible_bias(box_ref, f, BLOCK) for f in range(frames)]
    attend_back(packed_ref, gatt, gpacked, lambda b: biases[b], frames, width)
    qkv_back(normed, gpacked, wqkv_ref, grads, gqv_ref, gnorm, width)
    for f in range(frames):
        part = pl.ds(f * BLOCK, BLOCK)
        n, r = normalize(x_ref[part, :].astype(F32))
        g = gnorm[part, :]
        sums[0][f] = jnp.sum(g, axis=0, keepdims=True)
        sums[1][f] = jnp.sum(g * n, axis=0, keepdims=True)
        scale = frame_row(table_ref, 1, clip[f])
        gm = gmid_ref[:, f].reshape(BLOCK, width).astype(F32)
        gx_ref[part, :] = (gm + normalize_back(n, r, g * (1.0 + scale))).astype(BF)
    all_clips = clips * lax.axis_size("dp")
    mine = lax.axis_index("dp") * clips
    small_ref[...] = jnp.zeros_like(small_ref)
    for member in range(9):
        for c in range(clips):
            if member < 3:
                total = jnp.zeros((1, width), F32)
                for f in range(frames):
                    total = total + jnp.where(clip[f] == c, sums[member][f], 0.0)
            else:
                source = gclip_b_ref if member < 6 else gclip_c_ref
                total = source[member % 3, c : c + 1, :]
            small_ref[pl.ds(member * all_clips + mine + c, 1), :] = total
    at = 9 * all_clips
    t = jnp.where(lax.axis_index("seq") == 0, t_ref[...].astype(F32), 0.0)
    for c in range(clips):
        small_ref[pl.ds(at + mine + c, 1), :] = t[c : c + 1]
    at += all_clips
    for source in (gqv_ref, goutb_ref, gqv_b_ref, goutb_b_ref, gupb_0_ref, gupb_1_ref, gdownb_ref):
        for i in range(source.shape[0]):
            small_ref[at : at + 1, :] = source[i] if len(source.shape) == 3 else source[i : i + 1, :]
            at += 1


def space_backward(frame_clip, boxes, tokens, *rest):
    rows, width = tokens.shape
    t_embed = rest[7]
    members = rest[-1].shape[0] + sum(value.shape[0] for value in rest[10:-1])
    extra = 3 + 10 * t_embed.shape[0] * lax.axis_size("dp") + members
    return pl.pallas_call(
        space_backward_kernel,
        in_specs=[smem(), smem()] + [vmem()] * (1 + len(rest)),
        out_specs=[vmem()] * 4,
        out_shape=[
            jax.ShapeDtypeStruct((rows, width), BF),
            jax.ShapeDtypeStruct((2 * width, width), BF),
            jax.ShapeDtypeStruct((2 * width, width), BF),
            jax.ShapeDtypeStruct((-(-extra // 8) * 8, width), F32),
        ],
        scratch_shapes=[
            pltpu.VMEM((rows, width), BF),
            pltpu.VMEM((rows, width), BF),
            pltpu.VMEM((rows, width), BF),
            pltpu.VMEM((rows, 3 * width), BF),
            pltpu.VMEM((rows, width), F32),
            pltpu.VMEM((1, width), F32),
            pltpu.VMEM((2, width), F32),
        ],
        compiler_params=params(),
        cost_estimate=LONG,
        name="space_backward",
    )(frame_clip, boxes, tokens, *rest)


def routes(owners):
    depth = owners // 4
    places = [
        (x, z, y, c) for x in range(2) for z in range(depth) for y in range(2) for c in range(2)
    ]
    number = lambda x, z, y, c: x * owners + (z * 2 + y) * 2 + c
    pairs = lambda move: [(number(*p), number(*move(*p))) for p in places]
    over_x = lambda x, z, y, c: (1 - x, z, y, c)
    over_y = lambda x, z, y, c: (x, z, 1 - y, c)
    return {
        "core": pairs(lambda x, z, y, c: (x, z, y, 1 - c)),
        "first": pairs(lambda *p: (over_y if p[3] else over_x)(*p)),
        "second": pairs(lambda *p: (over_x if p[3] else over_y)(*p)),
        "x": pairs(over_x),
        "y": pairs(over_y),
        "depth": [
            pairs(lambda x, z, y, c, s=s: (x, (z + s) % depth, y, c)) for s in range(1, depth)
        ],
        "swap": [
            pairs(lambda x, z, y, c, s=s: (x, z ^ s, y, c))
            for s in (1 << i for i in range(depth.bit_length() - 1))
        ],
    }


def place():
    x, s = lax.axis_index("dp"), lax.axis_index("seq")
    return x, s >> 2, (s >> 1) & 1, s & 1


def move(value, pairs):
    return lax.ppermute(value, BOTH, pairs)


def tie(*values):
    return lax.optimization_barrier(values)


def hbm():
    return pl.BlockSpec(memory_space=pltpu.HBM)


def dma(count):
    return pltpu.SemaphoreType.DMA((count,))


def copies(pairs, semaphores):
    started = [
        pltpu.make_async_copy(source, target, semaphores.at[i])
        for i, (source, target) in enumerate(pairs)
    ]
    for copy in started:
        copy.start()
    return started


def side(stage, core):
    x, _, y, _ = place()
    return jnp.where(core == stage, x, y)


def cross_kernel(stage, kept_ref, got_ref, send_ref, out_ref, a, b, total, sem_a, sem_b, sem_out):
    count, rows, _ = total.shape
    each = count // 2
    bit = side(stage, place()[3])
    spots = [(half, pl.ds(i * rows, rows)) for half in (1 - bit, bit) for i in range(each)]
    from_a = copies([(kept_ref.at[h, r], a.at[i]) for i, (h, r) in enumerate(spots)], sem_a)
    from_b = copies([(got_ref.at[h, r], b.at[i]) for i, (h, r) in enumerate(spots)], sem_b)
    out = []
    for i, (_, r) in enumerate(spots):
        from_a[i].wait()
        from_b[i].wait()
        total[i] = (a[i].astype(F32) + b[i].astype(F32)).astype(BF)
        target = (send_ref if i < each else out_ref).at[r]
        out += copies([(total.at[i], target)], sem_out.at[pl.ds(i, 1)])
    for copy in out:
        copy.wait()


def cross_sum(cost, stage, kept, got):
    height, width = kept.shape[0] // 2, kept.shape[1]
    each = max(1, height // 384)
    buffer = pltpu.VMEM((2 * each, height // each, width), BF)
    half = jax.ShapeDtypeStruct((height, width), BF)
    return pl.pallas_call(
        functools.partial(cross_kernel, stage),
        in_specs=[hbm(), hbm()],
        out_specs=[hbm(), hbm()],
        out_shape=[half, half],
        scratch_shapes=[buffer] * 3 + [dma(2 * each)] * 3,
        compiler_params=alone(),
        cost_estimate=cost,
        name="cross_sum",
    )(kept.reshape(2, height, width), got.reshape(2, height, width))


def along_kernel(kept_ref, got_ref, *refs):
    depth = kept_ref.shape[0]
    targets = refs[:depth]
    a, b, total, sem_a, sem_b, sem_out = refs[depth:]
    z = place()[1]
    turns = list(range(1, depth)) + [0]
    parts = [lax.rem(z + s, depth) for s in turns]
    from_a = copies([(kept_ref.at[p], a.at[i]) for i, p in enumerate(parts)], sem_a)
    from_b = copies([(got_ref.at[p], b.at[i]) for i, p in enumerate(parts)], sem_b)
    out = []
    for i, s in enumerate(turns):
        from_a[i].wait()
        from_b[i].wait()
        total[i] = (a[i].astype(F32) + b[i].astype(F32)).astype(BF)
        out += copies([(total.at[i], targets[s])], sem_out.at[pl.ds(i, 1)])
    for copy in out:
        copy.wait()


def along_sum(cost, depth, kept, got):
    height, width = kept.shape[0] // depth, kept.shape[1]
    buffer = pltpu.VMEM((depth, height, width), BF)
    return pl.pallas_call(
        along_kernel,
        in_specs=[hbm()] * 2,
        out_specs=[hbm()] * depth,
        out_shape=[jax.ShapeDtypeStruct((height, width), BF)] * depth,
        scratch_shapes=[buffer] * 3 + [dma(depth)] * 3,
        compiler_params=alone(),
        cost_estimate=cost,
        name="along_sum",
    )(kept.reshape(depth, height, width), got.reshape(depth, height, width))


def finish_kernel(*refs):
    total = refs[0][...].astype(F32)
    for ref in refs[1:-1]:
        total = total + ref[...].astype(F32)
    refs[-1][...] = total.astype(refs[-1].dtype)


def finish_sum(cost, *parts):
    return pl.pallas_call(
        finish_kernel,
        in_specs=[vmem()] * len(parts),
        out_specs=vmem(),
        out_shape=jax.ShapeDtypeStruct(parts[0].shape, parts[0].dtype),
        compiler_params=alone(),
        cost_estimate=cost,
        name="finish_sum",
    )(*parts)


def collect_kernel(*refs):
    *parts, target, held, sem_in, sem_out = refs
    depth = target.shape[0]
    z = place()[1]
    for copy in copies(
        [(ref, held.at[lax.rem(z + depth - s, depth)]) for s, ref in enumerate(parts)], sem_in
    ):
        copy.wait()
    copies([(held, target)], sem_out)[0].wait()


def collect(cost, *parts):
    depth = len(parts)
    height, width = parts[0].shape
    return pl.pallas_call(
        collect_kernel,
        in_specs=[hbm()] * depth,
        out_specs=hbm(),
        out_shape=jax.ShapeDtypeStruct((depth, height, width), BF),
        scratch_shapes=[pltpu.VMEM((depth, height, width), BF), dma(depth), dma(1)],
        compiler_params=alone(),
        cost_estimate=cost,
        name="collect",
    )(*parts).reshape(depth * height, width)


class Sum:
    def __init__(self, kept, other, route):
        self.route = route
        self.kept = kept
        self.wait = move(other, route["core"])

    def cross(self, stage):
        send, self.kept = cross_sum(self.cost, stage, self.kept, self.wait)
        self.wait = move(send, self.route[("first", "second")[stage]])
        return "kept"

    def along(self):
        self.kept, *send = along_sum(self.cost, len(self.route["depth"]) + 1, self.kept, self.wait)
        self.wait = tuple(move(part, pairs) for part, pairs in zip(send, self.route["depth"]))
        return "kept"

    def finish(self):
        self.kept = finish_sum(self.cost, self.kept, *self.wait)
        self.wait = tuple(move(self.kept, pairs) for pairs in self.route["depth"])
        return "kept"

    def gather(self):
        self.near = collect(self.cost, self.kept, *self.wait)
        self.wait, self.across, self.core = (
            move(self.near, self.route[link]) for link in ("second", "first", "core")
        )
        return "near"

    def relay(self):
        self.far = self.wait
        got, self.core_far = (move(self.far, self.route[link]) for link in ("first", "core"))
        self.wait = (self.across, got)
        return "far"

    def reflect(self):
        self.across, self.across_far = self.wait
        self.wait = (self.core, self.core_far) + tuple(
            move(value, self.route["core"]) for value in self.wait
        )
        return "across"


class Order:
    def __init__(self):
        self.before = None
        self.cost = BRIEF

    def after(self, value):
        if self.before is not None:
            owner, name = self.before
            flat = value if isinstance(value, tuple) else (value,)
            *flat, late = tie(*flat, getattr(owner, name))
            setattr(owner, name, late)
            value = tuple(flat) if isinstance(value, tuple) else flat[0]
        return value

    def run(self, total, step, *args):
        total.cost = self.cost
        total.wait = self.after(total.wait)
        self.before = (total, getattr(total, step)(*args))


class Held:
    def __init__(self, value):
        self.value = value


def widen_kernel(other, spots, *refs):
    sources, (first_ref, second_ref), (held, wide, sem_in, sem_out) = refs[:4], refs[-6:-4], refs[-4:]
    height, width = held.shape[1:]
    loads = copies([(ref, held.at[i]) for i, ref in enumerate(sources)], sem_in)
    core = place()[3] ^ other
    stores = []
    for i, load in enumerate(loads):
        near, far = side(0, core) ^ (i >> 1), side(1, core) ^ (i & 1)
        block = core * 4 + near * 2 + far
        load.wait()
        wide[i] = held[i].astype(F32)
        in_first, (row, column), (row_2, column_2) = spots(block)
        place_1 = first_ref.at[
            pl.ds(pl.multiple_of(row * height, height), height),
            pl.ds(pl.multiple_of(column * width, width), width),
        ]
        place_2 = second_ref.at[
            pl.ds(pl.multiple_of(row_2 * height, height), height),
            pl.ds(pl.multiple_of(column_2 * width, width), width),
        ]
        store_1 = pltpu.make_async_copy(wide.at[i], place_1, sem_out.at[i])
        store_2 = pltpu.make_async_copy(wide.at[i], place_2, sem_out.at[i])
        pl.when(in_first)(store_1.start)
        pl.when(jnp.logical_not(in_first))(store_2.start)
        stores.append((in_first, store_1, store_2))
    for in_first, store_1, store_2 in stores:
        pl.when(in_first)(store_1.wait)
        pl.when(jnp.logical_not(in_first))(store_2.wait)


def widen(cost, other, parts, spots, shapes, before=()):
    height, width = parts[0].shape
    return pl.pallas_call(
        functools.partial(widen_kernel, other, spots),
        in_specs=[hbm()] * (4 + len(before)),
        out_specs=[hbm()] * 2,
        out_shape=[jax.ShapeDtypeStruct(shape, F32) for shape in shapes],
        input_output_aliases={4 + i: i for i in range(len(before))},
        scratch_shapes=[
            pltpu.VMEM((4, height, width), BF),
            pltpu.VMEM((4, height, width), F32),
            dma(4),
            dma(4),
        ],
        compiler_params=alone(),
        cost_estimate=cost,
        name="widen",
    )(*parts, *before)


def spots_of(split, first, second):
    def spots(block):
        return (
            block < split,
            first(jnp.minimum(block, split - 1)),
            second(jnp.maximum(block - split, 0)),
        )

    return spots


def widen_plain_kernel(split, maps, in_ref, first_ref, second_ref, held, wide, sem_in, sem_out):
    count, height, width = held.shape
    loads = copies(
        [(in_ref.at[pl.ds(i * height, height)], held.at[i]) for i in range(count)], sem_in
    )
    stores = []
    for i, load in enumerate(loads):
        load.wait()
        wide[i] = held[i].astype(F32)
        row, column = maps[0](i) if i < split else maps[1](i - split)
        target = (first_ref if i < split else second_ref).at[
            pl.ds(row * height, height), pl.ds(column * width, width)
        ]
        stores += copies([(wide.at[i], target)], sem_out.at[pl.ds(i, 1)])
    for store in stores:
        store.wait()


def widen_plain(summed, split, shapes, maps):
    width = summed.shape[1]
    height = summed.shape[0] // 8
    return pl.pallas_call(
        functools.partial(widen_plain_kernel, split, maps),
        in_specs=[hbm()],
        out_specs=[hbm()] * 2,
        out_shape=[jax.ShapeDtypeStruct(shape, F32) for shape in shapes],
        scratch_shapes=[
            pltpu.VMEM((8, height, width), BF),
            pltpu.VMEM((8, height, width), F32),
            dma(8),
            dma(8),
        ],
        compiler_params=alone(),
        cost_estimate=BRIEF,
        name="widen_plain",
    )(summed)


def mod_weight_kernel(t_ref, g_ref, out_ref, smooth, parts, wide, sem_out):
    members, clips, width = g_ref.shape
    t = t_ref[...]
    value = (t / (1.0 + jnp.exp(-t))).astype(BF).astype(F32)
    smooth[...] = jnp.zeros_like(smooth)
    parts[...] = jnp.zeros_like(parts)
    for i in range(3):
        smooth[i * clips : (i + 1) * clips, :] = value
    left = smooth[...].astype(BF)
    slots = wide.shape[0]
    stores = []
    for member in range(members):
        rest = g_ref[member]
        for i in range(3):
            piece = rest.astype(BF).astype(F32)
            parts[i * clips : (i + 1) * clips, :] = piece
            rest = rest - piece
        if member >= slots:
            stores[member - slots].wait()
        wide[member % slots] = dot_tn(left, parts[...].astype(BF))
        target = out_ref.at[:, pl.ds(member * width, width)]
        stores += copies([(wide.at[member % slots], target)], sem_out.at[pl.ds(member, 1)])
    for store in stores[-slots:]:
        store.wait()


def mod_weight_grad(t_all, grad_clip):
    clips, width = t_all.shape
    members = grad_clip.shape[0]
    deep = -(-3 * clips // 16) * 16
    return pl.pallas_call(
        mod_weight_kernel,
        in_specs=[vmem(), vmem()],
        out_specs=hbm(),
        out_shape=jax.ShapeDtypeStruct((width, members * width), F32),
        scratch_shapes=[pltpu.VMEM((deep, width), F32)] * 2
        + [pltpu.VMEM((5, width, width), F32), dma(members)],
        compiler_params=alone(),
        cost_estimate=BRIEF,
        name="mod_weight_grad",
    )(t_all, grad_clip)


def per_device(
    tokens, t_embed, frame_clip, boxes, mod_weight, mod_bias, space_qkv, space_qv_bias, space_out,
    space_out_bias, time_qkv, time_qv_bias, time_out, time_out_bias, up_weight, up_bias,
    down_weight, down_bias, cotangent,
):
    owners = lax.axis_size("seq")
    groups = lax.axis_size("dp")
    frames = boxes.shape[0]
    width = tokens.shape[1]
    patches = tokens.shape[0] // frames
    group_frames = frame_clip.shape[0]
    pos = patches // owners
    clips = t_embed.shape[0]
    ff = up_weight.shape[1]
    depth = owners // 4
    own_route = depth <= 4
    route = routes(owners)

    clip_col = frame_clip[:, None]
    per_block = BLOCK // group_frames
    ids_row = (
        jnp.arange(per_block, dtype=jnp.int32)[:, None] * clips + frame_clip[None, :]
    ).reshape(1, BLOCK)

    def exchange(x):
        return lax.all_to_all(x, "seq", split_axis=0, concat_axis=0, tiled=True)

    qkv_maps = (lambda i: (i % 2, i // 2), lambda i: (i, 0))

    cot_send = cotangent.reshape(frames, owners, pos, width).transpose(1, 0, 2, 3)
    cot = exchange(cot_send)
    table_a = modulation(t_embed, mod_weight, mod_bias, 0, 3)
    mid_send, packed_a, attended_a, branch_a = space_forward(
        frame_clip, boxes, tokens, table_a, space_qkv, space_qv_bias, space_out, space_out_bias, owners,
    )
    mid_send, cot, t_late = tie(mid_send, cot, t_embed)
    mid = exchange(mid_send).reshape(group_frames, pos, width)
    cot = cot.reshape(group_frames, pos, width)
    table = modulation(t_late, mod_weight, mod_bias, 3, 6)
    xa, packed_b, attended_b, branch_b, mid_b, normed_c, gbranch_c, cot, gdown_b = time_forward(
        mid, cot, table, clip_col, ids_row, time_qkv, time_qv_bias, time_out, time_out_bias
    )
    ff_args = (up_weight, up_bias, down_weight, mid_b, cot, table, clip_col, down_bias)
    grad_f, gup_b0, branch_c, gnorm_c = ff_half(0, normed_c, gbranch_c, None, None, *ff_args)
    ff_shapes = ((width, ff), (ff, width))
    qkv_shapes = ((width, 3 * width), (width, width))
    qkv_spots = spots_of(6, lambda i: (i % 2, i // 2), lambda i: (i, 0))
    all_clips = clips * groups

    def mod_grads(small):
        gclip = small[: 9 * all_clips].reshape(9, all_clips, width)
        return mod_weight_grad(small[9 * all_clips : 10 * all_clips], gclip), jnp.sum(gclip, axis=1)

    def after_ff(gmid_b):
        return owner_backward(
            xa, packed_b, attended_b, branch_b, gmid_b, table, clip_col, ids_row, time_qkv, time_out
        )

    def after_time(gmid_a, gclip_b, gtout_b, gtqv_b):
        return space_backward(
            frame_clip, boxes, tokens, packed_a, attended_a, branch_a, gmid_a, table_a, space_qkv,
            space_out, t_embed, gclip_b, gclip_c, gtqv_b, gtout_b, gup_b0, gup_b1, gdown_b,
        )

    grad_f, gup_b1, gmid_b, result_send, gclip_c = ff_half(
        1, normed_c, gbranch_c, branch_c, gnorm_c, *ff_args, grad_f
    )
    result_send = result_send.reshape(owners, frames, pos, width)
    grad_f = grad_f.reshape(-1, width)
    part_f = Held(lax.psum_scatter(grad_f, BOTH, scatter_dimension=0, tiled=True))
    if own_route:
        sums = {}
        order = Order()
        wide = {}
        small = Held(None)
        small_links = [route["core"], route["x"], route["y"]] + route["swap"]
        for name, *step in SCHEDULE:
            if name == "time":
                gmid_b = order.after(gmid_b)
                gmid_send, kept_t, other_t, gclip_b, gtout_b, gtqv_b = after_ff(gmid_b)
                result = exchange(result_send)
                gmid_send, result = tie(gmid_send, result)
                gmid_a = exchange(gmid_send.reshape(owners, frames, pos, width))
                sums["t"] = Sum(kept_t, other_t, route)
                order.before = None
            elif name == "space":
                gmid_a = order.after(gmid_a)
                grad_tokens, kept_s, other_s, small.value = after_time(
                    gmid_a, gclip_b, gtout_b, gtqv_b
                )
                sums["s"] = Sum(kept_s, other_s, route)
                order.before = None
                order.cost = LONG
            elif name == "ff":
                part_f.value = order.after(part_f.value)
                order.before = (part_f, "value")
            elif name == "small":
                small.value = order.after(small.value)
                small.value = finish_sum(order.cost, small.value, move(small.value, small_links.pop(0)))
                order.before = (small, "value")
            elif name == "mod":
                small.value = order.after(small.value)
                grad_mod, grad_mod_b = mod_grads(small.value)
                mod = Held(grad_mod)
                order.before = (mod, "value")
            elif step[0] == "widen":
                total = sums[name]
                if step[1]:
                    total.wait = order.after(total.wait)
                    parts = total.wait
                else:
                    total.across = order.after(total.across)
                    parts = (total.near, total.far, total.across, total.across_far)
                before = (wide[name].value, wide[name].other) if name in wide else ()
                pair = widen(order.cost, step[1], parts, qkv_spots, qkv_shapes, before)
                done = wide[name] = Held(pair[0])
                done.other = pair[1]
                order.before = (done, "value")
            else:
                order.run(sums[name], *step)
                order.cost = BRIEF
        small, grad_mod = small.value, mod.value
        wide_time, wide_space = ((wide[k].value, wide[k].other) for k in ("t", "s"))
    else:
        result = exchange(result_send)
        gmid_send, kept_t, other_t, gclip_b, gtout_b, gtqv_b = after_ff(gmid_b)
        gmid_a = exchange(gmid_send.reshape(owners, frames, pos, width))
        grad_tokens, kept_s, other_s, small = after_time(gmid_a, gclip_b, gtout_b, gtqv_b)
        small = lax.psum(small, BOTH)
        grad_mod, grad_mod_b = mod_grads(small)
        core = place()[3]

        def whole(kept, other):
            halves = [jnp.where(core == half, kept, other) for half in range(2)]
            return lax.psum(jnp.concatenate(halves, axis=0), BOTH)

        qkv_maps = (lambda i: (i % 2, i // 2), lambda i: (i, 0))
        wide_time = widen_plain(whole(kept_t, other_t), 6, qkv_shapes, qkv_maps)
        wide_space = widen_plain(whole(kept_s, other_s), 6, qkv_shapes, qkv_maps)
    sum_f = lax.all_gather(part_f.value, BOTH, axis=0, tiled=True)
    wide_ff = widen_plain(sum_f, 4, ff_shapes, (lambda i: (0, i), lambda i: (i, 0)))
    rest = small[10 * all_clips :]
    cut = lambda start, count: rest[start : start + count].reshape(-1)
    up_rows = ff // width
    return (
        result.transpose(1, 0, 2, 3).reshape(tokens.shape),
        grad_tokens,
        grad_mod,
        grad_mod_b.reshape(-1),
        wide_space[0],
        cut(0, 2),
        wide_space[1],
        cut(2, 1),
        wide_time[0],
        cut(3, 2),
        wide_time[1],
        cut(5, 1),
        wide_ff[0],
        cut(6, up_rows),
        wide_ff[1],
        cut(6 + up_rows, 1),
    )


def solution(mesh):
    split = P(BOTH, None)
    placed = (split, P("dp", None), P("dp"), split) + (P(),) * 14 + (split,)
    return jax.shard_map(
        per_device,
        mesh=mesh,
        in_specs=placed,
        out_specs=(split, split) + (P(),) * 14,
        check_vma=False,
    )
```

time: 2290 us -> 420 us (0.18); the launches traced: 2260 us -> 414 us
  blocking collectives: 964 us -> 0 us
  local copies, waits for them, and re-layouts: 574 us -> 23 us
  waiting for transfers between devices: 506 us -> 123 us
  Pallas kernels: 0 us -> 183 us
  matrix products: 130 us -> 0 us
  starting transfers between devices: 24.6 us -> 69.7 us
  other arithmetic: 40.6 us -> 0.14 us
    unnamed x1 -> x0, blocking collectives: 938 us -> none
    unnamed x2, waiting for transfers between devices: 447 us -> 0.03 us
    unnamed x232 -> x80, local copies, waits for them, and re-layouts: 341 us -> 14.3 us
    pallas_call x0 -> x29, Pallas kernels: none -> 183 us  [the longest x2 30.1 us: ff_half(): pl.pallas_call(functools.partial(ff_kernel, last), grid=(steps,), in_spec...]
    reshape x21 -> x6, local copies, waits for them, and re-layouts: 135 us -> 5.22 us  [the longest x1 2.1 us: per_device(): cotangent.reshape(frames, owners, pos, width).transpose(1, 0, 2, 3)]
    dot_general x33 -> x0, matrix products: 123 us -> none  [the longest x1 11.9 us: per_device(): jnp.dot(smooth.astype(jnp.float32).T, grad_clip, precision=HIGH)]
    ppermute x0 -> x37, waiting for transfers between devices: none -> 98.1 us  [move(): return lax.ppermute(value, BOTH, pairs)]
    slice x18 -> x5, local copies, waits for them, and re-layouts: 66.6 us -> 1.24 us  [the longest x3 1.23 us: per_device(): cut = lambda start, count: rest[start:start + count].reshape(-1)]
  transfers between devices with their start and end apart: 4 -> 43, of which waited for: 4 -> 19; matrix products, arithmetic and copies ran while one was open for 2% -> 2% of each run, Pallas kernels for 0% -> 31%
where the time goes in v1:
time: 420 us; the launch traced here: 414 us
  Pallas kernels  183 us (44%)
  waiting for transfers between devices  123 us (29%)
  starting transfers between devices  69.7 us (17%)
  local copies, waits for them, and re-layouts  23 us (5%)
  between operations  14.7 us (4%)
    ppermute x37, waiting for transfers between devices, move(): return lax.ppermute(value, BOTH, pairs)  98.1 us
    ppermute x37, starting transfers between devices, move(): return lax.ppermute(value, BOTH, pairs)  44.9 us
    pallas_call x2, Pallas kernels, ff_half(): pl.pallas_call(functools.partial(ff_kernel, last), grid=(steps,), in_spec...  30.1 us
    pallas_call x1, Pallas kernels, owner_backward(): pl.pallas_call(owner_backward_kernel, in_specs=[vmem()] * 10, out_specs=[...  25.5 us
    pallas_call x1, Pallas kernels, space_backward(): pl.pallas_call(space_backward_kernel, in_specs=[smem(), smem()] + [vmem()...  25.3 us
    all_to_all x4, waiting for transfers between devices, exchange(): return lax.all_to_all(x, 'seq', split_axis=0, concat_axis=0, tiled=True)  24.8 us
    all_to_all x4, starting transfers between devices, exchange(): return lax.all_to_all(x, 'seq', split_axis=0, concat_axis=0, tiled=True)  24.2 us
    pallas_call x1, Pallas kernels, time_forward(): pl.pallas_call(time_forward_kernel, in_specs=[vmem()] * 9, out_specs=[vme...  15.4 us
  transfers between devices with their start and end apart: 43, of which 19 were waited for; matrix products, arithmetic and copies ran while one was open for 2% of the time, Pallas kernels for 31%

profile of v1, /device:TPU:0, one launch (start us, length us, event | category | flops | bytes accessed | tf_op | source)
XLA Modules:
  0.0 413.9 jit_solution(13704455372049477851)
XLA Ops:
  9.3 7.4 %all-to-all-start = ((bf16[16,2,16,768]{3,2,1,0:T(8,128)(2,1)}), bf16[16,2,16,768]{3,2,1,0:T(8,128)(2,1)S(1)}, u32[]{:S(2)}, u32[]{:S(2)}) async-start(bf16[16,2,16,768]{3,2,1,0:T(8,128)(2,1)} %bitcast.25), calls=%async_computation | async-start | bytes 1572864 | tf_op jit(solution)/shard_map/all_to_all | solution.py:1134
  20.4 12.8 %space_forward.1 = (bf16[16,2,16,768]{3,2,1,0:T(8,128)(2,1)}, bf16[512,2304]{1,0:T(8,128)(2,1)}, bf16[512,768]{1,0:T(8,128)(2,1)}, f32[512,768]{1,0:T(8,128)}) custom-call(s32[32]{0:T(128)} %clip_ref.3, s32[2,4]{1,0:T(2,128)} %box_ref.3, bf16[512,768]{1,0:T(8,128)(2,1)} %x_ref.3, f32[3,2,768]{2,1,0:T(2,128)} %modulation.2.table_ref, ...), custom_call_target="tpu_custom_call" | custom-call | flops 1000 | bytes 1000 | tf_op jit(solution)/shard_map/space_forward/pallas_call | solution.py:256
  42.9 6.0 %modulation.3.table_ref = f32[6,2,768]{2,1,0:T(2,128)} custom-call(bf16[2,768]{1,0:T(2,128)(2,1)} %t_ref.4, bf16[768,6912]{1,0:T(8,128)(2,1)} %w_ref.3, bf16[6912]{0:T(1024)(128)(2,1)} %b_ref.3), custom_call_target="tpu_custom_call" | custom-call | flops 1000 | bytes 1000 | tf_op jit(solution)/shard_map/modulation/pallas_call | solution.py:164
  48.9 10.7 %all-to-all-done.1 = bf16[16,2,16,768]{3,2,1,0:T(8,128)(2,1)S(1)} async-done(((bf16[16,2,16,768]{3,2,1,0:T(8,128)(2,1)}), bf16[16,2,16,768]{3,2,1,0:T(8,128)(2,1)S(1)}, u32[]{:S(2)}, u32[]{:S(2)}) %all-to-all-start.1) | async-done | bytes 786464 | tf_op jit(solution)/shard_map/all_to_all | solution.py:1134
  60.5 15.4 %time_forward.1 = (bf16[512,768]{1,0:T(8,128)(2,1)}, bf16[512,2304]{1,0:T(8,128)(2,1)}, bf16[512,768]{1,0:T(8,128)(2,1)}, f32[512,768]{1,0:T(8,128)}, f32[512,76...) custom-call(bf16[32,16,768]{2,1,0:T(8,128)(2,1)} %bitcast.28, ...), custom_call_target="tpu_custom_call" | custom-call | flops 1000 | bytes 1000 | tf_op jit(solution)/shard_map/time_forward/pallas_call | solution.py:377
  75.9 13.1 %ff_half_0.1 = (bf16[2,3072,768]{2,1,0:T(8,128)(2,1)}, f32[2,1,768]{2,1,0:T(1,128)}, f32[512,768]{1,0:T(8,128)}, f32[512,768]{1,0:T(8,128)}) custom-call(bf16[512,768]{1,0:T(8,128)(2,1)} %get-tuple-element.150.normed_ref, bf16[512,768]{1,0:T(8,128)(2,1)} %get-tuple-element.151.gbranch_ref, f32[512,768]{1,0:T(8,128)} %get-tuple-element.152.branch_in.gnorm_in.midb_ref, ...), custom_call_target="tpu_custom_call" | custom-call | flops 1000 | bytes 1000 | tf_op jit(solution)/shard_map/ff_half_0/pallas_call | solution.py:508
  89.0 17.0 %ff_half_1.1 = (bf16[2,3072,768]{2,1,0:T(8,128)(2,1)}, f32[2,1,768]{2,1,0:T(1,128)}, f32[512,768]{1,0:T(8,128)}, bf16[32,16,768]{2,1,0:T(8,128)(2,1)}, f32[3,2,768]{2,1,0:T(2,128)}) custom-call(bf16[512,768]{1,0:T(8,128)(2,1)} %get-tuple-element.150.normed_ref, bf16[512,768]{1,0:T(8,128)(2,1)} %get-tuple-element.151.gbranch_ref, ...), custom_call_target="tpu_custom_call", output_to_operand_aliasing={{0}: (12, {})} | custom-call | flops 1000 | bytes 1000 | tf_op jit(solution)/shard_map/ff_half_1/pallas_call | solution.py:508
  106.1 5.5 %all-to-all-start.2 = ((bf16[16,2,16,768]{3,2,1,0:T(8,128)(2,1)}), bf16[16,2,16,768]{3,2,1,0:T(8,128)(2,1)S(1)}, u32[]{:S(2)}, u32[]{:S(2)}) async-start(bf16[16,2,16,768]{3,2,1,0:T(8,128)(2,1)} %bitcast.5), calls=%async_computation.2 | async-start | bytes 1572864 | tf_op jit(solution)/shard_map/all_to_all | solution.py:1134
  111.5 25.5 %owner_backward.1 = (bf16[32,16,768]{2,1,0:T(8,128)(2,1)}, bf16[1536,768]{1,0:T(8,128)(2,1)}, bf16[1536,768]{1,0:T(8,128)(2,1)}, f32[3,2,768]{2,1,0:T(2,128)}, f32[1,768]{1,0:T(1,128)}, /*index=5*/f32[2,768]{1,0:T(2,128)}) custom-call(bf16[512,768]{1,0:T(8,128)(2,1)} %get-tuple-element.146.xa_ref, bf16[512,2304]{1,0:T(8,128)(2,1)} %get-tuple-element.147.packed_ref, ...), custom_call_target="tpu_custom_call" | custom-call | flops 30000001024 | bytes 1000 | tf_op jit(solution)/shard_map/owner_backward/pallas_call | solution.py:606
  137.5 5.8 %all-to-all-start.3 = ((bf16[16,2,16,768]{3,2,1,0:T(8,128)(2,1)}), bf16[16,2,16,768]{3,2,1,0:T(8,128)(2,1)}, u32[]{:S(2)}, u32[]{:S(2)}) async-start(bf16[16,2,16,768]{3,2,1,0:T(8,128)(2,1)} %bitcast.46), calls=%async_computation.3 | async-start | bytes 1572864 | tf_op jit(solution)/shard_map/all_to_all | solution.py:1134
  150.1 12.0 %all-to-all-done.3.gmid_ref = bf16[16,2,16,768]{3,2,1,0:T(8,128)(2,1)} async-done(((bf16[16,2,16,768]{3,2,1,0:T(8,128)(2,1)}), bf16[16,2,16,768]{3,2,1,0:T(8,128)(2,1)}, u32[]{:S(2)}, u32[]{:S(2)}) %all-to-all-start.3) | async-done | bytes 786464 | tf_op jit(solution)/shard_map/all_to_all | solution.py:1134
  162.1 25.3 %space_backward.1 = (bf16[512,768]{1,0:T(8,128)(2,1)}, bf16[1536,768]{1,0:T(8,128)(2,1)}, bf16[1536,768]{1,0:T(8,128)(2,1)}, f32[56,768]{1,0:T(8,128)}) custom-call(s32[32]{0:T(128)} %clip_ref.3, s32[2,4]{1,0:T(2,128)} %box_ref.3, bf16[512,768]{1,0:T(8,128)(2,1)} %x_ref.3, bf16[512,2304]{1,0:T(8,128)(2,1)} %get-tuple-element.161.packed_ref, ...), custom_call_target="tpu_custom_call" | custom-call | flops 30000001024 | bytes 1000 | tf_op jit(solution)/shard_map/space_backward/pallas_call | solution.py:700
  203.9 16.3 %collective-permute-done.2 = bf16[384,768]{1,0:T(8,128)(2,1)S(1)} collective-permute-done((bf16[384,768]{1,0:T(8,128)(2,1)S(1)}, bf16[384,768]{1,0:T(8,128)(2,1)S(1)}, u32[]{:S(2)}, u32[]{:S(2)}) %collective-permute-start.2) | collective-permute-done | bytes 589856 | tf_op jit(solution)/shard_map/ppermute | solution.py:756
  223.3 5.6 %collective-permute-done.9.refs_1_ = f32[56,768]{1,0:T(8,128)S(1)} collective-permute-done((f32[56,768]{1,0:T(8,128)}, f32[56,768]{1,0:T(8,128)S(1)}, u32[]{:S(2)}, u32[]{:S(2)}) %collective-permute-start.9) | collective-permute-done | bytes 172064 | tf_op jit(solution)/shard_map/ppermute | solution.py:756
  247.2 8.2 %collective-permute-done.6.refs_2_ = bf16[96,768]{1,0:T(8,128)(2,1)S(1)} collective-permute-done((bf16[96,768]{1,0:T(8,128)(2,1)S(1)}, bf16[96,768]{1,0:T(8,128)(2,1)S(1)}, u32[]{:S(2)}, u32[]{:S(2)}) %collective-permute-start.6) | collective-permute-done | bytes 147488 | tf_op jit(solution)/shard_map/ppermute | solution.py:756
  271.0 7.1 %collective-permute-done.11.refs_2_ = bf16[96,768]{1,0:T(8,128)(2,1)S(1)} collective-permute-done((bf16[96,768]{1,0:T(8,128)(2,1)}, bf16[96,768]{1,0:T(8,128)(2,1)S(1)}, u32[]{:S(2)}, u32[]{:S(2)}) %collective-permute-start.11) | collective-permute-done | bytes 147488 | tf_op jit(solution)/shard_map/ppermute | solution.py:756
  291.2 5.6 %collective-permute-done.16.refs_1_ = bf16[96,768]{1,0:T(8,128)(2,1)S(1)} collective-permute-done((bf16[96,768]{1,0:T(8,128)(2,1)}, bf16[96,768]{1,0:T(8,128)(2,1)S(1)}, u32[]{:S(2)}, u32[]{:S(2)}) %collective-permute-start.16) | collective-permute-done | bytes 147488 | tf_op jit(solution)/shard_map/ppermute | solution.py:756
  296.8 8.5 %collective-permute-done.17.refs_2_ = bf16[96,768]{1,0:T(8,128)(2,1)S(1)} collective-permute-done((bf16[96,768]{1,0:T(8,128)(2,1)}, bf16[96,768]{1,0:T(8,128)(2,1)S(1)}, u32[]{:S(2)}, u32[]{:S(2)}) %collective-permute-start.17) | collective-permute-done | bytes 147488 | tf_op jit(solution)/shard_map/ppermute | solution.py:756
  308.8 8.0 %collective-permute-start.22 = (f32[56,768]{1,0:T(8,128)}, f32[56,768]{1,0:T(8,128)S(1)}, u32[]{:S(2)}, u32[]{:S(2)}) collective-permute-start(f32[56,768]{1,0:T(8,128)} %finish_sum.10.refs_0_), channel_id=1, source_target_pairs={{0,4},{1,5},{2,6},{3,7},{4,0},{5,1},{6,2},{7,3},{8,12},{9,13},{10,... | collective-permute-start | bytes 516104 | tf_op jit(solution)/shard_map/ppermute | solution.py:756
  319.2 15.0 %collective-permute-done.22.refs_1_ = f32[56,768]{1,0:T(8,128)S(1)} collective-permute-done((f32[56,768]{1,0:T(8,128)}, f32[56,768]{1,0:T(8,128)S(1)}, u32[]{:S(2)}, u32[]{:S(2)}) %collective-permute-start.22) | collective-permute-done | bytes 172064 | tf_op jit(solution)/shard_map/ppermute | solution.py:756
  336.7 7.0 %collective-permute-done.21.refs_3_ = bf16[96,768]{1,0:T(8,128)(2,1)S(1)} collective-permute-done((bf16[96,768]{1,0:T(8,128)(2,1)}, bf16[96,768]{1,0:T(8,128)(2,1)S(1)}, u32[]{:S(2)}, u32[]{:S(2)}) %collective-permute-start.21) | collective-permute-done | bytes 147488 | tf_op jit(solution)/shard_map/ppermute | solution.py:756
  348.3 14.7 %collective-permute-done.27.refs_1_ = f32[56,768]{1,0:T(8,128)S(1)} collective-permute-done((f32[56,768]{1,0:T(8,128)}, f32[56,768]{1,0:T(8,128)S(1)}, u32[]{:S(2)}, u32[]{:S(2)}) %collective-permute-start.27) | collective-permute-done | bytes 172064 | tf_op jit(solution)/shard_map/ppermute | solution.py:756
  376.2 8.8 %mod_weight_grad.1 = f32[768,6912]{1,0:T(8,128)} custom-call(f32[4,768]{1,0:T(4,128)} %get-tuple-element.272.t_ref, f32[9,4,768]{2,1,0:T(4,128)} %reshape.169.g_ref), custom_call_target="tpu_custom_call" | custom-call | flops 1000 | bytes 1000 | tf_op jit(solution)/shard_map/mod_weight_grad/pallas_call | solution.py:1096
  397.8 9.0 %widen_plain.1 = (f32[768,3072]{1,0:T(8,128)}, f32[3072,768]{1,0:T(8,128)}) custom-call(bf16[6144,768]{1,0:T(8,128)(2,1)} %all-gather.2.cloned.1.call-done.in_ref), custom_call_target="tpu_custom_call" | custom-call | flops 1000 | bytes 1000 | tf_op jit(solution)/shard_map/widen_plain/pallas_call | solution.py:1049
  (190 shorter events, 128.8 us)
Async XLA Ops:
  9.3 26.1 %all-to-all-start = ((bf16[16,2,16,768]{3,2,1,0:T(8,128)(2,1)}), bf16[16,2,16,768]{3,2,1,0:T(8,128)(2,1)S(1)}, u32[]{:S(2)}, u32[]{:S(2)}) async-start(bf16[16,2,16,768]{3,2,1,0:T(8,128)(2,1)} %bitcast.25), calls=%async_computation | async-start | bytes 1572864 | tf_op jit(solution)/shard_map/all_to_all | solution.py:1134
  35.4 24.2 %all-to-all-start.1 = ((bf16[16,2,16,768]{3,2,1,0:T(8,128)(2,1)}), bf16[16,2,16,768]{3,2,1,0:T(8,128)(2,1)S(1)}, u32[]{:S(2)}, u32[]{:S(2)}) async-start(bf16[16,2,16,768]{3,2,1,0:T(8,128)(2,1)} %get-tuple-element.143), calls=%async_computation.1 | async-start | bytes 1572864 | tf_op jit(solution)/shard_map/all_to_all | solution.py:1134
  40.9 217.1 %reduce-scatter.2.cloned.1.call-start = ((), (), s32[]{:S(2)}) async-start(), calls=%async_computation.5 | async-start | bytes 9732096 | tf_op jit(solution)/shard_map/reduce_scatter | solution.py:1178
  106.1 31.4 %all-to-all-start.2 = ((bf16[16,2,16,768]{3,2,1,0:T(8,128)(2,1)}), bf16[16,2,16,768]{3,2,1,0:T(8,128)(2,1)S(1)}, u32[]{:S(2)}, u32[]{:S(2)}) async-start(bf16[16,2,16,768]{3,2,1,0:T(8,128)(2,1)} %bitcast.5), calls=%async_computation.2 | async-start | bytes 1572864 | tf_op jit(solution)/shard_map/all_to_all | solution.py:1134
  137.5 24.6 %all-to-all-start.3 = ((bf16[16,2,16,768]{3,2,1,0:T(8,128)(2,1)}), bf16[16,2,16,768]{3,2,1,0:T(8,128)(2,1)}, u32[]{:S(2)}, u32[]{:S(2)}) async-start(bf16[16,2,16,768]{3,2,1,0:T(8,128)(2,1)} %bitcast.46), calls=%async_computation.3 | async-start | bytes 1572864 | tf_op jit(solution)/shard_map/all_to_all | solution.py:1134
  143.3 254.5 %all-gather.2.cloned.1.call-start = ((), (), s32[]{:S(2)}) async-start(), calls=%async_computation.6 | async-start | bytes 9732096 | tf_op jit(solution)/shard_map/all_gather | solution.py:1248
  148.6 39.1 %collective-permute-start.1 = (bf16[768,768]{1,0:T(8,128)(2,1)}, bf16[768,768]{1,0:T(8,128)(2,1)}, u32[]{:S(2)}, u32[]{:S(2)}) collective-permute-start(bf16[768,768]{1,0:T(8,128)(2,1)} %get-tuple-element.179), channel_id=1, source_target_pairs={{0,16},{1,3},{2,18},{3,1},{4,20},{5,7},{6,22},{7,5},{8,24},{9,11},... | collective-permute-start | bytes 3538952 | tf_op jit(solution)/shard_map/ppermute | solution.py:756
  197.1 34.2 %collective-permute-start.8 = (bf16[768,768]{1,0:T(8,128)(2,1)}, bf16[768,768]{1,0:T(8,128)(2,1)S(1)}, u32[]{:S(2)}, u32[]{:S(2)}) collective-permute-start(bf16[768,768]{1,0:T(8,128)(2,1)} %get-tuple-element.197), channel_id=1, source_target_pairs={{0,16},{1,3},{2,18},{3,1},{4,20},{5,7},{6,22},{7,5},{8,24},{9,11},... | collective-permute-start | bytes 3538952 | tf_op jit(solution)/shard_map/ppermute | solution.py:756
  198.8 21.5 %collective-permute-start.2 = (bf16[384,768]{1,0:T(8,128)(2,1)S(1)}, bf16[384,768]{1,0:T(8,128)(2,1)S(1)}, u32[]{:S(2)}, u32[]{:S(2)}) collective-permute-start(bf16[384,768]{1,0:T(8,128)(2,1)S(1)} %copy-done.36), channel_id=1, source_target_pairs={{0,2},{1,17},{2,0},{3,19},{4,6},{5,21},{6,4},{7,23},{8,10},{9,25},... | collective-permute-start | bytes 1769480 | tf_op jit(solution)/shard_map/ppermute | solution.py:756
  234.9 23.1 %collective-permute-start.13 = (bf16[384,768]{1,0:T(8,128)(2,1)}, bf16[384,768]{1,0:T(8,128)(2,1)S(1)}, u32[]{:S(2)}, u32[]{:S(2)}) collective-permute-start(bf16[384,768]{1,0:T(8,128)(2,1)} %get-tuple-element.207), channel_id=1, source_target_pairs={{0,2},{1,17},{2,0},{3,19},{4,6},{5,21},{6,4},{7,23},{8,10},{9,25},... | collective-permute-start | bytes 1769480 | tf_op jit(solution)/shard_map/ppermute | solution.py:756
  281.3 27.1 %collective-permute-start.15 = (bf16[384,768]{1,0:T(8,128)(2,1)}, bf16[384,768]{1,0:T(8,128)(2,1)S(1)}, u32[]{:S(2)}, u32[]{:S(2)}) collective-permute-start(bf16[384,768]{1,0:T(8,128)(2,1)} %bitcast.38), channel_id=1, source_target_pairs={{0,2},{1,17},{2,0},{3,19},{4,6},{5,21},{6,4},{7,23},{8,10},{9,25},... | collective-permute-start | bytes 1769480 | tf_op jit(solution)/shard_map/ppermute | solution.py:756
  287.2 18.0 %collective-permute-start.17 = (bf16[96,768]{1,0:T(8,128)(2,1)}, bf16[96,768]{1,0:T(8,128)(2,1)S(1)}, u32[]{:S(2)}, u32[]{:S(2)}) collective-permute-start(bf16[96,768]{1,0:T(8,128)(2,1)} %get-tuple-element.217), channel_id=1, source_target_pairs={{0,8},{1,9},{2,10},{3,11},{4,12},{5,13},{6,14},{7,15},{8,0},{9,1},... | collective-permute-start | bytes 442376 | tf_op jit(solution)/shard_map/ppermute | solution.py:756
  290.5 56.0 %collective-permute-start.25 = (bf16[384,768]{1,0:T(8,128)(2,1)}, bf16[384,768]{1,0:T(8,128)(2,1)}, u32[]{:S(2)}, u32[]{:S(2)}) collective-permute-start(bf16[384,768]{1,0:T(8,128)(2,1)} %bitcast.39), channel_id=1, source_target_pairs={{0,16},{1,3},{2,18},{3,1},{4,20},{5,7},{6,22},{7,5},{8,24},{9,11},... | collective-permute-start | bytes 1769480 | tf_op jit(solution)/shard_map/ppermute | solution.py:756
  308.4 38.1 %collective-permute-start.26 = (bf16[384,768]{1,0:T(8,128)(2,1)S(1)}, bf16[384,768]{1,0:T(8,128)(2,1)}, u32[]{:S(2)}, u32[]{:S(2)}) collective-permute-start(bf16[384,768]{1,0:T(8,128)(2,1)S(1)} %collective-permute-done.15.refs_1_), channel_id=1, source_target_pairs={{0,16},{1,3},{2,18},{3,1},{4,20},{5,7},{6,22},{7,5},{8,24},{9,11},... | collective-permute-start | bytes 1769480 | tf_op jit(solution)/shard_map/ppermute | solution.py:756
  308.8 25.4 %collective-permute-start.22 = (f32[56,768]{1,0:T(8,128)}, f32[56,768]{1,0:T(8,128)S(1)}, u32[]{:S(2)}, u32[]{:S(2)}) collective-permute-start(f32[56,768]{1,0:T(8,128)} %finish_sum.10.refs_0_), channel_id=1, source_target_pairs={{0,4},{1,5},{2,6},{3,7},{4,0},{5,1},{6,2},{7,3},{8,12},{9,13},{10,... | collective-permute-start | bytes 516104 | tf_op jit(solution)/shard_map/ppermute | solution.py:756
  316.8 19.8 %collective-permute-start.19 = (bf16[96,768]{1,0:T(8,128)(2,1)}, bf16[96,768]{1,0:T(8,128)(2,1)S(1)}, u32[]{:S(2)}, u32[]{:S(2)}) collective-permute-start(bf16[96,768]{1,0:T(8,128)(2,1)} %finish_sum.11.refs_0_), channel_id=1, source_target_pairs={{0,4},{1,5},{2,6},{3,7},{4,8},{5,9},{6,10},{7,11},{8,12},{9,13},{1... | collective-permute-start | bytes 442376 | tf_op jit(solution)/shard_map/ppermute | solution.py:756
  316.8 19.9 %collective-permute-start.20 = (bf16[96,768]{1,0:T(8,128)(2,1)}, bf16[96,768]{1,0:T(8,128)(2,1)S(1)}, u32[]{:S(2)}, u32[]{:S(2)}) collective-permute-start(bf16[96,768]{1,0:T(8,128)(2,1)} %finish_sum.11.refs_0_), channel_id=1, source_target_pairs={{0,8},{1,9},{2,10},{3,11},{4,12},{5,13},{6,14},{7,15},{8,0},{9,1},... | collective-permute-start | bytes 442376 | tf_op jit(solution)/shard_map/ppermute | solution.py:756
  346.4 22.4 %collective-permute-start.24 = (bf16[384,768]{1,0:T(8,128)(2,1)}, bf16[384,768]{1,0:T(8,128)(2,1)}, u32[]{:S(2)}, u32[]{:S(2)}) collective-permute-start(bf16[384,768]{1,0:T(8,128)(2,1)} %bitcast.34), channel_id=1, source_target_pairs={{0,2},{1,17},{2,0},{3,19},{4,6},{5,21},{6,4},{7,23},{8,10},{9,25},... | collective-permute-start | bytes 1769480 | tf_op jit(solution)/shard_map/ppermute | solution.py:756
  346.5 22.8 %collective-permute-start.29 = (bf16[384,768]{1,0:T(8,128)(2,1)S(1)}, bf16[384,768]{1,0:T(8,128)(2,1)S(1)}, u32[]{:S(2)}, u32[]{:S(2)}) collective-permute-start(bf16[384,768]{1,0:T(8,128)(2,1)S(1)} %bitcast.41), channel_id=1, source_target_pairs={{0,1},{1,0},{2,3},{3,2},{4,5},{5,4},{6,7},{7,6},{8,9},{9,8},{10,11... | collective-permute-start | bytes 1769480 | tf_op jit(solution)/shard_map/ppermute | solution.py:756
  346.6 16.5 %collective-permute-start.27 = (f32[56,768]{1,0:T(8,128)}, f32[56,768]{1,0:T(8,128)S(1)}, u32[]{:S(2)}, u32[]{:S(2)}) collective-permute-start(f32[56,768]{1,0:T(8,128)} %finish_sum.12.refs_0_), channel_id=1, source_target_pairs={{0,8},{1,9},{2,10},{3,11},{4,12},{5,13},{6,14},{7,15},{8,0},{9,1},... | collective-permute-start | bytes 516104 | tf_op jit(solution)/shard_map/ppermute | solution.py:756
  347.8 23.1 %collective-permute-start.30 = (bf16[384,768]{1,0:T(8,128)(2,1)S(1)}, bf16[384,768]{1,0:T(8,128)(2,1)}, u32[]{:S(2)}, u32[]{:S(2)}) collective-permute-start(bf16[384,768]{1,0:T(8,128)(2,1)S(1)} %collective-permute-done.15.refs_1_), channel_id=1, source_target_pairs={{0,1},{1,0},{2,3},{3,2},{4,5},{5,4},{6,7},{7,6},{8,9},{9,8},{10,11... | collective-permute-start | bytes 1769480 | tf_op jit(solution)/shard_map/ppermute | solution.py:756
  347.9 22.9 %collective-permute-start.31 = (bf16[384,768]{1,0:T(8,128)(2,1)}, bf16[384,768]{1,0:T(8,128)(2,1)}, u32[]{:S(2)}, u32[]{:S(2)}) collective-permute-start(bf16[384,768]{1,0:T(8,128)(2,1)} %collective-permute-done.25.refs_2_), channel_id=1, source_target_pairs={{0,1},{1,0},{2,3},{3,2},{4,5},{5,4},{6,7},{7,6},{8,9},{9,8},{10,11... | collective-permute-start | bytes 1769480 | tf_op jit(solution)/shard_map/ppermute | solution.py:756
  370.9 22.3 %collective-permute-start.33 = (bf16[384,768]{1,0:T(8,128)(2,1)S(1)}, bf16[384,768]{1,0:T(8,128)(2,1)S(1)}, u32[]{:S(2)}, u32[]{:S(2)}) collective-permute-start(bf16[384,768]{1,0:T(8,128)(2,1)S(1)} %bitcast.37), channel_id=1, source_target_pairs={{0,1},{1,0},{2,3},{3,2},{4,5},{5,4},{6,7},{7,6},{8,9},{9,8},{10,11... | collective-permute-start | bytes 1769480 | tf_op jit(solution)/shard_map/ppermute | solution.py:756
  370.9 22.3 %collective-permute-start.34 = (bf16[384,768]{1,0:T(8,128)(2,1)}, bf16[384,768]{1,0:T(8,128)(2,1)S(1)}, u32[]{:S(2)}, u32[]{:S(2)}) collective-permute-start(bf16[384,768]{1,0:T(8,128)(2,1)} %collective-permute-done.24.refs_1_), channel_id=1, source_target_pairs={{0,1},{1,0},{2,3},{3,2},{4,5},{5,4},{6,7},{7,6},{8,9},{9,8},{10,11... | collective-permute-start | bytes 1769480 | tf_op jit(solution)/shard_map/ppermute | solution.py:756
  (60 other events, 538.2 us)
Sparse Core Ops, SparseCore 0:
  106.2 150.1 reduce-scatter.1
  259.7 104.4 all-gather.1

commit v2 on v1

--- a/solution.py
+++ b/solution.py
@@ -18,33 +18,37 @@
 VMEM_BYTES = 56 * 1024 * 1024
 BOTH = ("dp", "seq")
 BRIEF = pl.CostEstimate(flops=1000, bytes_accessed=1000, transcendentals=0)
+MIDDLE = pl.CostEstimate(flops=10**10, bytes_accessed=1000, transcendentals=0)
 LONG = pl.CostEstimate(flops=3 * 10**10, bytes_accessed=1000, transcendentals=0)
 
+COSTS = {
+    ("t", "cross", 1): LONG,
+    ("t", "along"): MIDDLE,
+    ("t", "finish"): MIDDLE,
+    ("s", "along"): MIDDLE,
+    ("t", "gather"): MIDDLE,
+    ("s", "finish"): MIDDLE,
+    ("s", "gather"): MIDDLE,
+}
 SCHEDULE = (
     ("time",),
     ("t", "cross", 0),
     ("space",),
     ("t", "cross", 1),
     ("s", "cross", 0),
-    ("small",),
     ("t", "along"),
-    ("small",),
     ("s", "cross", 1),
     ("t", "finish"),
-    ("ff",),
     ("s", "along"),
-    ("small",),
     ("t", "gather"),
     ("s", "finish"),
+    ("ff",),
     ("t", "relay"),
-    ("small",),
     ("s", "gather"),
     ("t", "reflect"),
-    ("small",),
     ("t", "widen", 0),
     ("s", "relay"),
     ("t", "widen", 1),
-    ("mod",),
     ("s", "reflect"),
     ("s", "widen", 0),
     ("s", "widen", 1),
@@ -127,14 +131,14 @@
             dq = dk = dv = 0.0
             for half in halves:
                 kh = k * half
-                s = dot_nt(q, kh) * factor + bias(b)
-                e = jnp.exp(s - jnp.max(s, axis=-1, keepdims=True))
-                p = e * (1.0 / jnp.sum(e, axis=-1, keepdims=True))
-                gs = dot_nt(g, v * half)
-                ds = (p * (gs - jnp.sum(p * gs, axis=-1, keepdims=True))).astype(BF)
-                dv = dv + dot_tn(p.astype(BF), g * half)
-                dq = dq + dot_nn(ds, kh)
-                dk = dk + dot_tn(ds, q * half)
+                s = dot_nt(kh, q) * factor + bias(b)
+                e = jnp.exp(s - jnp.max(s, axis=0, keepdims=True))
+                p = e * (1.0 / jnp.sum(e, axis=0, keepdims=True))
+                gs = dot_nt(v * half, g)
+                ds = (p * (gs - jnp.sum(p * gs, axis=0, keepdims=True))).astype(BF)
+                dv = dv + dot_nn(p.astype(BF), g * half)
+                dq = dq + dot_tn(ds, kh)
+                dk = dk + dot_nn(ds, q * half)
             grad_packed[rows, pl.ds(off, 2 * HD)] = (dq * factor).astype(BF)
             grad_packed[rows, pl.ds(width + off, 2 * HD)] = (dk * factor).astype(BF)
             grad_packed[rows, pl.ds(2 * width + off, 2 * HD)] = dv.astype(BF)
@@ -216,22 +220,34 @@
 
 
 def space_forward_kernel(
-    clip_ref, box_ref, x_ref, table_ref, wqkv_ref, bqv_ref, wout_ref, bout_ref,
-    send_ref, packed_ref, attended_ref, branch_ref, normed,
+    ready, flush,
+    clip_ref, box_ref, t_ref, modw_ref, modb_ref, x_ref, wqkv_ref, bqv_ref, wout_ref, bout_ref,
+    send_ref, packed_ref, attended_ref, branch_ref, table_ref, normed,
 ):
     frames = box_ref.shape[0]
     width = x_ref.shape[1]
     dst, _, pos, _ = send_ref.shape
     clip = own_clips(clip_ref, frames)
+    t = t_ref[...].astype(F32)
+    smooth = (t / (1.0 + jnp.exp(-t))).astype(BF)
+    ready(modw_ref)
+    for k in range(3):
+        cols = pl.ds(k * width, width)
+        table_ref[k] = dot_nn(smooth, modw_ref[:, cols]) + as_row(modb_ref[cols])
+    ready(x_ref)
     for f in range(frames):
         rows = pl.ds(f * BLOCK, BLOCK)
         n, _ = normalize(x_ref[rows, :].astype(F32))
         shift = frame_row(table_ref, 0, clip[f])
         scale = frame_row(table_ref, 1, clip[f])
         normed[rows, :] = (n * (1.0 + scale) + shift).astype(BF)
+    ready(wqkv_ref)
     project_qkv(normed, wqkv_ref, bqv_ref, packed_ref, width)
+    flush(packed_ref)
     biases = [visible_bias(box_ref, f, BLOCK) for f in range(frames)]
     attend(packed_ref, attended_ref, lambda b: biases[b], frames, width)
+    flush(attended_ref)
+    ready(wout_ref)
     for f in range(frames):
         rows = pl.ds(f * BLOCK, BLOCK)
         branch = dot_nn(attended_ref[rows, :], wout_ref[...]) + as_row(bout_ref[...])
@@ -239,6 +255,7 @@
         gate = frame_row(table_ref, 2, clip[f])
         mid = x_ref[rows, :].astype(F32) + gate * branch
         send_ref[:, f] = mid.astype(BF).reshape(dst, pos, width)
+    flush(send_ref, branch_ref)
 
 
 def vmem():
@@ -249,25 +266,105 @@
     return pl.BlockSpec(memory_space=pltpu.SMEM)
 
 
-def space_forward(frame_clip, boxes, tokens, table, wqkv, bqv, wout, bout, owners):
+def hbm():
+    return pl.BlockSpec(memory_space=pltpu.HBM)
+
+
+def dma(count):
+    return pltpu.SemaphoreType.DMA((count,))
+
+
+def copies(pairs, semaphores):
+    started = [
+        pltpu.make_async_copy(source, target, semaphores.at[i])
+        for i, (source, target) in enumerate(pairs)
+    ]
+    for copy in started:
+        copy.start()
+    return started
+
+
+def streamed(body, args, late, out_shape, late_out, scratch, cost, name, small=0, cut=()):
+    cut = dict(cut)
+    n, m = len(args), len(out_shape)
+
+    def shape_of(i):
+        shape = args[i].shape
+        return shape[:-1] + (cut[i],) if i in cut else shape
+
+    def kernel(*refs):
+        refs = list(refs)
+        ins, outs, rest = refs[:n], refs[n : n + m], refs[n + m :]
+        own, rest = rest[: len(scratch)], rest[len(scratch) :]
+        in_buffers, out_buffers, (sem_in, sem_out) = rest[: len(late)], rest[len(late) : -2], rest[-2:]
+        sources = [ins[i].at[:, pl.ds(0, cut[i])] if i in cut else ins[i] for i in late]
+        waiting = list(zip(in_buffers, copies(list(zip(sources, in_buffers)), sem_in)))
+        for i, buffer in zip(late, in_buffers):
+            ins[i] = buffer
+        pending = dict(zip(late_out, out_buffers))
+        targets = {i: outs[i] for i in late_out}
+        for i in late_out:
+            outs[i] = pending[i]
+        leaving = []
+
+        def ready(*buffers):
+            for buffer in buffers:
+                for entry in list(waiting):
+                    if entry[0] is buffer:
+                        entry[1].wait()
+                        waiting.remove(entry)
+
+        def flush(*buffers):
+            for buffer in buffers:
+                for k, i in enumerate(late_out):
+                    if out_buffers[k] is buffer:
+                        leaving.extend(copies([(buffer, targets[i])], sem_out.at[pl.ds(k, 1)]))
+
+        body(ready, flush, *ins, *outs, *own)
+        for copy in leaving:
+            copy.wait()
+
+    in_specs = [smem() if i < small else hbm() if i in late else vmem() for i in range(n)]
+    return pl.pallas_call(
+        kernel,
+        in_specs=in_specs,
+        out_specs=[hbm() if i in late_out else vmem() for i in range(m)],
+        out_shape=out_shape,
+        scratch_shapes=list(scratch)
+        + [pltpu.VMEM(shape_of(i), args[i].dtype) for i in late]
+        + [pltpu.VMEM(out_shape[i].shape, out_shape[i].dtype) for i in late_out]
+        + [dma(max(1, len(late))), dma(max(1, len(late_out)))],
+        compiler_params=params(),
+        cost_estimate=cost,
+        name=name,
+    )(*args)
+
+
+def space_forward(
+    frame_clip, boxes, t_embed, mod_weight, mod_bias, tokens, wqkv, bqv, wout, bout, owners
+):
     rows, width = tokens.shape
     frames = boxes.shape[0]
     pos = rows // frames // owners
-    return pl.pallas_call(
+    args = (frame_clip, boxes, t_embed, mod_weight, mod_bias, tokens, wqkv, bqv, wout, bout)
+    return streamed(
         space_forward_kernel,
-        in_specs=[smem(), smem()] + [vmem()] * 6,
-        out_specs=[vmem()] * 4,
-        out_shape=[
+        args,
+        (3, 5, 6, 8),
+        [
             jax.ShapeDtypeStruct((owners, frames, pos, width), BF),
             jax.ShapeDtypeStruct((rows, 3 * width), BF),
             jax.ShapeDtypeStruct((rows, width), BF),
             jax.ShapeDtypeStruct((rows, width), F32),
-        ],
-        scratch_shapes=[pltpu.VMEM((rows, width), BF)],
-        compiler_params=params(),
-        cost_estimate=BRIEF,
-        name="space_forward",
-    )(frame_clip, boxes, tokens, table, wqkv, bqv, wout, bout)
+            jax.ShapeDtypeStruct((3, t_embed.shape[0], width), F32),
+        ],
+        (0, 1, 2, 3),
+        [pltpu.VMEM((rows, width), BF)],
+        BRIEF,
+        "space_forward",
+        small=2,
+        cut=((3, 3 * width),),
+    )
 
 
 def to_positions(source, stage, target):
@@ -331,199 +428,169 @@
     return v * half, slope
 
 
-def time_forward_kernel(
+def owner_forward_kernel(
     mid_ref, cot_ref, table_ref, clip_col_ref, ids_row_ref, wqkv_ref, bqv_ref, wout_ref, bout_ref,
-    xa_ref, packed_ref, attended_ref, branch_ref, midb_ref, normed_ref, gbranch_ref, cot_out, gdownb_ref,
-    stage, mid, cot, normed, bias,
+    up_ref, upb_ref, down_ref, downb_ref,
+    xa_ref, packed_ref, attended_ref, branch_ref, gmid_ref, result_ref, grad_ref, gclip_ref, gupb_ref,
+    gdownb_ref,
+    stage, mid, cot, normed, normed_t, gbranch, bias, act, ghid, branch_acc, gnorm_acc,
+    cot_in, wqkv, wout, xa, packed, attended, branch_out, sem_in, sem_out,
 ):
+    step = pl.program_id(0)
     frames, pos, width = mid_ref.shape
     blocks = frames * pos // BLOCK
     per_block = BLOCK // frames
     clips = table_ref.shape[1]
     clip_col = clip_col_ref[...]
+    leaving = [
+        (xa, xa_ref), (packed, packed_ref), (attended, attended_ref), (branch_out, branch_ref)
+    ]
 
     def modvec(member):
         return spread(frame_rows(table_ref, member, clip_col), per_block)
 
-    to_positions(mid_ref, stage, mid)
-    to_positions(cot_ref, stage, cot)
-    xa_ref[...] = mid[...].astype(BF)
-    cot_out[...] = cot[...].astype(BF)
-    bias[...] = time_mask(ids_row_ref, clip_col, per_block, clips)
-    shift_b, scale_b = modvec(0), modvec(1)
+    @pl.when(step == 0)
+    def _():
+        loads = copies([(wqkv_ref, wqkv), (cot_ref, cot_in), (wout_ref, wout)], sem_in)
+        to_positions(mid_ref, stage, mid)
+        xa[...] = mid[...].astype(BF)
+        copies(leaving[:1], sem_out)
+        bias[...] = time_mask(ids_row_ref, clip_col, per_block, clips)
+        shift_b, scale_b = modvec(0), modvec(1)
+        for b in range(blocks):
+            part = pl.ds(b * BLOCK, BLOCK)
+            n, _ = normalize(mid[part, :])
+            normed[part, :] = (n * (1.0 + scale_b) + shift_b).astype(BF)
+        loads[0].wait()
+        project_qkv(normed, wqkv, bqv_ref, packed, width)
+        copies(leaving[1:2], sem_out.at[pl.ds(1, 1)])
+        attend(packed, attended, lambda b: bias[...], blocks, width)
+        copies(leaving[2:3], sem_out.at[pl.ds(2, 1)])
+        loads[1].wait()
+        to_positions(cot_in, stage, cot)
+        gate_b, shift_c, scale_c, gate_c = modvec(2), modvec(3), modvec(4), modvec(5)
+        loads[2].wait()
+        for b in range(blocks):
+            part = pl.ds(b * BLOCK, BLOCK)
+            branch = dot_nn(attended[part, :], wout[...]) + as_row(bout_ref[...])
+            branch_out[part, :] = branch
+            mid_b = mid[part, :] + gate_b * branch
+            mid[part, :] = mid_b
+            n, _ = normalize(mid_b)
+            normed[part, :] = (n * (1.0 + scale_c) + shift_c).astype(BF)
+            gbranch[part, :] = (gate_c * cot[part, :]).astype(BF)
+        copies(leaving[3:], sem_out.at[pl.ds(3, 1)])
+        normed_t[...] = normed[...].T
+        gdownb_ref[...] = jnp.sum(gbranch[...].astype(F32), axis=0, keepdims=True)
+        branch_acc[...] = jnp.zeros_like(branch_acc)
+        gnorm_acc[...] = jnp.zeros_like(gnorm_acc)
+
+    up_bias = chunk_row(upb_ref, step, act.shape[1])
     for b in range(blocks):
         part = pl.ds(b * BLOCK, BLOCK)
-        n, _ = normalize(mid[part, :])
-        normed[part, :] = (n * (1.0 + scale_b) + shift_b).astype(BF)
-    project_qkv(normed, wqkv_ref, bqv_ref, packed_ref, width)
-    attend(packed_ref, attended_ref, lambda b: bias[...], blocks, width)
-    gate_b, shift_c, scale_c, gate_c = modvec(2), modvec(3), modvec(4), modvec(5)
-    for b in range(blocks):
-        part = pl.ds(b * BLOCK, BLOCK)
-        branch = dot_nn(attended_ref[part, :], wout_ref[...]) + as_row(bout_ref[...])
-        branch_ref[part, :] = branch
-        mid_b = mid[part, :] + gate_b * branch
-        midb_ref[part, :] = mid_b
-        n, _ = normalize(mid_b)
-        normed_ref[part, :] = (n * (1.0 + scale_c) + shift_c).astype(BF)
-        gbranch_ref[part, :] = (gate_c * cot[part, :]).astype(BF)
-    gdownb_ref[...] = jnp.sum(gbranch_ref[...].astype(F32), axis=0, keepdims=True)
-
-
-def time_forward(mid, cot, table, clip_col, ids_row, wqkv, bqv, wout, bout):
+        hidden = dot_nn(normed[part, :], up_ref[...]) + up_bias
+        value, slope = gelu_and_slope(hidden)
+        value = value.astype(BF)
+        act[part, :] = value
+        gh = (dot_nt(gbranch[part, :], down_ref[...]) * slope).astype(BF)
+        ghid[part, :] = gh
+        branch_acc[part, :] += dot_nn(value, down_ref[...])
+        gnorm_acc[part, :] += dot_nt(gh, up_ref[...])
+    grad_ref[0] = dot_nn(normed_t[...], ghid[...]).astype(BF)
+    grad_ref[1] = dot_tn(act[...], gbranch[...]).astype(BF)
+    gupb_ref[0] = jnp.sum(ghid[...].astype(F32), axis=0, keepdims=True)
+
+    @pl.when(step == pl.num_programs(0) - 1)
+    def _():
+        scale_c, gate_c = modvec(4), modvec(5)
+        sums = [0.0, 0.0, 0.0]
+        for b in range(blocks):
+            part = pl.ds(b * BLOCK, BLOCK)
+            up = cot[part, :]
+            branch = branch_acc[part, :] + as_row(downb_ref[...])
+            sums[2] = sums[2] + gather_frames(branch * up, frames)
+            mid_b = mid[part, :]
+            n, r = normalize(mid_b)
+            g = gnorm_acc[part, :]
+            sums[0] = sums[0] + gather_frames(g, frames)
+            sums[1] = sums[1] + gather_frames(g * n, frames)
+            gmid_ref[part, :] = up + normalize_back(n, r, g * (1.0 + scale_c))
+            stage_positions(stage, mid_b + gate_c * branch, frames, pos, b * per_block)
+        to_frames(stage, result_ref)
+        for member in range(3):
+            per_clip_sums(gclip_ref, member, sums[member], clip_col)
+        for i, (source, target) in enumerate(leaving):
+            pltpu.make_async_copy(source, target, sem_out.at[i]).wait()
+
+
+def owner_forward(mid, cot, table, clip_col, ids_row, wqkv, bqv, wout, bout, up, upb, down, downb):
     frames, pos, width = mid.shape
     rows = frames * pos
+    clips = table.shape[1]
+    ff = up.shape[1]
+    chunk = width
+    steps = ff // chunk
+    whole = lambda *shape: pl.BlockSpec(shape, lambda i: (0,) * len(shape))
     like = lambda cols, dtype: jax.ShapeDtypeStruct((rows, cols), dtype)
+    wide = pltpu.VMEM((rows, width), F32)
+    half = pltpu.VMEM((rows, width), BF)
     return pl.pallas_call(
-        time_forward_kernel,
-        in_specs=[vmem()] * 9,
-        out_specs=[vmem()] * 9,
+        owner_forward_kernel,
+        grid=(steps,),
+        in_specs=[vmem(), hbm(), vmem(), vmem(), vmem(), hbm(), vmem(), hbm(), vmem()]
+        + [
+            pl.BlockSpec((width, chunk), lambda i: (0, i)),
+            vmem(),
+            pl.BlockSpec((chunk, width), lambda i: (i, 0)),
+            vmem(),
+        ],
+        out_specs=[hbm()] * 4
+        + [
+            whole(rows, width),
+            whole(frames, pos, width),
+            pl.BlockSpec((2, width, chunk), lambda i: (0, i, 0)),
+            whole(3, clips, width),
+            pl.BlockSpec((1, 1, chunk), lambda i: (i, 0, 0)),
+            whole(1, width),
+        ],
         out_shape=[
             like(width, BF),
             like(3 * width, BF),
             like(width, BF),
             like(width, F32),
             like(width, F32),
-            like(width, BF),
-            like(width, BF),
-            like(width, BF),
+            jax.ShapeDtypeStruct((frames, pos, width), BF),
+            jax.ShapeDtypeStruct((2, ff, width), BF),
+            jax.ShapeDtypeStruct((3, clips, width), F32),
+            jax.ShapeDtypeStruct((steps, 1, chunk), F32),
             jax.ShapeDtypeStruct((1, width), F32),
         ],
         scratch_shapes=[
             pltpu.VMEM((width // LANES, rows, LANES), F32),
-            pltpu.VMEM((rows, width), F32),
-            pltpu.VMEM((rows, width), F32),
-            pltpu.VMEM((rows, width), BF),
+            wide,
+            wide,
+            half,
+            pltpu.VMEM((width, rows), BF),
+            half,
             pltpu.VMEM((BLOCK, BLOCK), F32),
+            pltpu.VMEM((rows, chunk), BF),
+            pltpu.VMEM((rows, chunk), BF),
+            wide,
+            wide,
+            pltpu.VMEM((frames, pos, width), BF),
+            pltpu.VMEM((width, 3 * width), BF),
+            pltpu.VMEM((width, width), BF),
+            half,
+            pltpu.VMEM((rows, 3 * width), BF),
+            half,
+            wide,
+            dma(3),
+            dma(4),
         ],
         compiler_params=params(),
         cost_estimate=BRIEF,
-        name="time_forward",
-    )(mid, cot, table, clip_col, ids_row, wqkv, bqv, wout, bout)
-
-
-def ff_kernel(
-    last, normed_ref, gbranch_ref, branch_in, gnorm_in, up_ref, upb_ref, down_ref,
-    midb_ref, cot_ref, table_ref, clip_col_ref, downb_ref, *refs,
-):
-    if last:
-        _, grad_ref, gupb_ref, gmid_ref, result_ref, gclip_ref = refs[:6]
-        normed_t, act, ghid, branch_acc, gnorm_acc, stage = refs[6:]
-    else:
-        grad_ref, gupb_ref, branch_acc, gnorm_acc, normed_t, act, ghid = refs
-    step = pl.program_id(0)
-    width = normed_ref.shape[1]
-    blocks = normed_ref.shape[0] // BLOCK
-    first = pl.num_programs(0) if last else 0
-    up_bias = chunk_row(upb_ref, first + step, act.shape[1])
-
-    @pl.when(step == 0)
-    def _():
-        normed_t[...] = normed_ref[...].T
-        if last:
-            branch_acc[...] = branch_in[...]
-            gnorm_acc[...] = gnorm_in[...]
-        else:
-            branch_acc[...] = jnp.zeros_like(branch_acc)
-            gnorm_acc[...] = jnp.zeros_like(gnorm_acc)
-
-    for b in range(blocks):
-        part = pl.ds(b * BLOCK, BLOCK)
-        hidden = dot_nn(normed_ref[part, :], up_ref[...]) + up_bias
-        value, slope = gelu_and_slope(hidden)
-        value = value.astype(BF)
-        act[part, :] = value
-        gh = (dot_nt(gbranch_ref[part, :], down_ref[...]) * slope).astype(BF)
-        ghid[part, :] = gh
-        branch_acc[part, :] += dot_nn(value, down_ref[...])
-        gnorm_acc[part, :] += dot_nt(gh, up_ref[...])
-    grad_up = dot_nn(normed_t[...], ghid[...])
-    grad_down = dot_tn(act[...], gbranch_ref[...])
-    grad_ref[0] = grad_up.astype(BF)
-    grad_ref[1] = grad_down.astype(BF)
-    gupb_ref[0] = jnp.sum(ghid[...].astype(F32), axis=0, keepdims=True)
-
-    if last:
-
-        @pl.when(step == pl.num_programs(0) - 1)
-        def _():
-            clip_col = clip_col_ref[...]
-            frames, pos, _ = result_ref.shape
-            per_block = BLOCK // frames
-
-            def modvec(member):
-                return spread(frame_rows(table_ref, member, clip_col), per_block)
-
-            scale_c, gate_c = modvec(4), modvec(5)
-            sums = [0.0, 0.0, 0.0]
-            for b in range(blocks):
-                part = pl.ds(b * BLOCK, BLOCK)
-                up = cot_ref[part, :].astype(F32)
-                branch = branch_acc[part, :] + as_row(downb_ref[...])
-                sums[2] = sums[2] + gather_frames(branch * up, frames)
-                mid_b = midb_ref[part, :]
-                n, r = normalize(mid_b)
-                g = gnorm_acc[part, :]
-                sums[0] = sums[0] + gather_frames(g, frames)
-                sums[1] = sums[1] + gather_frames(g * n, frames)
-                gmid_ref[part, :] = up + normalize_back(n, r, g * (1.0 + scale_c))
-                stage_positions(stage, mid_b + gate_c * branch, frames, pos, b * per_block)
-            to_frames(stage, result_ref)
-            for member in range(3):
-                per_clip_sums(gclip_ref, member, sums[member], clip_col)
-
-
-def ff_half(half, normed, gbranch, branch_in, gnorm_in, up, upb, down, midb, cot, table, clip_col, downb, *before):
-    rows, width = normed.shape
-    clips = table.shape[1]
-    frames = clip_col.shape[0]
-    pos = rows // frames
-    ff = up.shape[1]
-    chunk = width
-    steps = ff // chunk // 2
-    last = half == 1
-    first = half * steps
-    whole = lambda *shape: pl.BlockSpec(shape, lambda i: (0,) * len(shape))
-    grad_specs = [pl.BlockSpec((1, 1, chunk), lambda i: (i, 0, 0))]
-    grad_shapes = [jax.ShapeDtypeStruct((steps, 1, chunk), F32)]
-    grad_specs = [pl.BlockSpec((2, width, chunk), lambda i: (0, first + i, 0))] + grad_specs
-    grad_shapes = [jax.ShapeDtypeStruct((2, 2 * steps * width, chunk), BF)] + grad_shapes
-    wide = pltpu.VMEM((rows, width), F32)
-    scratch = [pltpu.VMEM((width, rows), BF), pltpu.VMEM((rows, chunk), BF), pltpu.VMEM((rows, chunk), BF)]
-    if last:
-        out_specs = grad_specs + [whole(rows, width), whole(frames, pos, width), whole(3, clips, width)]
-        out_shape = grad_shapes + [
-            jax.ShapeDtypeStruct((rows, width), F32),
-            jax.ShapeDtypeStruct((frames, pos, width), BF),
-            jax.ShapeDtypeStruct((3, clips, width), F32),
-        ]
-        scratch = scratch + [wide, wide, pltpu.VMEM((width // LANES, rows, LANES), F32)]
-    else:
-        out_specs = grad_specs + [whole(rows, width), whole(rows, width)]
-        out_shape = grad_shapes + [jax.ShapeDtypeStruct((rows, width), F32)] * 2
-    unused = pl.BlockSpec(memory_space=pl.ANY)
-    late = vmem() if last else unused
-    if not last:
-        branch_in = gnorm_in = midb
-    return pl.pallas_call(
-        functools.partial(ff_kernel, last),
-        grid=(steps,),
-        in_specs=[vmem(), vmem(), late, late]
-        + [
-            pl.BlockSpec((width, chunk), lambda i: (0, first + i)),
-            vmem(),
-            pl.BlockSpec((chunk, width), lambda i: (first + i, 0)),
-        ]
-        + [late] * 5
-        + [hbm()] * len(before),
-        input_output_aliases={12 + i: i for i in range(len(before))},
-        out_specs=out_specs,
-        out_shape=out_shape,
-        scratch_shapes=scratch,
-        compiler_params=params(),
-        cost_estimate=BRIEF,
-        name="ff_half_%d" % half,
-    )(normed, gbranch, branch_in, gnorm_in, up, upb, down, midb, cot, table, clip_col, downb, *before)
+        name="owner_forward",
+    )(mid, cot, table, clip_col, ids_row, wqkv, bqv, wout, bout, up, upb, down, downb)
 
 
 def put(grads, core, quarter, value):
@@ -552,6 +619,7 @@
 
 
 def owner_backward_kernel(
+    ready, flush,
     xa_ref, packed_ref, attended_ref, branch_ref, gmid_ref, table_ref, clip_col_ref, ids_row_ref,
     wqkv_ref, wout_ref,
     send_ref, kept_ref, other_ref, gclip_ref, goutb_ref, gqv_ref,
@@ -570,6 +638,7 @@
     shift, scale, gate = modvec(0), modvec(1), modvec(2)
     bias[...] = time_mask(ids_row_ref, clip_col, per_block, clips)
     gate_sum = 0.0
+    ready(gmid_ref, branch_ref, wout_ref, xa_ref)
     for b in range(blocks):
         part = pl.ds(b * BLOCK, BLOCK)
         gm = gmid_ref[part, :]
@@ -582,9 +651,13 @@
     per_clip_sums(gclip_ref, 2, gate_sum, clip_col)
     goutb_ref[...] = jnp.sum(gbranch[...].astype(F32), axis=0, keepdims=True)
     grads = (kept_ref, other_ref)
+    ready(attended_ref)
     put(grads, this_core(), 3, dot_tn(attended_ref[...], gbranch[...]))
+    ready(packed_ref)
     attend_back(packed_ref, gatt, gpacked, lambda b: bias[...], blocks, width)
+    ready(wqkv_ref)
     qkv_back(normed, gpacked, wqkv_ref, grads, gqv_ref, gnorm, width)
+    flush(other_ref, kept_ref)
     sums = [0.0, 0.0]
     for b in range(blocks):
         part = pl.ds(b * BLOCK, BLOCK)
@@ -603,11 +676,12 @@
     frames = clip_col.shape[0]
     rows, width = xa.shape
     clips = table.shape[1]
-    return pl.pallas_call(
+    half = pltpu.VMEM((rows, width), BF)
+    return streamed(
         owner_backward_kernel,
-        in_specs=[vmem()] * 10,
-        out_specs=[vmem()] * 6,
-        out_shape=[
+        (xa, packed, attended, branch, gmid, table, clip_col, ids_row, wqkv, wout),
+        (4, 3, 9, 0, 2, 1, 8),
+        [
             jax.ShapeDtypeStruct((frames, rows // frames, width), BF),
             jax.ShapeDtypeStruct((2 * width, width), BF),
             jax.ShapeDtypeStruct((2 * width, width), BF),
@@ -615,33 +689,36 @@
             jax.ShapeDtypeStruct((1, width), F32),
             jax.ShapeDtypeStruct((2, width), F32),
         ],
-        scratch_shapes=[
+        (1, 2),
+        [
             pltpu.VMEM((width // LANES, rows, LANES), F32),
-            pltpu.VMEM((rows, width), BF),
-            pltpu.VMEM((rows, width), BF),
-            pltpu.VMEM((rows, width), BF),
+            half,
+            half,
+            half,
             pltpu.VMEM((rows, 3 * width), BF),
             pltpu.VMEM((BLOCK, BLOCK), F32),
             pltpu.VMEM((rows, width), F32),
         ],
-        compiler_params=params(),
-        cost_estimate=LONG,
-        name="owner_backward",
-    )(xa, packed, attended, branch, gmid, table, clip_col, ids_row, wqkv, wout)
+        BRIEF,
+        "owner_backward",
+    )
 
 
 def space_backward_kernel(
+    ready, flush,
     clip_ref, box_ref, x_ref, packed_ref, attended_ref, branch_ref, gmid_ref, table_ref,
-    wqkv_ref, wout_ref, t_ref, gclip_b_ref, gclip_c_ref, gqv_b_ref, goutb_b_ref, gupb_0_ref, gupb_1_ref,
-    gdownb_ref,
-    gx_ref, kept_ref, other_ref, small_ref,
-    normed, gbranch, gatt, gpacked, gnorm, goutb_ref, gqv_ref,
+    wqkv_ref, wout_ref, t_ref, gclip_b_ref, gclip_c_ref, gqv_b_ref, goutb_b_ref, gupb_ref, gdownb_ref,
+    gx_ref, kept_ref, other_ref, small_out,
+    normed, gbranch, gatt, gpacked, gnorm, goutb_ref, gqv_ref, small_ref, bias,
 ):
     frames = box_ref.shape[0]
     width = x_ref.shape[1]
     clips = table_ref.shape[1]
     clip = own_clips(clip_ref, frames)
     sums = [[None] * frames for _ in range(3)]
+    for f in range(frames):
+        bias[f] = jnp.broadcast_to(visible_bias(box_ref, f, BLOCK), (BLOCK, BLOCK)).T
+    ready(gmid_ref, branch_ref, wout_ref, x_ref)
     for f in range(frames):
         part = pl.ds(f * BLOCK, BLOCK)
         gm = gmid_ref[:, f].reshape(BLOCK, width).astype(F32)
@@ -655,10 +732,13 @@
         normed[part, :] = (n * (1.0 + scale) + shift).astype(BF)
     goutb_ref[...] = jnp.sum(gbranch[...].astype(F32), axis=0, keepdims=True)
     grads = (kept_ref, other_ref)
+    ready(attended_ref)
     put(grads, this_core(), 3, dot_tn(attended_ref[...], gbranch[...]))
-    biases = [visible_bias(box_ref, f, BLOCK) for f in range(frames)]
-    attend_back(packed_ref, gatt, gpacked, lambda b: biases[b], frames, width)
+    ready(packed_ref)
+    attend_back(packed_ref, gatt, gpacked, lambda b: bias[b], frames, width)
+    ready(wqkv_ref)
     qkv_back(normed, gpacked, wqkv_ref, grads, gqv_ref, gnorm, width)
+    flush(other_ref, kept_ref)
     for f in range(frames):
         part = pl.ds(f * BLOCK, BLOCK)
         n, r = normalize(x_ref[part, :].astype(F32))
@@ -668,8 +748,6 @@
         scale = frame_row(table_ref, 1, clip[f])
         gm = gmid_ref[:, f].reshape(BLOCK, width).astype(F32)
         gx_ref[part, :] = (gm + normalize_back(n, r, g * (1.0 + scale))).astype(BF)
-    all_clips = clips * lax.axis_size("dp")
-    mine = lax.axis_index("dp") * clips
     small_ref[...] = jnp.zeros_like(small_ref)
     for member in range(9):
         for c in range(clips):
@@ -680,46 +758,52 @@
             else:
                 source = gclip_b_ref if member < 6 else gclip_c_ref
                 total = source[member % 3, c : c + 1, :]
-            small_ref[pl.ds(member * all_clips + mine + c, 1), :] = total
-    at = 9 * all_clips
+            small_ref[member * clips + c : member * clips + c + 1, :] = total
+    at = 9 * clips
     t = jnp.where(lax.axis_index("seq") == 0, t_ref[...].astype(F32), 0.0)
-    for c in range(clips):
-        small_ref[pl.ds(at + mine + c, 1), :] = t[c : c + 1]
-    at += all_clips
-    for source in (gqv_ref, goutb_ref, gqv_b_ref, goutb_b_ref, gupb_0_ref, gupb_1_ref, gdownb_ref):
+    small_ref[at : at + clips, :] = t
+    at += clips
+    for source in (gqv_ref, goutb_ref, gqv_b_ref, goutb_b_ref, gupb_ref, gdownb_ref):
         for i in range(source.shape[0]):
             small_ref[at : at + 1, :] = source[i] if len(source.shape) == 3 else source[i : i + 1, :]
             at += 1
+    small_out[...] = small_ref[...].astype(BF)
+    flush(gx_ref)
 
 
 def space_backward(frame_clip, boxes, tokens, *rest):
     rows, width = tokens.shape
     t_embed = rest[7]
     members = rest[-1].shape[0] + sum(value.shape[0] for value in rest[10:-1])
-    extra = 3 + 10 * t_embed.shape[0] * lax.axis_size("dp") + members
-    return pl.pallas_call(
+    extra = 3 + 10 * t_embed.shape[0] + members
+    half = pltpu.VMEM((rows, width), BF)
+    extra = -(-extra // 16) * 16
+    return streamed(
         space_backward_kernel,
-        in_specs=[smem(), smem()] + [vmem()] * (1 + len(rest)),
-        out_specs=[vmem()] * 4,
-        out_shape=[
+        (frame_clip, boxes, tokens) + rest,
+        (6, 5, 9, 2, 4, 3, 8),
+        [
             jax.ShapeDtypeStruct((rows, width), BF),
             jax.ShapeDtypeStruct((2 * width, width), BF),
             jax.ShapeDtypeStruct((2 * width, width), BF),
-            jax.ShapeDtypeStruct((-(-extra // 8) * 8, width), F32),
-        ],
-        scratch_shapes=[
-            pltpu.VMEM((rows, width), BF),
-            pltpu.VMEM((rows, width), BF),
-            pltpu.VMEM((rows, width), BF),
+            jax.ShapeDtypeStruct((extra, width), BF),
+        ],
+        (0, 1, 2),
+        [
+            half,
+            half,
+            half,
             pltpu.VMEM((rows, 3 * width), BF),
             pltpu.VMEM((rows, width), F32),
             pltpu.VMEM((1, width), F32),
             pltpu.VMEM((2, width), F32),
-        ],
-        compiler_params=params(),
-        cost_estimate=LONG,
-        name="space_backward",
-    )(frame_clip, boxes, tokens, *rest)
+            pltpu.VMEM((extra, width), F32),
+            pltpu.VMEM((boxes.shape[0], BLOCK, BLOCK), F32),
+        ],
+        LONG,
+        "space_backward",
+        small=2,
+    )
 
 
 def routes(owners):
@@ -758,24 +842,6 @@
 
 def tie(*values):
     return lax.optimization_barrier(values)
-
-
-def hbm():
-    return pl.BlockSpec(memory_space=pltpu.HBM)
-
-
-def dma(count):
-    return pltpu.SemaphoreType.DMA((count,))
-
-
-def copies(pairs, semaphores):
-    started = [
-        pltpu.make_async_copy(source, target, semaphores.at[i])
-        for i, (source, target) in enumerate(pairs)
-    ]
-    for copy in started:
-        copy.start()
-    return started
 
 
 def side(stage, core):
@@ -1063,47 +1129,124 @@
     )(summed)
 
 
-def mod_weight_kernel(t_ref, g_ref, out_ref, smooth, parts, wide, sem_out):
-    members, clips, width = g_ref.shape
-    t = t_ref[...]
-    value = (t / (1.0 + jnp.exp(-t))).astype(BF).astype(F32)
+def pack_kernel(*refs):
+    parts, target, held, sem_in, sem_out = refs[:2], refs[2], refs[3], refs[4], refs[5]
+    first = parts[0].shape[0]
+    places = [held.at[pl.ds(0, first)], held.at[pl.ds(first, parts[1].shape[0])]]
+    for copy in copies(list(zip(parts, places)), sem_in):
+        copy.wait()
+    copies([(held, target)], sem_out)[0].wait()
+
+
+def pack(*parts):
+    shape = (parts[0].shape[0] + parts[1].shape[0], parts[0].shape[1])
+    return pl.pallas_call(
+        pack_kernel,
+        in_specs=[hbm()] * 2,
+        out_specs=hbm(),
+        out_shape=jax.ShapeDtypeStruct(shape, BF),
+        scratch_shapes=[pltpu.VMEM(shape, BF), dma(2), dma(1)],
+        compiler_params=alone(),
+        cost_estimate=BRIEF,
+        name="pack",
+    )(*parts)
+
+
+def last_kernel(rows, groups, clips, sizes, src_ref, up_ref, down_ref, mod_ref, *refs):
+    vectors, (parts, held, wide, smooth, split, mods, sem_in, sem_out, sem_mod) = refs[:-9], refs[-9:]
+    count, height, width = held.shape
+    owners = height // rows
+    extra = parts.shape[1]
+    copies([(src_ref.at[:, pl.ds(rows, extra)], parts)], sem_in.at[pl.ds(count * owners, 1)])[0].wait()
+    loads = copies(
+        [
+            (src_ref.at[i * owners + k, pl.ds(0, rows)], held.at[i, pl.ds(k * rows, rows)])
+            for i in range(count)
+            for k in range(owners)
+        ],
+        sem_in,
+    )
+    each = parts.shape[0] // groups
+    small = [
+        jnp.sum(parts[pl.ds(i * each, each)].astype(F32), axis=0) for i in range(groups)
+    ]
+    members = 9
     smooth[...] = jnp.zeros_like(smooth)
-    parts[...] = jnp.zeros_like(parts)
-    for i in range(3):
-        smooth[i * clips : (i + 1) * clips, :] = value
+    split[...] = jnp.zeros_like(split)
+    for j, sums in enumerate(small):
+        t = sums[members * clips : (members + 1) * clips]
+        value = (t / (1.0 + jnp.exp(-t))).astype(BF).astype(F32)
+        for i in range(3):
+            smooth[pl.ds((i * groups + j) * clips, clips), :] = value
     left = smooth[...].astype(BF)
-    slots = wide.shape[0]
+    slots = mods.shape[0]
     stores = []
     for member in range(members):
-        rest = g_ref[member]
-        for i in range(3):
-            piece = rest.astype(BF).astype(F32)
-            parts[i * clips : (i + 1) * clips, :] = piece
-            rest = rest - piece
+        row = 0.0
+        for j, sums in enumerate(small):
+            rest = sums[member * clips : (member + 1) * clips]
+            row = row + jnp.sum(rest, axis=0)
+            for i in range(3):
+                piece = rest.astype(BF).astype(F32)
+                split[pl.ds((i * groups + j) * clips, clips), :] = piece
+                rest = rest - piece
+        vectors[0][pl.ds(member * width, width)] = row
         if member >= slots:
             stores[member - slots].wait()
-        wide[member % slots] = dot_tn(left, parts[...].astype(BF))
-        target = out_ref.at[:, pl.ds(member * width, width)]
-        stores += copies([(wide.at[member % slots], target)], sem_out.at[pl.ds(member, 1)])
-    for store in stores[-slots:]:
+        mods[member % slots] = dot_tn(left, split[...].astype(BF))
+        target = mod_ref.at[:, pl.ds(member * width, width)]
+        stores += copies([(mods.at[member % slots], target)], sem_mod.at[pl.ds(member, 1)])
+    at = (members + 1) * clips
+    for vector, size in zip(vectors[1:], sizes):
+        for i in range(size):
+            vector[pl.ds(i * width, width)] = sum(sums[at] for sums in small)
+            at += 1
+    later = []
+    for i in range(count):
+        for load in loads[i * owners : (i + 1) * owners]:
+            load.wait()
+        wide[i] = held[i].astype(F32)
+        if i < count // 2:
+            target = up_ref.at[:, pl.ds(i * width, width)]
+        else:
+            target = down_ref.at[pl.ds((i - count // 2) * height, height)]
+        later += copies([(wide.at[i], target)], sem_out.at[pl.ds(i, 1)])
+    for store in stores[-slots:] + later:
         store.wait()
 
 
-def mod_weight_grad(t_all, grad_clip):
-    clips, width = t_all.shape
-    members = grad_clip.shape[0]
-    deep = -(-3 * clips // 16) * 16
+def last_grads(gathered, rows, groups, clips, ff, sizes):
+    devices, extra, width = gathered.shape
+    extra -= rows
+    blocks = 2 * ff // width
+    deep = -(-3 * groups * clips // 16) * 16
+    vector = lambda size: jax.ShapeDtypeStruct((size * width,), F32)
     return pl.pallas_call(
-        mod_weight_kernel,
-        in_specs=[vmem(), vmem()],
-        out_specs=hbm(),
-        out_shape=jax.ShapeDtypeStruct((width, members * width), F32),
-        scratch_shapes=[pltpu.VMEM((deep, width), F32)] * 2
-        + [pltpu.VMEM((5, width, width), F32), dma(members)],
+        functools.partial(last_kernel, rows, groups, clips, sizes),
+        in_specs=[hbm()],
+        out_specs=[hbm()] * 3 + [vmem()] * (1 + len(sizes)),
+        out_shape=[
+            jax.ShapeDtypeStruct((width, ff), F32),
+            jax.ShapeDtypeStruct((ff, width), F32),
+            jax.ShapeDtypeStruct((width, 9 * width), F32),
+            vector(9),
+        ]
+        + [vector(size) for size in sizes],
+        scratch_shapes=[
+            pltpu.VMEM((devices, extra, width), BF),
+            pltpu.VMEM((blocks, width, width), BF),
+            pltpu.VMEM((blocks, width, width), F32),
+            pltpu.VMEM((deep, width), F32),
+            pltpu.VMEM((deep, width), F32),
+            pltpu.VMEM((5, width, width), F32),
+            dma(devices + 1),
+            dma(blocks),
+            dma(9),
+        ],
         compiler_params=alone(),
         cost_estimate=BRIEF,
-        name="mod_weight_grad",
-    )(t_all, grad_clip)
+        name="last_grads",
+    )(gathered)
 
 
 def per_device(
@@ -1137,27 +1280,23 @@
 
     cot_send = cotangent.reshape(frames, owners, pos, width).transpose(1, 0, 2, 3)
     cot = exchange(cot_send)
-    table_a = modulation(t_embed, mod_weight, mod_bias, 0, 3)
-    mid_send, packed_a, attended_a, branch_a = space_forward(
-        frame_clip, boxes, tokens, table_a, space_qkv, space_qv_bias, space_out, space_out_bias, owners,
+    mid_send, packed_a, attended_a, branch_a, table_a = space_forward(
+        frame_clip, boxes, t_embed, mod_weight, mod_bias, tokens, space_qkv, space_qv_bias, space_out,
+        space_out_bias, owners,
     )
     mid_send, cot, t_late = tie(mid_send, cot, t_embed)
     mid = exchange(mid_send).reshape(group_frames, pos, width)
     cot = cot.reshape(group_frames, pos, width)
     table = modulation(t_late, mod_weight, mod_bias, 3, 6)
-    xa, packed_b, attended_b, branch_b, mid_b, normed_c, gbranch_c, cot, gdown_b = time_forward(
-        mid, cot, table, clip_col, ids_row, time_qkv, time_qv_bias, time_out, time_out_bias
+    (
+        xa, packed_b, attended_b, branch_b, gmid_b, result_send, grad_f, gclip_c, gup_b, gdown_b,
+    ) = owner_forward(
+        mid, cot, table, clip_col, ids_row, time_qkv, time_qv_bias, time_out, time_out_bias, up_weight,
+        up_bias, down_weight, down_bias,
     )
-    ff_args = (up_weight, up_bias, down_weight, mid_b, cot, table, clip_col, down_bias)
-    grad_f, gup_b0, branch_c, gnorm_c = ff_half(0, normed_c, gbranch_c, None, None, *ff_args)
     ff_shapes = ((width, ff), (ff, width))
     qkv_shapes = ((width, 3 * width), (width, width))
     qkv_spots = spots_of(6, lambda i: (i % 2, i // 2), lambda i: (i, 0))
-    all_clips = clips * groups
-
-    def mod_grads(small):
-        gclip = small[: 9 * all_clips].reshape(9, all_clips, width)
-        return mod_weight_grad(small[9 * all_clips : 10 * all_clips], gclip), jnp.sum(gclip, axis=1)
 
     def after_ff(gmid_b):
         return owner_backward(
@@ -1167,12 +1306,9 @@
     def after_time(gmid_a, gclip_b, gtout_b, gtqv_b):
         return space_backward(
             frame_clip, boxes, tokens, packed_a, attended_a, branch_a, gmid_a, table_a, space_qkv,
-            space_out, t_embed, gclip_b, gclip_c, gtqv_b, gtout_b, gup_b0, gup_b1, gdown_b,
+            space_out, t_embed, gclip_b, gclip_c, gtqv_b, gtout_b, gup_b, gdown_b,
         )
 
-    grad_f, gup_b1, gmid_b, result_send, gclip_c = ff_half(
-        1, normed_c, gbranch_c, branch_c, gnorm_c, *ff_args, grad_f
-    )
     result_send = result_send.reshape(owners, frames, pos, width)
     grad_f = grad_f.reshape(-1, width)
     part_f = Held(lax.psum_scatter(grad_f, BOTH, scatter_dimension=0, tiled=True))
@@ -1180,37 +1316,27 @@
         sums = {}
         order = Order()
         wide = {}
-        small = Held(None)
-        small_links = [route["core"], route["x"], route["y"]] + route["swap"]
         for name, *step in SCHEDULE:
             if name == "time":
                 gmid_b = order.after(gmid_b)
                 gmid_send, kept_t, other_t, gclip_b, gtout_b, gtqv_b = after_ff(gmid_b)
-                result = exchange(result_send)
-                gmid_send, result = tie(gmid_send, result)
                 gmid_a = exchange(gmid_send.reshape(owners, frames, pos, width))
                 sums["t"] = Sum(kept_t, other_t, route)
                 order.before = None
             elif name == "space":
                 gmid_a = order.after(gmid_a)
-                grad_tokens, kept_s, other_s, small.value = after_time(
+                gmid_a, result_send = tie(gmid_a, result_send)
+                result = exchange(result_send)
+                grad_tokens, kept_s, other_s, small = after_time(
                     gmid_a, gclip_b, gtout_b, gtqv_b
                 )
                 sums["s"] = Sum(kept_s, other_s, route)
+                kept_s, result = tie(sums["s"].kept, result)
+                sums["s"].kept = kept_s
                 order.before = None
-                order.cost = LONG
             elif name == "ff":
-                part_f.value = order.after(part_f.value)
+                part_f.value = pack(order.after(part_f.value), small)
                 order.before = (part_f, "value")
-            elif name == "small":
-                small.value = order.after(small.value)
-                small.value = finish_sum(order.cost, small.value, move(small.value, small_links.pop(0)))
-                order.before = (small, "value")
-            elif name == "mod":
-                small.value = order.after(small.value)
-                grad_mod, grad_mod_b = mod_grads(small.value)
-                mod = Held(grad_mod)
-                order.before = (mod, "value")
             elif step[0] == "widen":
                 total = sums[name]
                 if step[1]:
@@ -1225,17 +1351,22 @@
                 done.other = pair[1]
                 order.before = (done, "value")
             else:
+                order.cost = COSTS.get((name, *step), BRIEF)
                 order.run(sums[name], *step)
-                order.cost = BRIEF
-        small, grad_mod = small.value, mod.value
+        gathered = lax.all_gather(part_f.value, BOTH, axis=0)
         wide_time, wide_space = ((wide[k].value, wide[k].other) for k in ("t", "s"))
     else:
         result = exchange(result_send)
         gmid_send, kept_t, other_t, gclip_b, gtout_b, gtqv_b = after_ff(gmid_b)
         gmid_a = exchange(gmid_send.reshape(owners, frames, pos, width))
         grad_tokens, kept_s, other_s, small = after_time(gmid_a, gclip_b, gtout_b, gtqv_b)
-        small = lax.psum(small, BOTH)
-        grad_mod, grad_mod_b = mod_grads(small)
+        small = lax.psum(small.astype(F32), "seq").astype(BF)
+        small = lax.all_gather(small, "dp", axis=0)
+        blocks = 2 * ff // width
+        sum_f = lax.all_gather(part_f.value, BOTH, axis=0, tiled=True).reshape(blocks, -1, width)
+        gathered = jnp.zeros((blocks,) + small.shape[1:], BF)
+        gathered = gathered.at[jnp.arange(groups) * (blocks // groups)].set(small)
+        gathered = jnp.concatenate([sum_f, gathered], axis=1)
         core = place()[3]
 
         def whole(kept, other):
@@ -1245,28 +1376,28 @@
         qkv_maps = (lambda i: (i % 2, i // 2), lambda i: (i, 0))
         wide_time = widen_plain(whole(kept_t, other_t), 6, qkv_shapes, qkv_maps)
         wide_space = widen_plain(whole(kept_s, other_s), 6, qkv_shapes, qkv_maps)
-    sum_f = lax.all_gather(part_f.value, BOTH, axis=0, tiled=True)
-    wide_ff = widen_plain(sum_f, 4, ff_shapes, (lambda i: (0, i), lambda i: (i, 0)))
-    rest = small[10 * all_clips :]
-    cut = lambda start, count: rest[start : start + count].reshape(-1)
-    up_rows = ff // width
+    rows = 2 * ff // gathered.shape[0]
+    sizes = (2, 1, 2, 1, ff // width, 1)
+    grad_up, grad_down, grad_mod, grad_mod_b, *biases = last_grads(
+        gathered, rows, groups, clips, ff, sizes
+    )
     return (
         result.transpose(1, 0, 2, 3).reshape(tokens.shape),
         grad_tokens,
         grad_mod,
-        grad_mod_b.reshape(-1),
+        grad_mod_b,
         wide_space[0],
-        cut(0, 2),
+        biases[0],
         wide_space[1],
-        cut(2, 1),
+        biases[1],
         wide_time[0],
-        cut(3, 2),
+        biases[2],
         wide_time[1],
-        cut(5, 1),
-        wide_ff[0],
-        cut(6, up_rows),
-        wide_ff[1],
-        cut(6 + up_rows, 1),
+        biases[3],
+        grad_up,
+        biases[4],
+        grad_down,
+        biases[5],
     )
 
 

time: 420 us -> 394 us (0.938)
  Pallas kernels: 183 us -> 158 us
  waiting for transfers between devices: 123 us -> 138 us
  local copies, waits for them, and re-layouts: 23 us -> 13.6 us
  starting transfers between devices: 69.7 us -> 63.9 us
    all_gather x1, waiting for transfers between devices: 0.02 us -> 27.8 us  [per_device(): gathered = lax.all_gather(part_f.value, BOTH, axis=0)]
    ppermute x37 -> x32, waiting for transfers between devices: 98.1 us -> 73.5 us  [move(): return lax.ppermute(value, BOTH, pairs)]
    pallas_call x8 -> x6, Pallas kernels: 127 us -> 114 us  [the longest x3 57.8 us: streamed(): pl.pallas_call(kernel, in_specs=in_specs, out_specs=[hbm() if i in late_o...]
    reduce_scatter x1, waiting for transfers between devices: 0.01 us -> 8.61 us  [per_device(): lax.psum_scatter(grad_f, BOTH, scatter_dimension=0, tiled=True)]
    pallas_call x7 -> x2, Pallas kernels: 12.2 us -> 3.72 us  [finish_sum(): pl.pallas_call(finish_kernel, in_specs=[vmem()] * len(parts), out_specs=v...]
    ppermute x37 -> x32, starting transfers between devices: 44.9 us -> 39.4 us  [move(): return lax.ppermute(value, BOTH, pairs)]
    unnamed x80 -> x56, local copies, waits for them, and re-layouts: 14.3 us -> 9.2 us
    pallas_call x2 -> x1, Pallas kernels: 9.79 us -> 6.05 us  [modulation(): pl.pallas_call(functools.partial(modulation_kernel, first), grid=(count,)...]
  transfers between devices with their start and end apart: 43 -> 38, of which waited for: 19 -> 15; matrix products, arithmetic and copies ran while one was open for 2% -> 1% of each run, Pallas kernels for 31% -> 21%
where the time goes in v2:
time: 394 us; the launch traced here: 389 us
  Pallas kernels  158 us (40%)
  waiting for transfers between devices  138 us (35%)
  starting transfers between devices  63.9 us (16%)
  between operations  14.8 us (4%)
  local copies, waits for them, and re-layouts  13.6 us (3%)
    ppermute x32, waiting for transfers between devices, move(): return lax.ppermute(value, BOTH, pairs)  73.5 us
    pallas_call x3, Pallas kernels, streamed(): pl.pallas_call(kernel, in_specs=in_specs, out_specs=[hbm() if i in late_o...  57.8 us
    ppermute x32, starting transfers between devices, move(): return lax.ppermute(value, BOTH, pairs)  39.4 us
    pallas_call x1, Pallas kernels, owner_forward(): pl.pallas_call(owner_forward_kernel, grid=(steps,), in_specs=[vmem(), hbm...  35.7 us
    all_to_all x4, waiting for transfers between devices, exchange(): return lax.all_to_all(x, 'seq', split_axis=0, concat_axis=0, tiled=True)  28.2 us
    all_gather x1, waiting for transfers between devices, per_device(): gathered = lax.all_gather(part_f.value, BOTH, axis=0)  27.8 us
    all_to_all x4, starting transfers between devices, exchange(): return lax.all_to_all(x, 'seq', split_axis=0, concat_axis=0, tiled=True)  23.9 us
    pallas_call x1, Pallas kernels, last_grads(): pl.pallas_call(functools.partial(last_kernel, rows, groups, clips, sizes)...  18.7 us
  transfers between devices with their start and end apart: 38, of which 15 were waited for; matrix products, arithmetic and copies ran while one was open for 1% of the time, Pallas kernels for 21%

profile of v2, /device:TPU:0, one launch (start us, length us, event | category | flops | bytes accessed | tf_op | source)
XLA Modules:
  0.0 388.8 jit_solution(13093840103869861040)
XLA Ops:
  9.3 7.4 %all-to-all-start = ((bf16[16,2,16,768]{3,2,1,0:T(8,128)(2,1)}), bf16[16,2,16,768]{3,2,1,0:T(8,128)(2,1)S(1)}, u32[]{:S(2)}, u32[]{:S(2)}) async-start(bf16[16,2,16,768]{3,2,1,0:T(8,128)(2,1)} %bitcast.26), calls=%async_computation | async-start | bytes 1572864 | tf_op jit(solution)/shard_map/all_to_all | solution.py:1277
  16.7 14.7 %space_forward.1 = (bf16[16,2,16,768]{3,2,1,0:T(8,128)(2,1)}, bf16[512,2304]{1,0:T(8,128)(2,1)}, bf16[512,768]{1,0:T(8,128)(2,1)}, f32[512,768]{1,0:T(8,128)}, f32[3,2,768]{2,1,0:T(2,128)}) custom-call(s32[32]{0:T(128)} %refs_0_.3, s32[2,4]{1,0:T(2,128)} %refs_1_.3, bf16[2,768]{1,0:T(2,128)(2,1)} %refs_10_.1, bf16[768,6912]{1,0:T(8,128)(2,1)} %w_ref.1, ...), custom_call_target="tpu_custom_call" | custom-call | flops 1000 | bytes 1000 | tf_op jit(solution)/shard_map/space_forward/pallas_call | solution.py:328
  31.4 4.0 %all-to-all-done = bf16[16,2,16,768]{3,2,1,0:T(8,128)(2,1)S(1)} async-done(((bf16[16,2,16,768]{3,2,1,0:T(8,128)(2,1)}), bf16[16,2,16,768]{3,2,1,0:T(8,128)(2,1)S(1)}, u32[]{:S(2)}, u32[]{:S(2)}) %all-to-all-start) | async-done | bytes 786464 | tf_op jit(solution)/shard_map/all_to_all | solution.py:1277
  35.4 5.5 %all-to-all-start.1 = ((bf16[16,2,16,768]{3,2,1,0:T(8,128)(2,1)}), bf16[16,2,16,768]{3,2,1,0:T(8,128)(2,1)S(1)}, u32[]{:S(2)}, u32[]{:S(2)}) async-start(bf16[16,2,16,768]{3,2,1,0:T(8,128)(2,1)} %get-tuple-element.136), calls=%async_computation.1 | async-start | bytes 1572864 | tf_op jit(solution)/shard_map/all_to_all | solution.py:1277
  42.6 6.0 %modulation.1.table_ref.refs_5_ = f32[6,2,768]{2,1,0:T(2,128)} custom-call(bf16[2,768]{1,0:T(2,128)(2,1)} %refs_10_.1, bf16[768,6912]{1,0:T(8,128)(2,1)} %w_ref.1, bf16[6912]{0:T(1024)(128)(2,1)} %b_ref.1), custom_call_target="tpu_custom_call" | custom-call | flops 1000 | bytes 1000 | tf_op jit(solution)/shard_map/modulation/pallas_call | solution.py:168
  48.7 10.9 %all-to-all-done.1 = bf16[16,2,16,768]{3,2,1,0:T(8,128)(2,1)S(1)} async-done(((bf16[16,2,16,768]{3,2,1,0:T(8,128)(2,1)}), bf16[16,2,16,768]{3,2,1,0:T(8,128)(2,1)S(1)}, u32[]{:S(2)}, u32[]{:S(2)}) %all-to-all-start.1) | async-done | bytes 786464 | tf_op jit(solution)/shard_map/all_to_all | solution.py:1277
  60.5 35.7 %owner_forward.1 = (bf16[512,768]{1,0:T(8,128)(2,1)}, bf16[512,2304]{1,0:T(8,128)(2,1)}, bf16[512,768]{1,0:T(8,128)(2,1)}, f32[512,768]{1,0:T(8,128)}, f32[512,7...) custom-call(bf16[32,16,768]{2,1,0:T(8,128)(2,1)} %bitcast.30, ...), custom_call_target="tpu_custom_call" | custom-call | flops 1000 | bytes 1000 | tf_op jit(solution)/shard_map/owner_forward/pallas_call | solution.py:537
  96.1 21.7 %owner_backward.1 = (bf16[32,16,768]{2,1,0:T(8,128)(2,1)}, bf16[1536,768]{1,0:T(8,128)(2,1)}, bf16[1536,768]{1,0:T(8,128)(2,1)}, f32[3,2,768]{2,1,0:T(2,128)}, f32[1,768]{1,0:T(1,128)}, /*index=5*/f32[2,768]{1,0:T(2,128)}) custom-call(bf16[512,768]{1,0:T(8,128)(2,1)} %get-tuple-element.139.refs_0_, bf16[512,2304]{1,0:T(8,128)(2,1)} %get-tuple-element.140.refs_1_, ...), custom_call_target="tpu_custom_call" | custom-call | flops 1000 | bytes 1000 | tf_op jit(solution)/shard_map/owner_backward/pallas_call | solution.py:328
  118.1 5.5 %all-to-all-start.2 = ((bf16[16,2,16,768]{3,2,1,0:T(8,128)(2,1)}), bf16[16,2,16,768]{3,2,1,0:T(8,128)(2,1)S(1)}, u32[]{:S(2)}, u32[]{:S(2)}) async-start(bf16[16,2,16,768]{3,2,1,0:T(8,128)(2,1)} %bitcast.40), calls=%async_computation.2 | async-start | bytes 1572864 | tf_op jit(solution)/shard_map/all_to_all | solution.py:1277
  125.1 4.0 %cross_sum.4 = (bf16[768,768]{1,0:T(8,128)(2,1)}, bf16[768,768]{1,0:T(8,128)(2,1)}) custom-call(bf16[2,768,768]{2,1,0:T(8,128)(2,1)} %bitcast.33, bf16[2,768,768]{2,1,0:T(8,128)(2,1)} %bitcast.35), custom_call_target="tpu_custom_call" | custom-call | flops 1000 | bytes 1000 | tf_op jit(solution)/shard_map/cross_sum/pallas_call | solution.py:875
  129.1 13.3 %all-to-all-done.2.refs_6_ = bf16[16,2,16,768]{3,2,1,0:T(8,128)(2,1)S(1)} async-done(((bf16[16,2,16,768]{3,2,1,0:T(8,128)(2,1)}), bf16[16,2,16,768]{3,2,1,0:T(8,128)(2,1)S(1)}, u32[]{:S(2)}, u32[]{:S(2)}) %all-to-all-start.2) | async-done | bytes 786464 | tf_op jit(solution)/shard_map/all_to_all | solution.py:1277
  142.4 5.5 %all-to-all-start.3 = ((bf16[16,2,16,768]{3,2,1,0:T(8,128)(2,1)}), bf16[16,2,16,768]{3,2,1,0:T(8,128)(2,1)S(1)}, u32[]{:S(2)}, u32[]{:S(2)}) async-start(bf16[16,2,16,768]{3,2,1,0:T(8,128)(2,1)} %bitcast.8), calls=%async_computation.3 | async-start | bytes 1572864 | tf_op jit(solution)/shard_map/all_to_all | solution.py:1277
  149.6 21.5 %space_backward.1 = (bf16[512,768]{1,0:T(8,128)(2,1)}, bf16[1536,768]{1,0:T(8,128)(2,1)}, bf16[1536,768]{1,0:T(8,128)(2,1)}, bf16[32,768]{1,0:T(8,128)(2,1)}) custom-call(s32[32]{0:T(128)} %refs_0_.3, s32[2,4]{1,0:T(2,128)} %refs_1_.3, bf16[512,768]{1,0:T(8,128)(2,1)} %refs_2_.3, bf16[512,2304]{1,0:T(8,128)(2,1)} %get-tuple-element.132.refs_3_, ...), custom_call_target="tpu_custom_call" | custom-call | flops 30000001024 | bytes 1000 | tf_op jit(solution)/shard_map/space_backward/pallas_call | solution.py:328
  182.4 9.4 %collective-permute-done.2 = bf16[384,768]{1,0:T(8,128)(2,1)} collective-permute-done((bf16[384,768]{1,0:T(8,128)(2,1)}, bf16[384,768]{1,0:T(8,128)(2,1)}, u32[]{:S(2)}, u32[]{:S(2)}) %collective-permute-start.2) | collective-permute-done | bytes 589856 | tf_op jit(solution)/shard_map/ppermute | solution.py:840
  199.1 9.5 %collective-permute-done.4 = bf16[768,768]{1,0:T(8,128)(2,1)S(1)} collective-permute-done((bf16[768,768]{1,0:T(8,128)(2,1)}, bf16[768,768]{1,0:T(8,128)(2,1)S(1)}, u32[]{:S(2)}, u32[]{:S(2)}) %collective-permute-start.4) | collective-permute-done | bytes 1179680 | tf_op jit(solution)/shard_map/ppermute | solution.py:840
  226.8 13.9 %collective-permute-done.10.refs_2_ = bf16[96,768]{1,0:T(8,128)(2,1)S(1)} collective-permute-done((bf16[96,768]{1,0:T(8,128)(2,1)}, bf16[96,768]{1,0:T(8,128)(2,1)S(1)}, u32[]{:S(2)}, u32[]{:S(2)}) %collective-permute-start.10) | collective-permute-done | bytes 147488 | tf_op jit(solution)/shard_map/ppermute | solution.py:840
  240.7 4.6 %collective-permute-start.13 = (bf16[96,768]{1,0:T(8,128)(2,1)}, bf16[96,768]{1,0:T(8,128)(2,1)S(1)}, u32[]{:S(2)}, u32[]{:S(2)}) collective-permute-start(bf16[96,768]{1,0:T(8,128)(2,1)} %get-tuple-element.194), channel_id=1, source_target_pairs={{0,4},{1,5},{2,6},{3,7},{4,8},{5,9},{6,10},{7,11},{8,12},{9,13},{1... | collective-permute-start | bytes 442376 | tf_op jit(solution)/shard_map/ppermute | solution.py:840
  245.3 5.1 %collective-permute-start.14 = (bf16[96,768]{1,0:T(8,128)(2,1)}, bf16[96,768]{1,0:T(8,128)(2,1)S(1)}, u32[]{:S(2)}, u32[]{:S(2)}) collective-permute-start(bf16[96,768]{1,0:T(8,128)(2,1)} %get-tuple-element.195), channel_id=1, source_target_pairs={{0,8},{1,9},{2,10},{3,11},{4,12},{5,13},{6,14},{7,15},{8,0},{9,1},... | collective-permute-start | bytes 442376 | tf_op jit(solution)/shard_map/ppermute | solution.py:840
  259.9 8.6 %reduce-scatter.2.cloned.1.call-done.refs_0_ = bf16[192,768]{1,0:T(8,128)(2,1)} async-done(((bf16[6144,768]{1,0:T(8,128)(2,1)}), bf16[192,768]{1,0:T(8,128)(2,1)}) %reduce-scatter.2.cloned.1.call-update) | async-done | bytes 294928 | tf_op jit(solution)/shard_map/reduce_scatter | solution.py:1314
  277.3 12.2 %collective-permute-done.17.refs_2_ = bf16[96,768]{1,0:T(8,128)(2,1)S(1)} collective-permute-done((bf16[96,768]{1,0:T(8,128)(2,1)}, bf16[96,768]{1,0:T(8,128)(2,1)S(1)}, u32[]{:S(2)}, u32[]{:S(2)}) %collective-permute-start.17) | collective-permute-done | bytes 147488 | tf_op jit(solution)/shard_map/ppermute | solution.py:840
  297.4 11.6 %collective-permute-done.20.refs_1_ = bf16[384,768]{1,0:T(8,128)(2,1)} collective-permute-done((bf16[384,768]{1,0:T(8,128)(2,1)}, bf16[384,768]{1,0:T(8,128)(2,1)}, u32[]{:S(2)}, u32[]{:S(2)}) %collective-permute-start.20) | collective-permute-done | bytes 589856 | tf_op jit(solution)/shard_map/ppermute | solution.py:840
  319.2 6.3 %collective-permute-done.25.refs_3_ = bf16[384,768]{1,0:T(8,128)(2,1)} collective-permute-done((bf16[384,768]{1,0:T(8,128)(2,1)}, bf16[384,768]{1,0:T(8,128)(2,1)}, u32[]{:S(2)}, u32[]{:S(2)}) %collective-permute-start.25) | collective-permute-done | bytes 589856 | tf_op jit(solution)/shard_map/ppermute | solution.py:840
  335.2 27.8 %all-gather.3.cloned.1.call-done = bf16[7168,768]{1,0:T(8,128)(2,1)} async-done(((bf16[224,768]{1,0:T(8,128)(2,1)}), bf16[7168,768]{1,0:T(8,128)(2,1)}) %all-gather.3.cloned.1.call-update) | async-done | bytes 11010064 | tf_op jit(solution)/shard_map/all_gather | solution.py:1356
  363.0 18.7 %last_grads.1 = (f32[768,3072]{1,0:T(8,128)}, f32[3072,768]{1,0:T(8,128)}, f32[768,6912]{1,0:T(8,128)}, f32[6912]{0:T(1024)}, f32[1536]{0:T(1024)}, /*index=5*/f...) custom-call(bf16[32,224,768]{2,1,0:T(8,128)(2,1)} %bitcast.27), custom_call_target="tpu_custom_call" | custom-call | flops 1000 | bytes 1000 | tf_op jit(solution)/shard_map/last_grads/pallas_call | solution.py:1224
  (137 shorter events, 90.8 us)
Async XLA Ops:
  9.3 26.1 %all-to-all-start = ((bf16[16,2,16,768]{3,2,1,0:T(8,128)(2,1)}), bf16[16,2,16,768]{3,2,1,0:T(8,128)(2,1)S(1)}, u32[]{:S(2)}, u32[]{:S(2)}) async-start(bf16[16,2,16,768]{3,2,1,0:T(8,128)(2,1)} %bitcast.26), calls=%async_computation | async-start | bytes 1572864 | tf_op jit(solution)/shard_map/all_to_all | solution.py:1277
  35.4 24.2 %all-to-all-start.1 = ((bf16[16,2,16,768]{3,2,1,0:T(8,128)(2,1)}), bf16[16,2,16,768]{3,2,1,0:T(8,128)(2,1)S(1)}, u32[]{:S(2)}, u32[]{:S(2)}) async-start(bf16[16,2,16,768]{3,2,1,0:T(8,128)(2,1)} %get-tuple-element.136), calls=%async_computation.1 | async-start | bytes 1572864 | tf_op jit(solution)/shard_map/all_to_all | solution.py:1277
  40.9 227.7 %reduce-scatter.2.cloned.1.call-start = ((), (), s32[]{:S(2)}) async-start(), calls=%async_computation.5 | async-start | bytes 9732096 | tf_op jit(solution)/shard_map/reduce_scatter | solution.py:1314
  118.1 24.2 %all-to-all-start.2 = ((bf16[16,2,16,768]{3,2,1,0:T(8,128)(2,1)}), bf16[16,2,16,768]{3,2,1,0:T(8,128)(2,1)S(1)}, u32[]{:S(2)}, u32[]{:S(2)}) async-start(bf16[16,2,16,768]{3,2,1,0:T(8,128)(2,1)} %bitcast.40), calls=%async_computation.2 | async-start | bytes 1572864 | tf_op jit(solution)/shard_map/all_to_all | solution.py:1277
  142.4 33.5 %all-to-all-start.3 = ((bf16[16,2,16,768]{3,2,1,0:T(8,128)(2,1)}), bf16[16,2,16,768]{3,2,1,0:T(8,128)(2,1)S(1)}, u32[]{:S(2)}, u32[]{:S(2)}) async-start(bf16[16,2,16,768]{3,2,1,0:T(8,128)(2,1)} %bitcast.8), calls=%async_computation.3 | async-start | bytes 1572864 | tf_op jit(solution)/shard_map/all_to_all | solution.py:1277
  147.9 215.2 %all-gather.3.cloned.1.call-start = ((), (), s32[]{:S(2)}) async-start(), calls=%async_computation.6 | async-start | bytes 11354112 | tf_op jit(solution)/shard_map/all_gather | solution.py:1356
  148.1 23.4 %collective-permute-start.1 = (bf16[768,768]{1,0:T(8,128)(2,1)}, bf16[768,768]{1,0:T(8,128)(2,1)}, u32[]{:S(2)}, u32[]{:S(2)}) collective-permute-start(bf16[768,768]{1,0:T(8,128)(2,1)} %get-tuple-element.163), channel_id=1, source_target_pairs={{0,16},{1,3},{2,18},{3,1},{4,20},{5,7},{6,22},{7,5},{8,24},{9,11},... | collective-permute-start | bytes 3538952 | tf_op jit(solution)/shard_map/ppermute | solution.py:840
  174.2 17.7 %collective-permute-start.2 = (bf16[384,768]{1,0:T(8,128)(2,1)}, bf16[384,768]{1,0:T(8,128)(2,1)}, u32[]{:S(2)}, u32[]{:S(2)}) collective-permute-start(bf16[384,768]{1,0:T(8,128)(2,1)} %get-tuple-element.164), channel_id=1, source_target_pairs={{0,2},{1,17},{2,0},{3,19},{4,6},{5,21},{6,4},{7,23},{8,10},{9,25},... | collective-permute-start | bytes 1769480 | tf_op jit(solution)/shard_map/ppermute | solution.py:840
  180.9 27.7 %collective-permute-start.4 = (bf16[768,768]{1,0:T(8,128)(2,1)}, bf16[768,768]{1,0:T(8,128)(2,1)S(1)}, u32[]{:S(2)}, u32[]{:S(2)}) collective-permute-start(bf16[768,768]{1,0:T(8,128)(2,1)} %get-tuple-element.171), channel_id=1, source_target_pairs={{0,16},{1,3},{2,18},{3,1},{4,20},{5,7},{6,22},{7,5},{8,24},{9,11},... | collective-permute-start | bytes 3538952 | tf_op jit(solution)/shard_map/ppermute | solution.py:840
  194.0 18.2 %collective-permute-start.6 = (bf16[96,768]{1,0:T(8,128)(2,1)}, bf16[96,768]{1,0:T(8,128)(2,1)S(1)}, u32[]{:S(2)}, u32[]{:S(2)}) collective-permute-start(bf16[96,768]{1,0:T(8,128)(2,1)} %get-tuple-element.178), channel_id=1, source_target_pairs={{0,4},{1,5},{2,6},{3,7},{4,8},{5,9},{6,10},{7,11},{8,12},{9,13},{1... | collective-permute-start | bytes 442376 | tf_op jit(solution)/shard_map/ppermute | solution.py:840
  195.3 17.0 %collective-permute-start.7 = (bf16[96,768]{1,0:T(8,128)(2,1)}, bf16[96,768]{1,0:T(8,128)(2,1)S(1)}, u32[]{:S(2)}, u32[]{:S(2)}) collective-permute-start(bf16[96,768]{1,0:T(8,128)(2,1)} %get-tuple-element.179), channel_id=1, source_target_pairs={{0,8},{1,9},{2,10},{3,11},{4,12},{5,13},{6,14},{7,15},{8,0},{9,1},... | collective-permute-start | bytes 442376 | tf_op jit(solution)/shard_map/ppermute | solution.py:840
  219.5 21.2 %collective-permute-start.10 = (bf16[96,768]{1,0:T(8,128)(2,1)}, bf16[96,768]{1,0:T(8,128)(2,1)S(1)}, u32[]{:S(2)}, u32[]{:S(2)}) collective-permute-start(bf16[96,768]{1,0:T(8,128)(2,1)} %finish_sum.2.refs_0_), channel_id=1, source_target_pairs={{0,8},{1,9},{2,10},{3,11},{4,12},{5,13},{6,14},{7,15},{8,0},{9,1},... | collective-permute-start | bytes 442376 | tf_op jit(solution)/shard_map/ppermute | solution.py:840
  219.5 21.2 %collective-permute-start.9 = (bf16[96,768]{1,0:T(8,128)(2,1)}, bf16[96,768]{1,0:T(8,128)(2,1)S(1)}, u32[]{:S(2)}, u32[]{:S(2)}) collective-permute-start(bf16[96,768]{1,0:T(8,128)(2,1)} %finish_sum.2.refs_0_), channel_id=1, source_target_pairs={{0,4},{1,5},{2,6},{3,7},{4,8},{5,9},{6,10},{7,11},{8,12},{9,13},{1... | collective-permute-start | bytes 442376 | tf_op jit(solution)/shard_map/ppermute | solution.py:840
  272.7 16.8 %collective-permute-start.17 = (bf16[96,768]{1,0:T(8,128)(2,1)}, bf16[96,768]{1,0:T(8,128)(2,1)S(1)}, u32[]{:S(2)}, u32[]{:S(2)}) collective-permute-start(bf16[96,768]{1,0:T(8,128)(2,1)} %finish_sum.3.refs_0_), channel_id=1, source_target_pairs={{0,8},{1,9},{2,10},{3,11},{4,12},{5,13},{6,14},{7,15},{8,0},{9,1},... | collective-permute-start | bytes 442376 | tf_op jit(solution)/shard_map/ppermute | solution.py:840
  273.1 16.4 %collective-permute-start.16 = (bf16[96,768]{1,0:T(8,128)(2,1)}, bf16[96,768]{1,0:T(8,128)(2,1)S(1)}, u32[]{:S(2)}, u32[]{:S(2)}) collective-permute-start(bf16[96,768]{1,0:T(8,128)(2,1)} %finish_sum.3.refs_0_), channel_id=1, source_target_pairs={{0,4},{1,5},{2,6},{3,7},{4,8},{5,9},{6,10},{7,11},{8,12},{9,13},{1... | collective-permute-start | bytes 442376 | tf_op jit(solution)/shard_map/ppermute | solution.py:840
  274.0 19.6 %collective-permute-start.21 = (bf16[384,768]{1,0:T(8,128)(2,1)S(1)}, bf16[384,768]{1,0:T(8,128)(2,1)}, u32[]{:S(2)}, u32[]{:S(2)}) collective-permute-start(bf16[384,768]{1,0:T(8,128)(2,1)S(1)} %bitcast.43), channel_id=1, source_target_pairs={{0,16},{1,3},{2,18},{3,1},{4,20},{5,7},{6,22},{7,5},{8,24},{9,11},... | collective-permute-start | bytes 1769480 | tf_op jit(solution)/shard_map/ppermute | solution.py:840
  275.3 18.2 %collective-permute-start.22 = (bf16[384,768]{1,0:T(8,128)(2,1)S(1)}, bf16[384,768]{1,0:T(8,128)(2,1)}, u32[]{:S(2)}, u32[]{:S(2)}) collective-permute-start(bf16[384,768]{1,0:T(8,128)(2,1)S(1)} %collective-permute-done.12.refs_1_), channel_id=1, source_target_pairs={{0,16},{1,3},{2,18},{3,1},{4,20},{5,7},{6,22},{7,5},{8,24},{9,11},... | collective-permute-start | bytes 1769480 | tf_op jit(solution)/shard_map/ppermute | solution.py:840
  292.9 16.2 %collective-permute-start.20 = (bf16[384,768]{1,0:T(8,128)(2,1)}, bf16[384,768]{1,0:T(8,128)(2,1)}, u32[]{:S(2)}, u32[]{:S(2)}) collective-permute-start(bf16[384,768]{1,0:T(8,128)(2,1)} %bitcast.45), channel_id=1, source_target_pairs={{0,2},{1,17},{2,0},{3,19},{4,6},{5,21},{6,4},{7,23},{8,10},{9,25},... | collective-permute-start | bytes 1769480 | tf_op jit(solution)/shard_map/ppermute | solution.py:840
  293.0 18.0 %collective-permute-start.27 = (bf16[384,768]{1,0:T(8,128)(2,1)S(1)}, bf16[384,768]{1,0:T(8,128)(2,1)S(1)}, u32[]{:S(2)}, u32[]{:S(2)}) collective-permute-start(bf16[384,768]{1,0:T(8,128)(2,1)S(1)} %collective-permute-done.12.refs_1_), channel_id=1, source_target_pairs={{0,1},{1,0},{2,3},{3,2},{4,5},{5,4},{6,7},{7,6},{8,9},{9,8},{10,11... | collective-permute-start | bytes 1769480 | tf_op jit(solution)/shard_map/ppermute | solution.py:840
  293.5 17.6 %collective-permute-start.28 = (bf16[384,768]{1,0:T(8,128)(2,1)}, bf16[384,768]{1,0:T(8,128)(2,1)}, u32[]{:S(2)}, u32[]{:S(2)}) collective-permute-start(bf16[384,768]{1,0:T(8,128)(2,1)} %collective-permute-done.21.refs_2_), channel_id=1, source_target_pairs={{0,1},{1,0},{2,3},{3,2},{4,5},{5,4},{6,7},{7,6},{8,9},{9,8},{10,11... | collective-permute-start | bytes 1769480 | tf_op jit(solution)/shard_map/ppermute | solution.py:840
  293.6 18.0 %collective-permute-start.29 = (bf16[384,768]{1,0:T(8,128)(2,1)}, bf16[384,768]{1,0:T(8,128)(2,1)}, u32[]{:S(2)}, u32[]{:S(2)}) collective-permute-start(bf16[384,768]{1,0:T(8,128)(2,1)} %collective-permute-done.22.refs_3_), channel_id=1, source_target_pairs={{0,1},{1,0},{2,3},{3,2},{4,5},{5,4},{6,7},{7,6},{8,9},{9,8},{10,11... | collective-permute-start | bytes 1769480 | tf_op jit(solution)/shard_map/ppermute | solution.py:840
  309.1 16.5 %collective-permute-start.25 = (bf16[384,768]{1,0:T(8,128)(2,1)}, bf16[384,768]{1,0:T(8,128)(2,1)}, u32[]{:S(2)}, u32[]{:S(2)}) collective-permute-start(bf16[384,768]{1,0:T(8,128)(2,1)} %collective-permute-done.20.refs_1_), channel_id=1, source_target_pairs={{0,16},{1,3},{2,18},{3,1},{4,20},{5,7},{6,22},{7,5},{8,24},{9,11},... | collective-permute-start | bytes 1769480 | tf_op jit(solution)/shard_map/ppermute | solution.py:840
  311.1 19.3 %collective-permute-start.19 = (bf16[384,768]{1,0:T(8,128)(2,1)}, bf16[384,768]{1,0:T(8,128)(2,1)S(1)}, u32[]{:S(2)}, u32[]{:S(2)}) collective-permute-start(bf16[384,768]{1,0:T(8,128)(2,1)} %bitcast.47), channel_id=1, source_target_pairs={{0,1},{1,0},{2,3},{3,2},{4,5},{5,4},{6,7},{7,6},{8,9},{9,8},{10,11... | collective-permute-start | bytes 1769480 | tf_op jit(solution)/shard_map/ppermute | solution.py:840
  311.1 19.3 %collective-permute-start.23 = (bf16[384,768]{1,0:T(8,128)(2,1)}, bf16[384,768]{1,0:T(8,128)(2,1)S(1)}, u32[]{:S(2)}, u32[]{:S(2)}) collective-permute-start(bf16[384,768]{1,0:T(8,128)(2,1)} %collective-permute-done.20.refs_1_), channel_id=1, source_target_pairs={{0,1},{1,0},{2,3},{3,2},{4,5},{5,4},{6,7},{7,6},{8,9},{9,8},{10,11... | collective-permute-start | bytes 1769480 | tf_op jit(solution)/shard_map/ppermute | solution.py:840
  (42 other events, 311.9 us)
Sparse Core Ops, SparseCore 0:
  118.3 150.2 reduce-scatter.1
  271.9 91.1 all-gather.2

commit v3 on v2

--- a/solution.py
+++ b/solution.py
@@ -18,6 +18,7 @@
 VMEM_BYTES = 56 * 1024 * 1024
 BOTH = ("dp", "seq")
 BRIEF = pl.CostEstimate(flops=1000, bytes_accessed=1000, transcendentals=0)
+SHORT = pl.CostEstimate(flops=4 * 10**9, bytes_accessed=1000, transcendentals=0)
 MIDDLE = pl.CostEstimate(flops=10**10, bytes_accessed=1000, transcendentals=0)
 LONG = pl.CostEstimate(flops=3 * 10**10, bytes_accessed=1000, transcendentals=0)
 
@@ -39,15 +40,19 @@
     ("t", "along"),
     ("s", "cross", 1),
     ("t", "finish"),
+    ("small", 0),
     ("s", "along"),
     ("t", "gather"),
+    ("small", 1),
     ("s", "finish"),
     ("ff",),
+    ("small", 2),
     ("t", "relay"),
     ("s", "gather"),
     ("t", "reflect"),
     ("t", "widen", 0),
     ("s", "relay"),
+    ("mod",),
     ("t", "widen", 1),
     ("s", "reflect"),
     ("s", "widen", 0),
@@ -708,8 +713,8 @@
     ready, flush,
     clip_ref, box_ref, x_ref, packed_ref, attended_ref, branch_ref, gmid_ref, table_ref,
     wqkv_ref, wout_ref, t_ref, gclip_b_ref, gclip_c_ref, gqv_b_ref, goutb_b_ref, gupb_ref, gdownb_ref,
-    gx_ref, kept_ref, other_ref, small_out,
-    normed, gbranch, gatt, gpacked, gnorm, goutb_ref, gqv_ref, small_ref, bias,
+    gx_ref, kept_ref, other_ref, small_ref,
+    normed, gbranch, gatt, gpacked, gnorm, goutb_ref, gqv_ref, bias,
 ):
     frames = box_ref.shape[0]
     width = x_ref.shape[1]
@@ -748,6 +753,8 @@
         scale = frame_row(table_ref, 1, clip[f])
         gm = gmid_ref[:, f].reshape(BLOCK, width).astype(F32)
         gx_ref[part, :] = (gm + normalize_back(n, r, g * (1.0 + scale))).astype(BF)
+    all_clips = clips * lax.axis_size("dp")
+    mine = lax.axis_index("dp") * clips
     small_ref[...] = jnp.zeros_like(small_ref)
     for member in range(9):
         for c in range(clips):
@@ -758,16 +765,16 @@
             else:
                 source = gclip_b_ref if member < 6 else gclip_c_ref
                 total = source[member % 3, c : c + 1, :]
-            small_ref[member * clips + c : member * clips + c + 1, :] = total
-    at = 9 * clips
+            small_ref[pl.ds(member * all_clips + mine + c, 1), :] = total
+    at = 9 * all_clips
     t = jnp.where(lax.axis_index("seq") == 0, t_ref[...].astype(F32), 0.0)
-    small_ref[at : at + clips, :] = t
-    at += clips
+    for c in range(clips):
+        small_ref[pl.ds(at + mine + c, 1), :] = t[c : c + 1]
+    at += all_clips
     for source in (gqv_ref, goutb_ref, gqv_b_ref, goutb_b_ref, gupb_ref, gdownb_ref):
         for i in range(source.shape[0]):
             small_ref[at : at + 1, :] = source[i] if len(source.shape) == 3 else source[i : i + 1, :]
             at += 1
-    small_out[...] = small_ref[...].astype(BF)
     flush(gx_ref)
 
 
@@ -775,9 +782,9 @@
     rows, width = tokens.shape
     t_embed = rest[7]
     members = rest[-1].shape[0] + sum(value.shape[0] for value in rest[10:-1])
-    extra = 3 + 10 * t_embed.shape[0] + members
+    extra = 3 + 10 * t_embed.shape[0] * lax.axis_size("dp") + members
     half = pltpu.VMEM((rows, width), BF)
-    extra = -(-extra // 16) * 16
+    extra = -(-extra // 8) * 8
     return streamed(
         space_backward_kernel,
         (frame_clip, boxes, tokens) + rest,
@@ -786,7 +793,7 @@
             jax.ShapeDtypeStruct((rows, width), BF),
             jax.ShapeDtypeStruct((2 * width, width), BF),
             jax.ShapeDtypeStruct((2 * width, width), BF),
-            jax.ShapeDtypeStruct((extra, width), BF),
+            jax.ShapeDtypeStruct((extra, width), F32),
         ],
         (0, 1, 2),
         [
@@ -797,7 +804,6 @@
             pltpu.VMEM((rows, width), F32),
             pltpu.VMEM((1, width), F32),
             pltpu.VMEM((2, width), F32),
-            pltpu.VMEM((extra, width), F32),
             pltpu.VMEM((boxes.shape[0], BLOCK, BLOCK), F32),
         ],
         LONG,
@@ -824,10 +830,8 @@
         "depth": [
             pairs(lambda x, z, y, c, s=s: (x, (z + s) % depth, y, c)) for s in range(1, depth)
         ],
-        "swap": [
-            pairs(lambda x, z, y, c, s=s: (x, z ^ s, y, c))
-            for s in (1 << i for i in range(depth.bit_length() - 1))
-        ],
+        "both": pairs(lambda x, z, y, c: (1 - x, z, 1 - y, c)),
+        "swap": [pairs(lambda x, z, y, c, s=s: (x, z ^ s, y, c)) for s in range(1, depth)],
     }
 
 
@@ -1129,68 +1133,25 @@
     )(summed)
 
 
-def pack_kernel(*refs):
-    parts, target, held, sem_in, sem_out = refs[:2], refs[2], refs[3], refs[4], refs[5]
-    first = parts[0].shape[0]
-    places = [held.at[pl.ds(0, first)], held.at[pl.ds(first, parts[1].shape[0])]]
-    for copy in copies(list(zip(parts, places)), sem_in):
-        copy.wait()
-    copies([(held, target)], sem_out)[0].wait()
-
-
-def pack(*parts):
-    shape = (parts[0].shape[0] + parts[1].shape[0], parts[0].shape[1])
-    return pl.pallas_call(
-        pack_kernel,
-        in_specs=[hbm()] * 2,
-        out_specs=hbm(),
-        out_shape=jax.ShapeDtypeStruct(shape, BF),
-        scratch_shapes=[pltpu.VMEM(shape, BF), dma(2), dma(1)],
-        compiler_params=alone(),
-        cost_estimate=BRIEF,
-        name="pack",
-    )(*parts)
-
-
-def last_kernel(rows, groups, clips, sizes, src_ref, up_ref, down_ref, mod_ref, *refs):
-    vectors, (parts, held, wide, smooth, split, mods, sem_in, sem_out, sem_mod) = refs[:-9], refs[-9:]
-    count, height, width = held.shape
-    owners = height // rows
-    extra = parts.shape[1]
-    copies([(src_ref.at[:, pl.ds(rows, extra)], parts)], sem_in.at[pl.ds(count * owners, 1)])[0].wait()
-    loads = copies(
-        [
-            (src_ref.at[i * owners + k, pl.ds(0, rows)], held.at[i, pl.ds(k * rows, rows)])
-            for i in range(count)
-            for k in range(owners)
-        ],
-        sem_in,
-    )
-    each = parts.shape[0] // groups
-    small = [
-        jnp.sum(parts[pl.ds(i * each, each)].astype(F32), axis=0) for i in range(groups)
-    ]
-    members = 9
+def mod_kernel(clips, sizes, small_ref, mod_ref, *refs):
+    vectors, (smooth, split, mods, sem_mod) = refs[:-4], refs[-4:]
+    members, width = 9, small_ref.shape[1]
+    t = small_ref[pl.ds(members * clips, clips), :]
+    value = (t / (1.0 + jnp.exp(-t))).astype(BF).astype(F32)
     smooth[...] = jnp.zeros_like(smooth)
     split[...] = jnp.zeros_like(split)
-    for j, sums in enumerate(small):
-        t = sums[members * clips : (members + 1) * clips]
-        value = (t / (1.0 + jnp.exp(-t))).astype(BF).astype(F32)
-        for i in range(3):
-            smooth[pl.ds((i * groups + j) * clips, clips), :] = value
+    for i in range(3):
+        smooth[i * clips : (i + 1) * clips, :] = value
     left = smooth[...].astype(BF)
     slots = mods.shape[0]
     stores = []
     for member in range(members):
-        row = 0.0
-        for j, sums in enumerate(small):
-            rest = sums[member * clips : (member + 1) * clips]
-            row = row + jnp.sum(rest, axis=0)
-            for i in range(3):
-                piece = rest.astype(BF).astype(F32)
-                split[pl.ds((i * groups + j) * clips, clips), :] = piece
-                rest = rest - piece
-        vectors[0][pl.ds(member * width, width)] = row
+        rest = small_ref[pl.ds(member * clips, clips), :]
+        vectors[0][pl.ds(member * width, width)] = jnp.sum(rest, axis=0)
+        for i in range(3):
+            piece = rest.astype(BF).astype(F32)
+            split[i * clips : (i + 1) * clips, :] = piece
+            rest = rest - piece
         if member >= slots:
             stores[member - slots].wait()
         mods[member % slots] = dot_tn(left, split[...].astype(BF))
@@ -1199,54 +1160,51 @@
     at = (members + 1) * clips
     for vector, size in zip(vectors[1:], sizes):
         for i in range(size):
-            vector[pl.ds(i * width, width)] = sum(sums[at] for sums in small)
+            vector[pl.ds(i * width, width)] = small_ref[at]
             at += 1
-    later = []
-    for i in range(count):
-        for load in loads[i * owners : (i + 1) * owners]:
-            load.wait()
-        wide[i] = held[i].astype(F32)
-        if i < count // 2:
-            target = up_ref.at[:, pl.ds(i * width, width)]
-        else:
-            target = down_ref.at[pl.ds((i - count // 2) * height, height)]
-        later += copies([(wide.at[i], target)], sem_out.at[pl.ds(i, 1)])
-    for store in stores[-slots:] + later:
+    for store in stores[-slots:]:
         store.wait()
 
 
-def last_grads(gathered, rows, groups, clips, ff, sizes):
-    devices, extra, width = gathered.shape
-    extra -= rows
-    blocks = 2 * ff // width
-    deep = -(-3 * groups * clips // 16) * 16
+def mod_grads(small, clips, sizes):
+    width = small.shape[1]
+    deep = -(-3 * clips // 16) * 16
     vector = lambda size: jax.ShapeDtypeStruct((size * width,), F32)
     return pl.pallas_call(
-        functools.partial(last_kernel, rows, groups, clips, sizes),
-        in_specs=[hbm()],
-        out_specs=[hbm()] * 3 + [vmem()] * (1 + len(sizes)),
-        out_shape=[
-            jax.ShapeDtypeStruct((width, ff), F32),
-            jax.ShapeDtypeStruct((ff, width), F32),
-            jax.ShapeDtypeStruct((width, 9 * width), F32),
-            vector(9),
-        ]
+        functools.partial(mod_kernel, clips, sizes),
+        in_specs=[vmem()],
+        out_specs=[hbm()] + [vmem()] * (1 + len(sizes)),
+        out_shape=[jax.ShapeDtypeStruct((width, 9 * width), F32), vector(9)]
         + [vector(size) for size in sizes],
         scratch_shapes=[
-            pltpu.VMEM((devices, extra, width), BF),
-            pltpu.VMEM((blocks, width, width), BF),
-            pltpu.VMEM((blocks, width, width), F32),
             pltpu.VMEM((deep, width), F32),
             pltpu.VMEM((deep, width), F32),
-            pltpu.VMEM((5, width, width), F32),
-            dma(devices + 1),
-            dma(blocks),
+            pltpu.VMEM((9, width, width), F32),
             dma(9),
         ],
         compiler_params=alone(),
         cost_estimate=BRIEF,
-        name="last_grads",
-    )(gathered)
+        name="mod_grads",
+    )(small)
+
+
+def quad_kernel(*refs):
+    values = [ref[...] for ref in refs[:-1]]
+    while len(values) > 1:
+        values = [a + b for a, b in zip(values[::2], values[1::2])]
+    refs[-1][...] = values[0]
+
+
+def pair_sum(*parts):
+    return pl.pallas_call(
+        quad_kernel,
+        in_specs=[vmem()] * len(parts),
+        out_specs=vmem(),
+        out_shape=jax.ShapeDtypeStruct(parts[0].shape, parts[0].dtype),
+        compiler_params=alone(),
+        cost_estimate=BRIEF,
+        name="pair_sum",
+    )(*parts)
 
 
 def per_device(
@@ -1296,6 +1254,8 @@
     )
     ff_shapes = ((width, ff), (ff, width))
     qkv_shapes = ((width, 3 * width), (width, width))
+    all_clips = clips * groups
+    sizes = (2, 1, 2, 1, ff // width, 1)
     qkv_spots = spots_of(6, lambda i: (i % 2, i // 2), lambda i: (i, 0))
 
     def after_ff(gmid_b):
@@ -1335,8 +1295,26 @@
                 sums["s"].kept = kept_s
                 order.before = None
             elif name == "ff":
-                part_f.value = pack(order.after(part_f.value), small)
+                part_f.value = order.after(part_f.value)
                 order.before = (part_f, "value")
+            elif name == "small":
+                links = (
+                    [route["core"]]
+                    if step[0] == 0
+                    else [route["x"], route["y"], route["both"]]
+                    if step[0] == 1
+                    else route["swap"]
+                )
+                if step[0]:
+                    small_got = order.after(small_got)
+                    small = pair_sum(small, *small_got)
+                    order.before = (Held(small), "value")
+                small_got = tuple(move(small, pairs) for pairs in links)
+            elif name == "mod":
+                small = pair_sum(small, *order.after(small_got))
+                mod = Held(None)
+                mod.value, *vectors = mod_grads(small, all_clips, sizes)
+                order.before = (mod, "value")
             elif step[0] == "widen":
                 total = sums[name]
                 if step[1]:
@@ -1353,20 +1331,17 @@
             else:
                 order.cost = COSTS.get((name, *step), BRIEF)
                 order.run(sums[name], *step)
-        gathered = lax.all_gather(part_f.value, BOTH, axis=0)
+        sum_f = lax.all_gather(part_f.value, BOTH, axis=0, tiled=True)
+        grad_mod = mod.value
         wide_time, wide_space = ((wide[k].value, wide[k].other) for k in ("t", "s"))
     else:
         result = exchange(result_send)
         gmid_send, kept_t, other_t, gclip_b, gtout_b, gtqv_b = after_ff(gmid_b)
         gmid_a = exchange(gmid_send.reshape(owners, frames, pos, width))
         grad_tokens, kept_s, other_s, small = after_time(gmid_a, gclip_b, gtout_b, gtqv_b)
-        small = lax.psum(small.astype(F32), "seq").astype(BF)
-        small = lax.all_gather(small, "dp", axis=0)
-        blocks = 2 * ff // width
-        sum_f = lax.all_gather(part_f.value, BOTH, axis=0, tiled=True).reshape(blocks, -1, width)
-        gathered = jnp.zeros((blocks,) + small.shape[1:], BF)
-        gathered = gathered.at[jnp.arange(groups) * (blocks // groups)].set(small)
-        gathered = jnp.concatenate([sum_f, gathered], axis=1)
+        small = lax.psum(small, BOTH)
+        grad_mod, *vectors = mod_grads(small, all_clips, sizes)
+        sum_f = lax.all_gather(part_f.value, BOTH, axis=0, tiled=True)
         core = place()[3]
 
         def whole(kept, other):
@@ -1376,11 +1351,8 @@
         qkv_maps = (lambda i: (i % 2, i // 2), lambda i: (i, 0))
         wide_time = widen_plain(whole(kept_t, other_t), 6, qkv_shapes, qkv_maps)
         wide_space = widen_plain(whole(kept_s, other_s), 6, qkv_shapes, qkv_maps)
-    rows = 2 * ff // gathered.shape[0]
-    sizes = (2, 1, 2, 1, ff // width, 1)
-    grad_up, grad_down, grad_mod, grad_mod_b, *biases = last_grads(
-        gathered, rows, groups, clips, ff, sizes
-    )
+    grad_up, grad_down = widen_plain(sum_f, 4, ff_shapes, (lambda i: (0, i), lambda i: (i, 0)))
+    grad_mod_b, *biases = vectors
     return (
         result.transpose(1, 0, 2, 3).reshape(tokens.shape),
         grad_tokens,

time: 394 us -> 385 us (0.977)
  waiting for transfers between devices: 138 us -> 104 us
  starting transfers between devices: 63.9 us -> 82.5 us
  Pallas kernels: 158 us -> 163 us
    ppermute x32 -> x39, waiting for transfers between devices: 73.5 us -> 52.7 us  [move(): return lax.ppermute(value, BOTH, pairs)]
    ppermute x32 -> x39, starting transfers between devices: 39.4 us -> 58.1 us  [move(): return lax.ppermute(value, BOTH, pairs)]
    all_gather x1, waiting for transfers between devices: 27.8 us -> 19.1 us  [per_device(): sum_f = lax.all_gather(part_f.value, BOTH, axis=0, tiled=True)]
    reduce_scatter x1, waiting for transfers between devices: 8.61 us -> 3.99 us  [per_device(): lax.psum_scatter(grad_f, BOTH, scatter_dimension=0, tiled=True)]
    pallas_call x2 -> x5, Pallas kernels: 20.4 us -> 23.8 us  [the longest x1 9.37 us: mod_grads(): pl.pallas_call(functools.partial(mod_kernel, clips, sizes), in_specs=[vme...]
    unnamed x56 -> x74, local copies, waits for them, and re-layouts: 9.2 us -> 10.8 us
  transfers between devices with their start and end apart: 38 -> 45, of which waited for: 15 -> 18; matrix products, arithmetic and copies ran while one was open for 1% -> 1% of each run, Pallas kernels for 21% -> 26%
where the time goes in v3:
time: 385 us; the launch traced here: 380 us
  Pallas kernels  163 us (42%)
  waiting for transfers between devices  104 us (27%)
  starting transfers between devices  82.5 us (21%)
  local copies, waits for them, and re-layouts  15.2 us (4%)
  between operations  14.9 us (4%)
    pallas_call x3, Pallas kernels, streamed(): pl.pallas_call(kernel, in_specs=in_specs, out_specs=[hbm() if i in late_o...  59.4 us
    ppermute x39, starting transfers between devices, move(): return lax.ppermute(value, BOTH, pairs)  58.1 us
    ppermute x39, waiting for transfers between devices, move(): return lax.ppermute(value, BOTH, pairs)  52.7 us
    pallas_call x1, Pallas kernels, owner_forward(): pl.pallas_call(owner_forward_kernel, grid=(steps,), in_specs=[vmem(), hbm...  35.7 us
    all_to_all x4, waiting for transfers between devices, exchange(): return lax.all_to_all(x, 'seq', split_axis=0, concat_axis=0, tiled=True)  28.2 us
    all_to_all x4, starting transfers between devices, exchange(): return lax.all_to_all(x, 'seq', split_axis=0, concat_axis=0, tiled=True)  23.9 us
    all_gather x1, waiting for transfers between devices, per_device(): sum_f = lax.all_gather(part_f.value, BOTH, axis=0, tiled=True)  19.1 us
    pallas_call x4, Pallas kernels, widen(): pl.pallas_call(functools.partial(widen_kernel, other, spots), in_specs=[h...  13.6 us
  transfers between devices with their start and end apart: 45, of which 18 were waited for; matrix products, arithmetic and copies ran while one was open for 1% of the time, Pallas kernels for 26%

profile of v3, /device:TPU:0, one launch (start us, length us, event | category | flops | bytes accessed | tf_op | source)
XLA Modules:
  0.0 380.1 jit_solution(15386176470847176827)
XLA Ops:
  9.3 7.4 %all-to-all-start = ((bf16[16,2,16,768]{3,2,1,0:T(8,128)(2,1)}), bf16[16,2,16,768]{3,2,1,0:T(8,128)(2,1)S(1)}, u32[]{:S(2)}, u32[]{:S(2)}) async-start(bf16[16,2,16,768]{3,2,1,0:T(8,128)(2,1)} %bitcast.25), calls=%async_computation | async-start | bytes 1572864 | tf_op jit(solution)/shard_map/all_to_all | solution.py:1235
  16.7 14.7 %space_forward.1 = (bf16[16,2,16,768]{3,2,1,0:T(8,128)(2,1)}, bf16[512,2304]{1,0:T(8,128)(2,1)}, bf16[512,768]{1,0:T(8,128)(2,1)}, f32[512,768]{1,0:T(8,128)}, f32[3,2,768]{2,1,0:T(2,128)}) custom-call(s32[32]{0:T(128)} %refs_0_.3, s32[2,4]{1,0:T(2,128)} %refs_1_.3, bf16[2,768]{1,0:T(2,128)(2,1)} %refs_10_.1, bf16[768,6912]{1,0:T(8,128)(2,1)} %w_ref.1, ...), custom_call_target="tpu_custom_call" | custom-call | flops 1000 | bytes 1000 | tf_op jit(solution)/shard_map/space_forward/pallas_call | solution.py:333
  31.4 4.0 %all-to-all-done = bf16[16,2,16,768]{3,2,1,0:T(8,128)(2,1)S(1)} async-done(((bf16[16,2,16,768]{3,2,1,0:T(8,128)(2,1)}), bf16[16,2,16,768]{3,2,1,0:T(8,128)(2,1)S(1)}, u32[]{:S(2)}, u32[]{:S(2)}) %all-to-all-start) | async-done | bytes 786464 | tf_op jit(solution)/shard_map/all_to_all | solution.py:1235
  35.4 5.5 %all-to-all-start.1 = ((bf16[16,2,16,768]{3,2,1,0:T(8,128)(2,1)}), bf16[16,2,16,768]{3,2,1,0:T(8,128)(2,1)S(1)}, u32[]{:S(2)}, u32[]{:S(2)}) async-start(bf16[16,2,16,768]{3,2,1,0:T(8,128)(2,1)} %get-tuple-element.144), calls=%async_computation.1 | async-start | bytes 1572864 | tf_op jit(solution)/shard_map/all_to_all | solution.py:1235
  42.6 6.0 %modulation.1.table_ref.refs_5_ = f32[6,2,768]{2,1,0:T(2,128)} custom-call(bf16[2,768]{1,0:T(2,128)(2,1)} %refs_10_.1, bf16[768,6912]{1,0:T(8,128)(2,1)} %w_ref.1, bf16[6912]{0:T(1024)(128)(2,1)} %b_ref.1), custom_call_target="tpu_custom_call" | custom-call | flops 1000 | bytes 1000 | tf_op jit(solution)/shard_map/modulation/pallas_call | solution.py:173
  48.7 10.9 %all-to-all-done.1 = bf16[16,2,16,768]{3,2,1,0:T(8,128)(2,1)S(1)} async-done(((bf16[16,2,16,768]{3,2,1,0:T(8,128)(2,1)}), bf16[16,2,16,768]{3,2,1,0:T(8,128)(2,1)S(1)}, u32[]{:S(2)}, u32[]{:S(2)}) %all-to-all-start.1) | async-done | bytes 786464 | tf_op jit(solution)/shard_map/all_to_all | solution.py:1235
  60.5 35.7 %owner_forward.1 = (bf16[512,768]{1,0:T(8,128)(2,1)}, bf16[512,2304]{1,0:T(8,128)(2,1)}, bf16[512,768]{1,0:T(8,128)(2,1)}, f32[512,768]{1,0:T(8,128)}, f32[512,7...) custom-call(bf16[32,16,768]{2,1,0:T(8,128)(2,1)} %bitcast.28, ...), custom_call_target="tpu_custom_call" | custom-call | flops 1000 | bytes 1000 | tf_op jit(solution)/shard_map/owner_forward/pallas_call | solution.py:542
  96.1 21.7 %owner_backward.1 = (bf16[32,16,768]{2,1,0:T(8,128)(2,1)}, bf16[1536,768]{1,0:T(8,128)(2,1)}, bf16[1536,768]{1,0:T(8,128)(2,1)}, f32[3,2,768]{2,1,0:T(2,128)}, f32[1,768]{1,0:T(1,128)}, /*index=5*/f32[2,768]{1,0:T(2,128)}) custom-call(bf16[512,768]{1,0:T(8,128)(2,1)} %get-tuple-element.147.refs_0_, bf16[512,2304]{1,0:T(8,128)(2,1)} %get-tuple-element.148.refs_1_, ...), custom_call_target="tpu_custom_call" | custom-call | flops 1000 | bytes 1000 | tf_op jit(solution)/shard_map/owner_backward/pallas_call | solution.py:333
  118.1 5.5 %all-to-all-start.2 = ((bf16[16,2,16,768]{3,2,1,0:T(8,128)(2,1)}), bf16[16,2,16,768]{3,2,1,0:T(8,128)(2,1)S(1)}, u32[]{:S(2)}, u32[]{:S(2)}) async-start(bf16[16,2,16,768]{3,2,1,0:T(8,128)(2,1)} %bitcast.38), calls=%async_computation.2 | async-start | bytes 1572864 | tf_op jit(solution)/shard_map/all_to_all | solution.py:1235
  125.1 4.0 %cross_sum.4 = (bf16[768,768]{1,0:T(8,128)(2,1)}, bf16[768,768]{1,0:T(8,128)(2,1)}) custom-call(bf16[2,768,768]{2,1,0:T(8,128)(2,1)} %bitcast.31, bf16[2,768,768]{2,1,0:T(8,128)(2,1)} %bitcast.33), custom_call_target="tpu_custom_call" | custom-call | flops 1000 | bytes 1000 | tf_op jit(solution)/shard_map/cross_sum/pallas_call | solution.py:879
  129.1 13.3 %all-to-all-done.2.refs_6_ = bf16[16,2,16,768]{3,2,1,0:T(8,128)(2,1)S(1)} async-done(((bf16[16,2,16,768]{3,2,1,0:T(8,128)(2,1)}), bf16[16,2,16,768]{3,2,1,0:T(8,128)(2,1)S(1)}, u32[]{:S(2)}, u32[]{:S(2)}) %all-to-all-start.2) | async-done | bytes 786464 | tf_op jit(solution)/shard_map/all_to_all | solution.py:1235
  142.4 5.5 %all-to-all-start.3 = ((bf16[16,2,16,768]{3,2,1,0:T(8,128)(2,1)}), bf16[16,2,16,768]{3,2,1,0:T(8,128)(2,1)S(1)}, u32[]{:S(2)}, u32[]{:S(2)}) async-start(bf16[16,2,16,768]{3,2,1,0:T(8,128)(2,1)} %bitcast.8), calls=%async_computation.3 | async-start | bytes 1572864 | tf_op jit(solution)/shard_map/all_to_all | solution.py:1235
  149.6 23.1 %space_backward.1 = (bf16[512,768]{1,0:T(8,128)(2,1)}, bf16[1536,768]{1,0:T(8,128)(2,1)}, bf16[1536,768]{1,0:T(8,128)(2,1)}, f32[56,768]{1,0:T(8,128)}) custom-call(s32[32]{0:T(128)} %refs_0_.3, s32[2,4]{1,0:T(2,128)} %refs_1_.3, bf16[512,768]{1,0:T(8,128)(2,1)} %refs_2_.3, bf16[512,2304]{1,0:T(8,128)(2,1)} %get-tuple-element.140.refs_3_, ...), custom_call_target="tpu_custom_call" | custom-call | flops 30000001024 | bytes 1000 | tf_op jit(solution)/shard_map/space_backward/pallas_call | solution.py:333
  183.8 6.5 %collective-permute-done.2 = bf16[384,768]{1,0:T(8,128)(2,1)} collective-permute-done((bf16[384,768]{1,0:T(8,128)(2,1)}, bf16[384,768]{1,0:T(8,128)(2,1)}, u32[]{:S(2)}, u32[]{:S(2)}) %collective-permute-start.2) | collective-permute-done | bytes 589856 | tf_op jit(solution)/shard_map/ppermute | solution.py:844
  197.7 9.2 %collective-permute-done.4 = bf16[768,768]{1,0:T(8,128)(2,1)S(1)} collective-permute-done((bf16[768,768]{1,0:T(8,128)(2,1)}, bf16[768,768]{1,0:T(8,128)(2,1)S(1)}, u32[]{:S(2)}, u32[]{:S(2)}) %collective-permute-start.4) | collective-permute-done | bytes 1179680 | tf_op jit(solution)/shard_map/ppermute | solution.py:844
  225.2 11.3 %collective-permute-done.10.refs_2_ = bf16[96,768]{1,0:T(8,128)(2,1)S(1)} collective-permute-done((bf16[96,768]{1,0:T(8,128)(2,1)}, bf16[96,768]{1,0:T(8,128)(2,1)S(1)}, u32[]{:S(2)}, u32[]{:S(2)}) %collective-permute-start.10) | collective-permute-done | bytes 147488 | tf_op jit(solution)/shard_map/ppermute | solution.py:844
  237.1 13.0 %collective-permute-start.18 = (bf16[96,768]{1,0:T(8,128)(2,1)}, bf16[96,768]{1,0:T(8,128)(2,1)S(1)}, u32[]{:S(2)}, u32[]{:S(2)}) collective-permute-start(bf16[96,768]{1,0:T(8,128)(2,1)} %get-tuple-element.204), channel_id=1, source_target_pairs={{0,4},{1,5},{2,6},{3,7},{4,8},{5,9},{6,10},{7,11},{8,12},{9,13},{1... | collective-permute-start | bytes 442376 | tf_op jit(solution)/shard_map/ppermute | solution.py:844
  268.4 4.0 %reduce-scatter.2.cloned.1.call-done = bf16[192,768]{1,0:T(8,128)(2,1)} async-done(((bf16[6144,768]{1,0:T(8,128)(2,1)}), bf16[192,768]{1,0:T(8,128)(2,1)}) %reduce-scatter.2.cloned.1.call-update) | async-done | bytes 294928 | tf_op jit(solution)/shard_map/reduce_scatter | solution.py:1274
  289.5 6.3 %collective-permute-start.29 = (f32[56,768]{1,0:T(8,128)S(1)}, f32[56,768]{1,0:T(8,128)S(1)}, u32[]{:S(2)}, u32[]{:S(2)}) collective-permute-start(f32[56,768]{1,0:T(8,128)S(1)} %copy-done.6), channel_id=1, source_target_pairs={{0,4},{1,5},{2,6},{3,7},{4,0},{5,1},{6,2},{7,3},{8,12},{9,13},{10,... | collective-permute-start | bytes 516104 | tf_op jit(solution)/shard_map/ppermute | solution.py:844
  299.1 9.1 %collective-permute-done.23.refs_3_ = bf16[384,768]{1,0:T(8,128)(2,1)} collective-permute-done((bf16[384,768]{1,0:T(8,128)(2,1)}, bf16[384,768]{1,0:T(8,128)(2,1)}, u32[]{:S(2)}, u32[]{:S(2)}) %collective-permute-start.23) | collective-permute-done | bytes 589856 | tf_op jit(solution)/shard_map/ppermute | solution.py:844
  313.6 5.4 %collective-permute-done.31.refs_3_ = f32[56,768]{1,0:T(8,128)S(1)} collective-permute-done((f32[56,768]{1,0:T(8,128)S(1)}, f32[56,768]{1,0:T(8,128)S(1)}, u32[]{:S(2)}, u32[]{:S(2)}) %collective-permute-start.31) | collective-permute-done | bytes 172064 | tf_op jit(solution)/shard_map/ppermute | solution.py:844
  321.5 9.4 %mod_grads.1 = (f32[768,6912]{1,0:T(8,128)}, f32[6912]{0:T(1024)}, f32[1536]{0:T(1024)}, f32[768]{0:T(1024)}, f32[1536]{0:T(1024)}, /*index=5*/f32[768]{0:T(1024)}, f32[3072]{0:T(1024)}, f32[768]{0:T(1024)}) custom-call(f32[56,768]{1,0:T(8,128)} %pair_sum.5.small_ref), custom_call_target="tpu_custom_call" | custom-call | flops 1000 | bytes 1000 | tf_op jit(solution)/shard_map/mod_grads/pallas_call | solution.py:1173
  344.9 19.1 %all-gather.2.cloned.1.call-done.in_ref = bf16[6144,768]{1,0:T(8,128)(2,1)} async-done(((bf16[192,768]{1,0:T(8,128)(2,1)}), bf16[6144,768]{1,0:T(8,128)(2,1)}) %all-gather.2.cloned.1.call-update) | async-done | bytes 9437200 | tf_op jit(solution)/shard_map/all_gather | solution.py:1334
  364.0 9.0 %widen_plain.1 = (f32[768,3072]{1,0:T(8,128)}, f32[3072,768]{1,0:T(8,128)}) custom-call(bf16[6144,768]{1,0:T(8,128)(2,1)} %all-gather.2.cloned.1.call-done.in_ref), custom_call_target="tpu_custom_call" | custom-call | flops 1000 | bytes 1000 | tf_op jit(solution)/shard_map/widen_plain/pallas_call | solution.py:1119
  (172 shorter events, 105.8 us)
Async XLA Ops:
  9.3 26.1 %all-to-all-start = ((bf16[16,2,16,768]{3,2,1,0:T(8,128)(2,1)}), bf16[16,2,16,768]{3,2,1,0:T(8,128)(2,1)S(1)}, u32[]{:S(2)}, u32[]{:S(2)}) async-start(bf16[16,2,16,768]{3,2,1,0:T(8,128)(2,1)} %bitcast.25), calls=%async_computation | async-start | bytes 1572864 | tf_op jit(solution)/shard_map/all_to_all | solution.py:1235
  35.4 24.2 %all-to-all-start.1 = ((bf16[16,2,16,768]{3,2,1,0:T(8,128)(2,1)}), bf16[16,2,16,768]{3,2,1,0:T(8,128)(2,1)S(1)}, u32[]{:S(2)}, u32[]{:S(2)}) async-start(bf16[16,2,16,768]{3,2,1,0:T(8,128)(2,1)} %get-tuple-element.144), calls=%async_computation.1 | async-start | bytes 1572864 | tf_op jit(solution)/shard_map/all_to_all | solution.py:1235
  40.9 231.5 %reduce-scatter.2.cloned.1.call-start = ((), (), s32[]{:S(2)}) async-start(), calls=%async_computation.5 | async-start | bytes 9732096 | tf_op jit(solution)/shard_map/reduce_scatter | solution.py:1274
  118.1 24.2 %all-to-all-start.2 = ((bf16[16,2,16,768]{3,2,1,0:T(8,128)(2,1)}), bf16[16,2,16,768]{3,2,1,0:T(8,128)(2,1)S(1)}, u32[]{:S(2)}, u32[]{:S(2)}) async-start(bf16[16,2,16,768]{3,2,1,0:T(8,128)(2,1)} %bitcast.38), calls=%async_computation.2 | async-start | bytes 1572864 | tf_op jit(solution)/shard_map/all_to_all | solution.py:1235
  142.4 35.0 %all-to-all-start.3 = ((bf16[16,2,16,768]{3,2,1,0:T(8,128)(2,1)}), bf16[16,2,16,768]{3,2,1,0:T(8,128)(2,1)S(1)}, u32[]{:S(2)}, u32[]{:S(2)}) async-start(bf16[16,2,16,768]{3,2,1,0:T(8,128)(2,1)} %bitcast.8), calls=%async_computation.3 | async-start | bytes 1572864 | tf_op jit(solution)/shard_map/all_to_all | solution.py:1235
  147.9 216.1 %all-gather.2.cloned.1.call-start = ((), (), s32[]{:S(2)}) async-start(), calls=%async_computation.6 | async-start | bytes 9732096 | tf_op jit(solution)/shard_map/all_gather | solution.py:1334
  148.1 25.0 %collective-permute-start.1 = (bf16[768,768]{1,0:T(8,128)(2,1)}, bf16[768,768]{1,0:T(8,128)(2,1)}, u32[]{:S(2)}, u32[]{:S(2)}) collective-permute-start(bf16[768,768]{1,0:T(8,128)(2,1)} %get-tuple-element.171), channel_id=1, source_target_pairs={{0,16},{1,3},{2,18},{3,1},{4,20},{5,7},{6,22},{7,5},{8,24},{9,11},... | collective-permute-start | bytes 3538952 | tf_op jit(solution)/shard_map/ppermute | solution.py:844
  182.4 24.4 %collective-permute-start.4 = (bf16[768,768]{1,0:T(8,128)(2,1)}, bf16[768,768]{1,0:T(8,128)(2,1)S(1)}, u32[]{:S(2)}, u32[]{:S(2)}) collective-permute-start(bf16[768,768]{1,0:T(8,128)(2,1)} %get-tuple-element.179), channel_id=1, source_target_pairs={{0,16},{1,3},{2,18},{3,1},{4,20},{5,7},{6,22},{7,5},{8,24},{9,11},... | collective-permute-start | bytes 3538952 | tf_op jit(solution)/shard_map/ppermute | solution.py:844
  192.5 19.7 %collective-permute-start.6 = (bf16[96,768]{1,0:T(8,128)(2,1)}, bf16[96,768]{1,0:T(8,128)(2,1)S(1)}, u32[]{:S(2)}, u32[]{:S(2)}) collective-permute-start(bf16[96,768]{1,0:T(8,128)(2,1)} %get-tuple-element.186), channel_id=1, source_target_pairs={{0,4},{1,5},{2,6},{3,7},{4,8},{5,9},{6,10},{7,11},{8,12},{9,13},{1... | collective-permute-start | bytes 442376 | tf_op jit(solution)/shard_map/ppermute | solution.py:844
  193.8 18.4 %collective-permute-start.7 = (bf16[96,768]{1,0:T(8,128)(2,1)}, bf16[96,768]{1,0:T(8,128)(2,1)S(1)}, u32[]{:S(2)}, u32[]{:S(2)}) collective-permute-start(bf16[96,768]{1,0:T(8,128)(2,1)} %get-tuple-element.187), channel_id=1, source_target_pairs={{0,8},{1,9},{2,10},{3,11},{4,12},{5,13},{6,14},{7,15},{8,0},{9,1},... | collective-permute-start | bytes 442376 | tf_op jit(solution)/shard_map/ppermute | solution.py:844
  197.7 57.0 %collective-permute-start.14 = (f32[56,768]{1,0:T(8,128)S(1)}, f32[56,768]{1,0:T(8,128)S(1)}, u32[]{:S(2)}, u32[]{:S(2)}) collective-permute-start(f32[56,768]{1,0:T(8,128)S(1)} %copy-done.15), channel_id=1, source_target_pairs={{0,1},{1,0},{2,3},{3,2},{4,5},{5,4},{6,7},{7,6},{8,9},{9,8},{10,11... | collective-permute-start | bytes 516104 | tf_op jit(solution)/shard_map/ppermute | solution.py:844
  218.4 18.1 %collective-permute-start.10 = (bf16[96,768]{1,0:T(8,128)(2,1)}, bf16[96,768]{1,0:T(8,128)(2,1)S(1)}, u32[]{:S(2)}, u32[]{:S(2)}) collective-permute-start(bf16[96,768]{1,0:T(8,128)(2,1)} %finish_sum.2.refs_0_), channel_id=1, source_target_pairs={{0,8},{1,9},{2,10},{3,11},{4,12},{5,13},{6,14},{7,15},{8,0},{9,1},... | collective-permute-start | bytes 442376 | tf_op jit(solution)/shard_map/ppermute | solution.py:844
  220.8 16.3 %collective-permute-start.11 = (bf16[96,768]{1,0:T(8,128)(2,1)}, bf16[96,768]{1,0:T(8,128)(2,1)S(1)}, u32[]{:S(2)}, u32[]{:S(2)}) collective-permute-start(bf16[96,768]{1,0:T(8,128)(2,1)} %finish_sum.2.refs_0_), channel_id=1, source_target_pairs={{0,12},{1,13},{2,14},{3,15},{4,0},{5,1},{6,2},{7,3},{8,4},{9,5},{1... | collective-permute-start | bytes 442376 | tf_op jit(solution)/shard_map/ppermute | solution.py:844
  237.1 20.0 %collective-permute-start.18 = (bf16[96,768]{1,0:T(8,128)(2,1)}, bf16[96,768]{1,0:T(8,128)(2,1)S(1)}, u32[]{:S(2)}, u32[]{:S(2)}) collective-permute-start(bf16[96,768]{1,0:T(8,128)(2,1)} %get-tuple-element.204), channel_id=1, source_target_pairs={{0,4},{1,5},{2,6},{3,7},{4,8},{5,9},{6,10},{7,11},{8,12},{9,13},{1... | collective-permute-start | bytes 442376 | tf_op jit(solution)/shard_map/ppermute | solution.py:844
  278.1 31.3 %collective-permute-start.12 = (bf16[384,768]{1,0:T(8,128)(2,1)S(1)}, bf16[384,768]{1,0:T(8,128)(2,1)S(1)}, u32[]{:S(2)}, u32[]{:S(2)}) collective-permute-start(bf16[384,768]{1,0:T(8,128)(2,1)S(1)} %bitcast.41), channel_id=1, source_target_pairs={{0,1},{1,0},{2,3},{3,2},{4,5},{5,4},{6,7},{7,6},{8,9},{9,8},{10,11... | collective-permute-start | bytes 1769480 | tf_op jit(solution)/shard_map/ppermute | solution.py:844
  282.5 25.7 %collective-permute-start.23 = (bf16[384,768]{1,0:T(8,128)(2,1)}, bf16[384,768]{1,0:T(8,128)(2,1)}, u32[]{:S(2)}, u32[]{:S(2)}) collective-permute-start(bf16[384,768]{1,0:T(8,128)(2,1)} %collective-permute-done.13.refs_1_), channel_id=1, source_target_pairs={{0,16},{1,3},{2,18},{3,1},{4,20},{5,7},{6,22},{7,5},{8,24},{9,11},... | collective-permute-start | bytes 1769480 | tf_op jit(solution)/shard_map/ppermute | solution.py:844
  289.4 20.6 %collective-permute-start.32 = (bf16[384,768]{1,0:T(8,128)(2,1)}, bf16[384,768]{1,0:T(8,128)(2,1)}, u32[]{:S(2)}, u32[]{:S(2)}) collective-permute-start(bf16[384,768]{1,0:T(8,128)(2,1)} %bitcast.23.refs_0_), channel_id=1, source_target_pairs={{0,2},{1,17},{2,0},{3,19},{4,6},{5,21},{6,4},{7,23},{8,10},{9,25},... | collective-permute-start | bytes 1769480 | tf_op jit(solution)/shard_map/ppermute | solution.py:844
  289.5 20.0 %collective-permute-start.29 = (f32[56,768]{1,0:T(8,128)S(1)}, f32[56,768]{1,0:T(8,128)S(1)}, u32[]{:S(2)}, u32[]{:S(2)}) collective-permute-start(f32[56,768]{1,0:T(8,128)S(1)} %copy-done.6), channel_id=1, source_target_pairs={{0,4},{1,5},{2,6},{3,7},{4,0},{5,1},{6,2},{7,3},{8,12},{9,13},{10,... | collective-permute-start | bytes 516104 | tf_op jit(solution)/shard_map/ppermute | solution.py:844
  296.0 17.5 %collective-permute-start.30 = (f32[56,768]{1,0:T(8,128)S(1)}, f32[56,768]{1,0:T(8,128)S(1)}, u32[]{:S(2)}, u32[]{:S(2)}) collective-permute-start(f32[56,768]{1,0:T(8,128)S(1)} %copy-done.6), channel_id=1, source_target_pairs={{0,8},{1,9},{2,10},{3,11},{4,12},{5,13},{6,14},{7,15},{8,0},{9,1},... | collective-permute-start | bytes 516104 | tf_op jit(solution)/shard_map/ppermute | solution.py:844
  309.4 21.5 %collective-permute-start.21 = (bf16[384,768]{1,0:T(8,128)(2,1)}, bf16[384,768]{1,0:T(8,128)(2,1)S(1)}, u32[]{:S(2)}, u32[]{:S(2)}) collective-permute-start(bf16[384,768]{1,0:T(8,128)(2,1)} %collective-permute-done.13.refs_1_), channel_id=1, source_target_pairs={{0,1},{1,0},{2,3},{3,2},{4,5},{5,4},{6,7},{7,6},{8,9},{9,8},{10,11... | collective-permute-start | bytes 1769480 | tf_op jit(solution)/shard_map/ppermute | solution.py:844
  309.5 21.5 %collective-permute-start.27 = (bf16[384,768]{1,0:T(8,128)(2,1)}, bf16[384,768]{1,0:T(8,128)(2,1)S(1)}, u32[]{:S(2)}, u32[]{:S(2)}) collective-permute-start(bf16[384,768]{1,0:T(8,128)(2,1)} %copy-done.14), channel_id=1, source_target_pairs={{0,1},{1,0},{2,3},{3,2},{4,5},{5,4},{6,7},{7,6},{8,9},{9,8},{10,11... | collective-permute-start | bytes 1769480 | tf_op jit(solution)/shard_map/ppermute | solution.py:844
  310.0 21.5 %collective-permute-start.28 = (bf16[384,768]{1,0:T(8,128)(2,1)}, bf16[384,768]{1,0:T(8,128)(2,1)}, u32[]{:S(2)}, u32[]{:S(2)}) collective-permute-start(bf16[384,768]{1,0:T(8,128)(2,1)} %collective-permute-done.23.refs_3_), channel_id=1, source_target_pairs={{0,1},{1,0},{2,3},{3,2},{4,5},{5,4},{6,7},{7,6},{8,9},{9,8},{10,11... | collective-permute-start | bytes 1769480 | tf_op jit(solution)/shard_map/ppermute | solution.py:844
  313.5 21.8 %collective-permute-start.35 = (bf16[384,768]{1,0:T(8,128)(2,1)}, bf16[384,768]{1,0:T(8,128)(2,1)}, u32[]{:S(2)}, u32[]{:S(2)}) collective-permute-start(bf16[384,768]{1,0:T(8,128)(2,1)} %bitcast.23.refs_0_), channel_id=1, source_target_pairs={{0,16},{1,3},{2,18},{3,1},{4,20},{5,7},{6,22},{7,5},{8,24},{9,11},... | collective-permute-start | bytes 1769480 | tf_op jit(solution)/shard_map/ppermute | solution.py:844
  319.0 16.4 %collective-permute-start.36 = (bf16[384,768]{1,0:T(8,128)(2,1)}, bf16[384,768]{1,0:T(8,128)(2,1)}, u32[]{:S(2)}, u32[]{:S(2)}) collective-permute-start(bf16[384,768]{1,0:T(8,128)(2,1)} %collective-permute-done.32.refs_1_), channel_id=1, source_target_pairs={{0,16},{1,3},{2,18},{3,1},{4,20},{5,7},{6,22},{7,5},{8,24},{9,11},... | collective-permute-start | bytes 1769480 | tf_op jit(solution)/shard_map/ppermute | solution.py:844
  (58 other events, 466.3 us)
Sparse Core Ops, SparseCore 0:
  118.3 154.0 reduce-scatter.1
  275.7 88.2 all-gather.1

commit v4 on v3

--- a/solution.py
+++ b/solution.py
@@ -376,7 +376,9 @@
     frames, pos, width = source.shape
     for lane in range(0, width, LANES):
         cols = pl.ds(lane, LANES)
-        stage[lane // LANES] = source[:, :, cols].astype(F32).reshape(frames * pos, LANES)
+        stage[lane // LANES, pl.ds(0, frames * pos), :] = (
+            source[:, :, cols].astype(F32).reshape(frames * pos, LANES)
+        )
         for p in range(pos):
             target[pl.ds(p * frames, frames), cols] = stage[
                 lane // LANES, pl.ds(p, frames, stride=pos), :
@@ -395,7 +397,7 @@
     frames, pos, width = target.shape
     for lane in range(0, width, LANES):
         target[:, :, pl.ds(lane, LANES)] = (
-            stage[lane // LANES].reshape(frames, pos, LANES).astype(BF)
+            stage[lane // LANES, pl.ds(0, frames * pos), :].reshape(frames, pos, LANES).astype(BF)
         )
 
 
@@ -571,7 +573,7 @@
             jax.ShapeDtypeStruct((1, width), F32),
         ],
         scratch_shapes=[
-            pltpu.VMEM((width // LANES, rows, LANES), F32),
+            pltpu.VMEM((width // LANES, rows + 16, LANES), F32),
             wide,
             wide,
             half,
@@ -696,7 +698,7 @@
         ],
         (1, 2),
         [
-            pltpu.VMEM((width // LANES, rows, LANES), F32),
+            pltpu.VMEM((width // LANES, rows + 16, LANES), F32),
             half,
             half,
             half,

time: 385 us -> 385 us (level)
  no operation moved by 1% of the time
where the time goes in v4:
time: 385 us; the launch traced here: 380 us
  Pallas kernels  163 us (42%)
  waiting for transfers between devices  104 us (27%)
  starting transfers between devices  82.6 us (21%)
  local copies, waits for them, and re-layouts  15.2 us (4%)
  between operations  14.9 us (4%)
    pallas_call x3, Pallas kernels, streamed(): pl.pallas_call(kernel, in_specs=in_specs, out_specs=[hbm() if i in late_o...  59.4 us
    ppermute x39, starting transfers between devices, move(): return lax.ppermute(value, BOTH, pairs)  58.2 us
    ppermute x39, waiting for transfers between devices, move(): return lax.ppermute(value, BOTH, pairs)  52.5 us
    pallas_call x1, Pallas kernels, owner_forward(): pl.pallas_call(owner_forward_kernel, grid=(steps,), in_specs=[vmem(), hbm...  35.7 us
    all_to_all x4, waiting for transfers between devices, exchange(): return lax.all_to_all(x, 'seq', split_axis=0, concat_axis=0, tiled=True)  28.2 us
    all_to_all x4, starting transfers between devices, exchange(): return lax.all_to_all(x, 'seq', split_axis=0, concat_axis=0, tiled=True)  23.9 us
    all_gather x1, waiting for transfers between devices, per_device(): sum_f = lax.all_gather(part_f.value, BOTH, axis=0, tiled=True)  19.2 us
    pallas_call x4, Pallas kernels, widen(): pl.pallas_call(functools.partial(widen_kernel, other, spots), in_specs=[h...  13.6 us
  transfers between devices with their start and end apart: 45, of which 18 were waited for; matrix products, arithmetic and copies ran while one was open for 1% of the time, Pallas kernels for 26%

profile of v4, /device:TPU:0, one launch (start us, length us, event | category | flops | bytes accessed | tf_op | source)
XLA Modules:
  0.0 380.1 jit_solution(3481464365305262528)
XLA Ops:
  9.3 7.4 %all-to-all-start = ((bf16[16,2,16,768]{3,2,1,0:T(8,128)(2,1)}), bf16[16,2,16,768]{3,2,1,0:T(8,128)(2,1)S(1)}, u32[]{:S(2)}, u32[]{:S(2)}) async-start(bf16[16,2,16,768]{3,2,1,0:T(8,128)(2,1)} %bitcast.25), calls=%async_computation | async-start | bytes 1572864 | tf_op jit(solution)/shard_map/all_to_all | solution.py:1237
  16.7 14.7 %space_forward.1 = (bf16[16,2,16,768]{3,2,1,0:T(8,128)(2,1)}, bf16[512,2304]{1,0:T(8,128)(2,1)}, bf16[512,768]{1,0:T(8,128)(2,1)}, f32[512,768]{1,0:T(8,128)}, f32[3,2,768]{2,1,0:T(2,128)}) custom-call(s32[32]{0:T(128)} %refs_0_.3, s32[2,4]{1,0:T(2,128)} %refs_1_.3, bf16[2,768]{1,0:T(2,128)(2,1)} %refs_10_.1, bf16[768,6912]{1,0:T(8,128)(2,1)} %w_ref.1, ...), custom_call_target="tpu_custom_call" | custom-call | flops 1000 | bytes 1000 | tf_op jit(solution)/shard_map/space_forward/pallas_call | solution.py:333
  31.4 4.0 %all-to-all-done = bf16[16,2,16,768]{3,2,1,0:T(8,128)(2,1)S(1)} async-done(((bf16[16,2,16,768]{3,2,1,0:T(8,128)(2,1)}), bf16[16,2,16,768]{3,2,1,0:T(8,128)(2,1)S(1)}, u32[]{:S(2)}, u32[]{:S(2)}) %all-to-all-start) | async-done | bytes 786464 | tf_op jit(solution)/shard_map/all_to_all | solution.py:1237
  35.4 5.5 %all-to-all-start.1 = ((bf16[16,2,16,768]{3,2,1,0:T(8,128)(2,1)}), bf16[16,2,16,768]{3,2,1,0:T(8,128)(2,1)S(1)}, u32[]{:S(2)}, u32[]{:S(2)}) async-start(bf16[16,2,16,768]{3,2,1,0:T(8,128)(2,1)} %get-tuple-element.144), calls=%async_computation.1 | async-start | bytes 1572864 | tf_op jit(solution)/shard_map/all_to_all | solution.py:1237
  42.6 6.0 %modulation.1.table_ref.refs_5_ = f32[6,2,768]{2,1,0:T(2,128)} custom-call(bf16[2,768]{1,0:T(2,128)(2,1)} %refs_10_.1, bf16[768,6912]{1,0:T(8,128)(2,1)} %w_ref.1, bf16[6912]{0:T(1024)(128)(2,1)} %b_ref.1), custom_call_target="tpu_custom_call" | custom-call | flops 1000 | bytes 1000 | tf_op jit(solution)/shard_map/modulation/pallas_call | solution.py:173
  48.7 10.9 %all-to-all-done.1 = bf16[16,2,16,768]{3,2,1,0:T(8,128)(2,1)S(1)} async-done(((bf16[16,2,16,768]{3,2,1,0:T(8,128)(2,1)}), bf16[16,2,16,768]{3,2,1,0:T(8,128)(2,1)S(1)}, u32[]{:S(2)}, u32[]{:S(2)}) %all-to-all-start.1) | async-done | bytes 786464 | tf_op jit(solution)/shard_map/all_to_all | solution.py:1237
  60.5 35.7 %owner_forward.1 = (bf16[512,768]{1,0:T(8,128)(2,1)}, bf16[512,2304]{1,0:T(8,128)(2,1)}, bf16[512,768]{1,0:T(8,128)(2,1)}, f32[512,768]{1,0:T(8,128)}, f32[512,7...) custom-call(bf16[32,16,768]{2,1,0:T(8,128)(2,1)} %bitcast.28, ...), custom_call_target="tpu_custom_call" | custom-call | flops 1000 | bytes 1000 | tf_op jit(solution)/shard_map/owner_forward/pallas_call | solution.py:544
  96.1 21.7 %owner_backward.1 = (bf16[32,16,768]{2,1,0:T(8,128)(2,1)}, bf16[1536,768]{1,0:T(8,128)(2,1)}, bf16[1536,768]{1,0:T(8,128)(2,1)}, f32[3,2,768]{2,1,0:T(2,128)}, f32[1,768]{1,0:T(1,128)}, /*index=5*/f32[2,768]{1,0:T(2,128)}) custom-call(bf16[512,768]{1,0:T(8,128)(2,1)} %get-tuple-element.147.refs_0_, bf16[512,2304]{1,0:T(8,128)(2,1)} %get-tuple-element.148.refs_1_, ...), custom_call_target="tpu_custom_call" | custom-call | flops 1000 | bytes 1000 | tf_op jit(solution)/shard_map/owner_backward/pallas_call | solution.py:333
  118.1 5.5 %all-to-all-start.2 = ((bf16[16,2,16,768]{3,2,1,0:T(8,128)(2,1)}), bf16[16,2,16,768]{3,2,1,0:T(8,128)(2,1)S(1)}, u32[]{:S(2)}, u32[]{:S(2)}) async-start(bf16[16,2,16,768]{3,2,1,0:T(8,128)(2,1)} %bitcast.38), calls=%async_computation.2 | async-start | bytes 1572864 | tf_op jit(solution)/shard_map/all_to_all | solution.py:1237
  125.1 4.0 %cross_sum.4 = (bf16[768,768]{1,0:T(8,128)(2,1)}, bf16[768,768]{1,0:T(8,128)(2,1)}) custom-call(bf16[2,768,768]{2,1,0:T(8,128)(2,1)} %bitcast.31, bf16[2,768,768]{2,1,0:T(8,128)(2,1)} %bitcast.33), custom_call_target="tpu_custom_call" | custom-call | flops 1000 | bytes 1000 | tf_op jit(solution)/shard_map/cross_sum/pallas_call | solution.py:881
  129.1 13.3 %all-to-all-done.2.refs_6_ = bf16[16,2,16,768]{3,2,1,0:T(8,128)(2,1)S(1)} async-done(((bf16[16,2,16,768]{3,2,1,0:T(8,128)(2,1)}), bf16[16,2,16,768]{3,2,1,0:T(8,128)(2,1)S(1)}, u32[]{:S(2)}, u32[]{:S(2)}) %all-to-all-start.2) | async-done | bytes 786464 | tf_op jit(solution)/shard_map/all_to_all | solution.py:1237
  142.4 5.5 %all-to-all-start.3 = ((bf16[16,2,16,768]{3,2,1,0:T(8,128)(2,1)}), bf16[16,2,16,768]{3,2,1,0:T(8,128)(2,1)S(1)}, u32[]{:S(2)}, u32[]{:S(2)}) async-start(bf16[16,2,16,768]{3,2,1,0:T(8,128)(2,1)} %bitcast.8), calls=%async_computation.3 | async-start | bytes 1572864 | tf_op jit(solution)/shard_map/all_to_all | solution.py:1237
  149.6 23.1 %space_backward.1 = (bf16[512,768]{1,0:T(8,128)(2,1)}, bf16[1536,768]{1,0:T(8,128)(2,1)}, bf16[1536,768]{1,0:T(8,128)(2,1)}, f32[56,768]{1,0:T(8,128)}) custom-call(s32[32]{0:T(128)} %refs_0_.3, s32[2,4]{1,0:T(2,128)} %refs_1_.3, bf16[512,768]{1,0:T(8,128)(2,1)} %refs_2_.3, bf16[512,2304]{1,0:T(8,128)(2,1)} %get-tuple-element.140.refs_3_, ...), custom_call_target="tpu_custom_call" | custom-call | flops 30000001024 | bytes 1000 | tf_op jit(solution)/shard_map/space_backward/pallas_call | solution.py:333
  183.8 6.5 %collective-permute-done.2 = bf16[384,768]{1,0:T(8,128)(2,1)} collective-permute-done((bf16[384,768]{1,0:T(8,128)(2,1)}, bf16[384,768]{1,0:T(8,128)(2,1)}, u32[]{:S(2)}, u32[]{:S(2)}) %collective-permute-start.2) | collective-permute-done | bytes 589856 | tf_op jit(solution)/shard_map/ppermute | solution.py:846
  197.7 9.2 %collective-permute-done.4 = bf16[768,768]{1,0:T(8,128)(2,1)S(1)} collective-permute-done((bf16[768,768]{1,0:T(8,128)(2,1)}, bf16[768,768]{1,0:T(8,128)(2,1)S(1)}, u32[]{:S(2)}, u32[]{:S(2)}) %collective-permute-start.4) | collective-permute-done | bytes 1179680 | tf_op jit(solution)/shard_map/ppermute | solution.py:846
  225.2 11.3 %collective-permute-done.10.refs_2_ = bf16[96,768]{1,0:T(8,128)(2,1)S(1)} collective-permute-done((bf16[96,768]{1,0:T(8,128)(2,1)}, bf16[96,768]{1,0:T(8,128)(2,1)S(1)}, u32[]{:S(2)}, u32[]{:S(2)}) %collective-permute-start.10) | collective-permute-done | bytes 147488 | tf_op jit(solution)/shard_map/ppermute | solution.py:846
  237.1 13.0 %collective-permute-start.18 = (bf16[96,768]{1,0:T(8,128)(2,1)}, bf16[96,768]{1,0:T(8,128)(2,1)S(1)}, u32[]{:S(2)}, u32[]{:S(2)}) collective-permute-start(bf16[96,768]{1,0:T(8,128)(2,1)} %get-tuple-element.204), channel_id=1, source_target_pairs={{0,4},{1,5},{2,6},{3,7},{4,8},{5,9},{6,10},{7,11},{8,12},{9,13},{1... | collective-permute-start | bytes 442376 | tf_op jit(solution)/shard_map/ppermute | solution.py:846
  268.4 4.0 %reduce-scatter.2.cloned.1.call-done = bf16[192,768]{1,0:T(8,128)(2,1)} async-done(((bf16[6144,768]{1,0:T(8,128)(2,1)}), bf16[192,768]{1,0:T(8,128)(2,1)}) %reduce-scatter.2.cloned.1.call-update) | async-done | bytes 294928 | tf_op jit(solution)/shard_map/reduce_scatter | solution.py:1276
  289.5 6.3 %collective-permute-start.29 = (f32[56,768]{1,0:T(8,128)S(1)}, f32[56,768]{1,0:T(8,128)S(1)}, u32[]{:S(2)}, u32[]{:S(2)}) collective-permute-start(f32[56,768]{1,0:T(8,128)S(1)} %copy-done.6), channel_id=1, source_target_pairs={{0,4},{1,5},{2,6},{3,7},{4,0},{5,1},{6,2},{7,3},{8,12},{9,13},{10,... | collective-permute-start | bytes 516104 | tf_op jit(solution)/shard_map/ppermute | solution.py:846
  299.1 8.9 %collective-permute-done.23.refs_3_ = bf16[384,768]{1,0:T(8,128)(2,1)} collective-permute-done((bf16[384,768]{1,0:T(8,128)(2,1)}, bf16[384,768]{1,0:T(8,128)(2,1)}, u32[]{:S(2)}, u32[]{:S(2)}) %collective-permute-start.23) | collective-permute-done | bytes 589856 | tf_op jit(solution)/shard_map/ppermute | solution.py:846
  313.5 5.4 %collective-permute-done.31.refs_3_ = f32[56,768]{1,0:T(8,128)S(1)} collective-permute-done((f32[56,768]{1,0:T(8,128)S(1)}, f32[56,768]{1,0:T(8,128)S(1)}, u32[]{:S(2)}, u32[]{:S(2)}) %collective-permute-start.31) | collective-permute-done | bytes 172064 | tf_op jit(solution)/shard_map/ppermute | solution.py:846
  321.5 9.4 %mod_grads.1 = (f32[768,6912]{1,0:T(8,128)}, f32[6912]{0:T(1024)}, f32[1536]{0:T(1024)}, f32[768]{0:T(1024)}, f32[1536]{0:T(1024)}, /*index=5*/f32[768]{0:T(1024)}, f32[3072]{0:T(1024)}, f32[768]{0:T(1024)}) custom-call(f32[56,768]{1,0:T(8,128)} %pair_sum.5.small_ref), custom_call_target="tpu_custom_call" | custom-call | flops 1000 | bytes 1000 | tf_op jit(solution)/shard_map/mod_grads/pallas_call | solution.py:1175
  344.8 19.2 %all-gather.2.cloned.1.call-done.in_ref = bf16[6144,768]{1,0:T(8,128)(2,1)} async-done(((bf16[192,768]{1,0:T(8,128)(2,1)}), bf16[6144,768]{1,0:T(8,128)(2,1)}) %all-gather.2.cloned.1.call-update) | async-done | bytes 9437200 | tf_op jit(solution)/shard_map/all_gather | solution.py:1336
  364.0 9.0 %widen_plain.1 = (f32[768,3072]{1,0:T(8,128)}, f32[3072,768]{1,0:T(8,128)}) custom-call(bf16[6144,768]{1,0:T(8,128)(2,1)} %all-gather.2.cloned.1.call-done.in_ref), custom_call_target="tpu_custom_call" | custom-call | flops 1000 | bytes 1000 | tf_op jit(solution)/shard_map/widen_plain/pallas_call | solution.py:1121
  (172 shorter events, 105.9 us)
Async XLA Ops:
  9.3 26.1 %all-to-all-start = ((bf16[16,2,16,768]{3,2,1,0:T(8,128)(2,1)}), bf16[16,2,16,768]{3,2,1,0:T(8,128)(2,1)S(1)}, u32[]{:S(2)}, u32[]{:S(2)}) async-start(bf16[16,2,16,768]{3,2,1,0:T(8,128)(2,1)} %bitcast.25), calls=%async_computation | async-start | bytes 1572864 | tf_op jit(solution)/shard_map/all_to_all | solution.py:1237
  35.4 24.2 %all-to-all-start.1 = ((bf16[16,2,16,768]{3,2,1,0:T(8,128)(2,1)}), bf16[16,2,16,768]{3,2,1,0:T(8,128)(2,1)S(1)}, u32[]{:S(2)}, u32[]{:S(2)}) async-start(bf16[16,2,16,768]{3,2,1,0:T(8,128)(2,1)} %get-tuple-element.144), calls=%async_computation.1 | async-start | bytes 1572864 | tf_op jit(solution)/shard_map/all_to_all | solution.py:1237
  40.9 231.5 %reduce-scatter.2.cloned.1.call-start = ((), (), s32[]{:S(2)}) async-start(), calls=%async_computation.5 | async-start | bytes 9732096 | tf_op jit(solution)/shard_map/reduce_scatter | solution.py:1276
  118.1 24.2 %all-to-all-start.2 = ((bf16[16,2,16,768]{3,2,1,0:T(8,128)(2,1)}), bf16[16,2,16,768]{3,2,1,0:T(8,128)(2,1)S(1)}, u32[]{:S(2)}, u32[]{:S(2)}) async-start(bf16[16,2,16,768]{3,2,1,0:T(8,128)(2,1)} %bitcast.38), calls=%async_computation.2 | async-start | bytes 1572864 | tf_op jit(solution)/shard_map/all_to_all | solution.py:1237
  142.4 35.0 %all-to-all-start.3 = ((bf16[16,2,16,768]{3,2,1,0:T(8,128)(2,1)}), bf16[16,2,16,768]{3,2,1,0:T(8,128)(2,1)S(1)}, u32[]{:S(2)}, u32[]{:S(2)}) async-start(bf16[16,2,16,768]{3,2,1,0:T(8,128)(2,1)} %bitcast.8), calls=%async_computation.3 | async-start | bytes 1572864 | tf_op jit(solution)/shard_map/all_to_all | solution.py:1237
  147.9 216.1 %all-gather.2.cloned.1.call-start = ((), (), s32[]{:S(2)}) async-start(), calls=%async_computation.6 | async-start | bytes 9732096 | tf_op jit(solution)/shard_map/all_gather | solution.py:1336
  148.1 25.0 %collective-permute-start.1 = (bf16[768,768]{1,0:T(8,128)(2,1)}, bf16[768,768]{1,0:T(8,128)(2,1)}, u32[]{:S(2)}, u32[]{:S(2)}) collective-permute-start(bf16[768,768]{1,0:T(8,128)(2,1)} %get-tuple-element.171), channel_id=1, source_target_pairs={{0,16},{1,3},{2,18},{3,1},{4,20},{5,7},{6,22},{7,5},{8,24},{9,11},... | collective-permute-start | bytes 3538952 | tf_op jit(solution)/shard_map/ppermute | solution.py:846
  182.5 24.4 %collective-permute-start.4 = (bf16[768,768]{1,0:T(8,128)(2,1)}, bf16[768,768]{1,0:T(8,128)(2,1)S(1)}, u32[]{:S(2)}, u32[]{:S(2)}) collective-permute-start(bf16[768,768]{1,0:T(8,128)(2,1)} %get-tuple-element.179), channel_id=1, source_target_pairs={{0,16},{1,3},{2,18},{3,1},{4,20},{5,7},{6,22},{7,5},{8,24},{9,11},... | collective-permute-start | bytes 3538952 | tf_op jit(solution)/shard_map/ppermute | solution.py:846
  192.5 19.7 %collective-permute-start.6 = (bf16[96,768]{1,0:T(8,128)(2,1)}, bf16[96,768]{1,0:T(8,128)(2,1)S(1)}, u32[]{:S(2)}, u32[]{:S(2)}) collective-permute-start(bf16[96,768]{1,0:T(8,128)(2,1)} %get-tuple-element.186), channel_id=1, source_target_pairs={{0,4},{1,5},{2,6},{3,7},{4,8},{5,9},{6,10},{7,11},{8,12},{9,13},{1... | collective-permute-start | bytes 442376 | tf_op jit(solution)/shard_map/ppermute | solution.py:846
  193.8 18.4 %collective-permute-start.7 = (bf16[96,768]{1,0:T(8,128)(2,1)}, bf16[96,768]{1,0:T(8,128)(2,1)S(1)}, u32[]{:S(2)}, u32[]{:S(2)}) collective-permute-start(bf16[96,768]{1,0:T(8,128)(2,1)} %get-tuple-element.187), channel_id=1, source_target_pairs={{0,8},{1,9},{2,10},{3,11},{4,12},{5,13},{6,14},{7,15},{8,0},{9,1},... | collective-permute-start | bytes 442376 | tf_op jit(solution)/shard_map/ppermute | solution.py:846
  197.7 57.0 %collective-permute-start.14 = (f32[56,768]{1,0:T(8,128)S(1)}, f32[56,768]{1,0:T(8,128)S(1)}, u32[]{:S(2)}, u32[]{:S(2)}) collective-permute-start(f32[56,768]{1,0:T(8,128)S(1)} %copy-done.15), channel_id=1, source_target_pairs={{0,1},{1,0},{2,3},{3,2},{4,5},{5,4},{6,7},{7,6},{8,9},{9,8},{10,11... | collective-permute-start | bytes 516104 | tf_op jit(solution)/shard_map/ppermute | solution.py:846
  218.4 18.1 %collective-permute-start.10 = (bf16[96,768]{1,0:T(8,128)(2,1)}, bf16[96,768]{1,0:T(8,128)(2,1)S(1)}, u32[]{:S(2)}, u32[]{:S(2)}) collective-permute-start(bf16[96,768]{1,0:T(8,128)(2,1)} %finish_sum.2.refs_0_), channel_id=1, source_target_pairs={{0,8},{1,9},{2,10},{3,11},{4,12},{5,13},{6,14},{7,15},{8,0},{9,1},... | collective-permute-start | bytes 442376 | tf_op jit(solution)/shard_map/ppermute | solution.py:846
  220.8 16.3 %collective-permute-start.11 = (bf16[96,768]{1,0:T(8,128)(2,1)}, bf16[96,768]{1,0:T(8,128)(2,1)S(1)}, u32[]{:S(2)}, u32[]{:S(2)}) collective-permute-start(bf16[96,768]{1,0:T(8,128)(2,1)} %finish_sum.2.refs_0_), channel_id=1, source_target_pairs={{0,12},{1,13},{2,14},{3,15},{4,0},{5,1},{6,2},{7,3},{8,4},{9,5},{1... | collective-permute-start | bytes 442376 | tf_op jit(solution)/shard_map/ppermute | solution.py:846
  237.1 20.0 %collective-permute-start.18 = (bf16[96,768]{1,0:T(8,128)(2,1)}, bf16[96,768]{1,0:T(8,128)(2,1)S(1)}, u32[]{:S(2)}, u32[]{:S(2)}) collective-permute-start(bf16[96,768]{1,0:T(8,128)(2,1)} %get-tuple-element.204), channel_id=1, source_target_pairs={{0,4},{1,5},{2,6},{3,7},{4,8},{5,9},{6,10},{7,11},{8,12},{9,13},{1... | collective-permute-start | bytes 442376 | tf_op jit(solution)/shard_map/ppermute | solution.py:846
  278.1 31.3 %collective-permute-start.12 = (bf16[384,768]{1,0:T(8,128)(2,1)S(1)}, bf16[384,768]{1,0:T(8,128)(2,1)S(1)}, u32[]{:S(2)}, u32[]{:S(2)}) collective-permute-start(bf16[384,768]{1,0:T(8,128)(2,1)S(1)} %bitcast.41), channel_id=1, source_target_pairs={{0,1},{1,0},{2,3},{3,2},{4,5},{5,4},{6,7},{7,6},{8,9},{9,8},{10,11... | collective-permute-start | bytes 1769480 | tf_op jit(solution)/shard_map/ppermute | solution.py:846
  282.5 25.6 %collective-permute-start.23 = (bf16[384,768]{1,0:T(8,128)(2,1)}, bf16[384,768]{1,0:T(8,128)(2,1)}, u32[]{:S(2)}, u32[]{:S(2)}) collective-permute-start(bf16[384,768]{1,0:T(8,128)(2,1)} %collective-permute-done.13.refs_1_), channel_id=1, source_target_pairs={{0,16},{1,3},{2,18},{3,1},{4,20},{5,7},{6,22},{7,5},{8,24},{9,11},... | collective-permute-start | bytes 1769480 | tf_op jit(solution)/shard_map/ppermute | solution.py:846
  289.4 20.5 %collective-permute-start.32 = (bf16[384,768]{1,0:T(8,128)(2,1)}, bf16[384,768]{1,0:T(8,128)(2,1)}, u32[]{:S(2)}, u32[]{:S(2)}) collective-permute-start(bf16[384,768]{1,0:T(8,128)(2,1)} %bitcast.23.refs_0_), channel_id=1, source_target_pairs={{0,2},{1,17},{2,0},{3,19},{4,6},{5,21},{6,4},{7,23},{8,10},{9,25},... | collective-permute-start | bytes 1769480 | tf_op jit(solution)/shard_map/ppermute | solution.py:846
  289.5 19.9 %collective-permute-start.29 = (f32[56,768]{1,0:T(8,128)S(1)}, f32[56,768]{1,0:T(8,128)S(1)}, u32[]{:S(2)}, u32[]{:S(2)}) collective-permute-start(f32[56,768]{1,0:T(8,128)S(1)} %copy-done.6), channel_id=1, source_target_pairs={{0,4},{1,5},{2,6},{3,7},{4,0},{5,1},{6,2},{7,3},{8,12},{9,13},{10,... | collective-permute-start | bytes 516104 | tf_op jit(solution)/shard_map/ppermute | solution.py:846
  296.0 17.4 %collective-permute-start.30 = (f32[56,768]{1,0:T(8,128)S(1)}, f32[56,768]{1,0:T(8,128)S(1)}, u32[]{:S(2)}, u32[]{:S(2)}) collective-permute-start(f32[56,768]{1,0:T(8,128)S(1)} %copy-done.6), channel_id=1, source_target_pairs={{0,8},{1,9},{2,10},{3,11},{4,12},{5,13},{6,14},{7,15},{8,0},{9,1},... | collective-permute-start | bytes 516104 | tf_op jit(solution)/shard_map/ppermute | solution.py:846
  309.4 21.5 %collective-permute-start.21 = (bf16[384,768]{1,0:T(8,128)(2,1)}, bf16[384,768]{1,0:T(8,128)(2,1)S(1)}, u32[]{:S(2)}, u32[]{:S(2)}) collective-permute-start(bf16[384,768]{1,0:T(8,128)(2,1)} %collective-permute-done.13.refs_1_), channel_id=1, source_target_pairs={{0,1},{1,0},{2,3},{3,2},{4,5},{5,4},{6,7},{7,6},{8,9},{9,8},{10,11... | collective-permute-start | bytes 1769480 | tf_op jit(solution)/shard_map/ppermute | solution.py:846
  309.5 21.5 %collective-permute-start.27 = (bf16[384,768]{1,0:T(8,128)(2,1)}, bf16[384,768]{1,0:T(8,128)(2,1)S(1)}, u32[]{:S(2)}, u32[]{:S(2)}) collective-permute-start(bf16[384,768]{1,0:T(8,128)(2,1)} %copy-done.14), channel_id=1, source_target_pairs={{0,1},{1,0},{2,3},{3,2},{4,5},{5,4},{6,7},{7,6},{8,9},{9,8},{10,11... | collective-permute-start | bytes 1769480 | tf_op jit(solution)/shard_map/ppermute | solution.py:846
  310.0 21.5 %collective-permute-start.28 = (bf16[384,768]{1,0:T(8,128)(2,1)}, bf16[384,768]{1,0:T(8,128)(2,1)}, u32[]{:S(2)}, u32[]{:S(2)}) collective-permute-start(bf16[384,768]{1,0:T(8,128)(2,1)} %collective-permute-done.23.refs_3_), channel_id=1, source_target_pairs={{0,1},{1,0},{2,3},{3,2},{4,5},{5,4},{6,7},{7,6},{8,9},{9,8},{10,11... | collective-permute-start | bytes 1769480 | tf_op jit(solution)/shard_map/ppermute | solution.py:846
  313.5 21.8 %collective-permute-start.35 = (bf16[384,768]{1,0:T(8,128)(2,1)}, bf16[384,768]{1,0:T(8,128)(2,1)}, u32[]{:S(2)}, u32[]{:S(2)}) collective-permute-start(bf16[384,768]{1,0:T(8,128)(2,1)} %bitcast.23.refs_0_), channel_id=1, source_target_pairs={{0,16},{1,3},{2,18},{3,1},{4,20},{5,7},{6,22},{7,5},{8,24},{9,11},... | collective-permute-start | bytes 1769480 | tf_op jit(solution)/shard_map/ppermute | solution.py:846
  318.9 16.4 %collective-permute-start.36 = (bf16[384,768]{1,0:T(8,128)(2,1)}, bf16[384,768]{1,0:T(8,128)(2,1)}, u32[]{:S(2)}, u32[]{:S(2)}) collective-permute-start(bf16[384,768]{1,0:T(8,128)(2,1)} %collective-permute-done.32.refs_1_), channel_id=1, source_target_pairs={{0,16},{1,3},{2,18},{3,1},{4,20},{5,7},{6,22},{7,5},{8,24},{9,11},... | collective-permute-start | bytes 1769480 | tf_op jit(solution)/shard_map/ppermute | solution.py:846
  (58 other events, 466.3 us)
Sparse Core Ops, SparseCore 0:
  118.3 154.0 reduce-scatter.1
  275.7 88.2 all-gather.1
